TPU v7x, 32 devices: a whole 2x2x4 slice. The times are simulated.
32 devices in a mesh: groups: 2 (over x), fsdp: 4 (over z), tensor: 4 (over y, core).
Axes of the slice: x: 2, y: 2, z: 4, core: 2. Of those that a mesh axis runs over, the one named last changes fastest.
Arguments:
- queries: bfloat16 [8, 64, 8192], P(None, ('groups', 'fsdp'), 'tensor'), parts along dimension 1, may hold values from -120 to 120
- cache: bfloat16 [64, 2, 8, 512, 128], P(('groups', 'fsdp', 'tensor')), parts along dimension 0, may hold values from -4 to 4
- decoded_key_value: bfloat16 [8, 64, 2048], P(None, ('groups', 'fsdp'), 'tensor'), parts along dimension 1, may hold values from -8 to 8
- lengths: int32 [64], P(('groups', 'fsdp', 'tensor')), parts along dimension 0, may hold values from 1 to 512, as said below
- frozen_output_weight: bfloat16 [8192, 8192], P('tensor'), may hold values from -0.0625 to 0.0625
- adapter_down_weight: bfloat16 [8192, 64], P('tensor', 'fsdp'), may hold values from -0.0625 to 0.0625
- adapter_up_weight: bfloat16 [64, 8192], P(None, ('fsdp', 'tensor')), may hold values from -0.75 to 0.75
Outputs:
- projected: bfloat16 [8, 64, 8192], P(None, ('groups', 'fsdp', 'tensor')), parts along dimension 1
There are 2 independent parts, one for each index of `groups`. A program takes and returns all parts, laid end to end along the dimension named above; an argument that names none is the same for every part. Nothing has to cross between parts.
Inputs may be any that keep to these rules, and one draw needn't show every extreme that they name: `lengths`: some row has 512 filled slots and some row has 1.
All inputs are finite; a program needn't handle non-finite values.
Results may differ from a plain program's by a relative error of at most 0.0058.
Values may be sent and summed in bfloat16 or wider, within the bound.
No kernel may reach another device: no remote copies, remote signals or barrier semaphores. Data moves between devices by JAX's collectives and lax.ppermute only.
A program may use at most 128 MiB of HBM per device.

v0:
```python
import jax
import jax.numpy as jnp
from jax import lax
from jax.sharding import PartitionSpec as P

HEADS = 64
KV_HEADS = 8
HEAD_DIM = 128


adapter_scale = 2.0


def attend(query_rows, cache_rows, new_rows, lengths):
    steps_count, rows_count, width = query_rows.shape
    cache_slots = cache_rows.shape[3]
    group = HEADS // KV_HEADS
    kv_width = KV_HEADS * HEAD_DIM
    scale = HEAD_DIM ** (-0.5)
    grouped = query_rows.reshape(steps_count, rows_count, KV_HEADS, group, HEAD_DIM)
    cache_keys = cache_rows[:, 0]
    cache_values = cache_rows[:, 1].astype(jnp.float32)
    new_keys = new_rows[:, :, :kv_width].reshape(steps_count, rows_count, KV_HEADS, HEAD_DIM)
    new_values = (
        new_rows[:, :, kv_width:]
        .reshape(steps_count, rows_count, KV_HEADS, HEAD_DIM)
        .astype(jnp.float32)
    )
    cache_scores = (
        jnp.einsum("srkgd,rkcd->rksgc", grouped, cache_keys, preferred_element_type=jnp.float32)
        * scale
    )
    new_scores = (
        jnp.einsum("srkgd,nrkd->rksgn", grouped, new_keys, preferred_element_type=jnp.float32)
        * scale
    )
    slot_ids = jnp.arange(cache_slots, dtype=jnp.int32)
    valid = (slot_ids[None, :] < lengths[:, None])[:, None, None, None, :]
    step_ids = jnp.arange(steps_count, dtype=jnp.int32)
    causal = (step_ids[None, :] <= step_ids[:, None])[None, None, :, None, :]
    masked_cache = jnp.where(valid, cache_scores, -1e30)
    masked_new = jnp.where(causal, new_scores, -1e30)
    highest = jnp.maximum(masked_cache.max(-1), masked_new.max(-1))[..., None]
    cache_probs = jnp.where(valid, jnp.exp(masked_cache - highest), 0.0)
    new_probs = jnp.where(causal, jnp.exp(masked_new - highest), 0.0)
    totals = cache_probs.sum(-1) + new_probs.sum(-1)
    mixed = jnp.einsum(
        "rksgc,rkcd->rksgd", cache_probs, cache_values, precision=lax.Precision.HIGHEST
    )
    mixed = mixed + jnp.einsum(
        "rksgn,nrkd->rksgd", new_probs, new_values, precision=lax.Precision.HIGHEST
    )
    result = (mixed / totals[..., None]).astype(jnp.bfloat16)
    return jnp.transpose(result, (2, 0, 1, 3, 4)).reshape(steps_count, rows_count, HEADS * HEAD_DIM)


def shards(
    queries,
    cache,
    decoded_key_value,
    lengths,
    frozen_output_weight,
    adapter_down_weight,
    adapter_up_weight,
):
    down_factor_matrix = lax.all_gather(adapter_down_weight, "fsdp", axis=1, tiled=True)
    up_factor_matrix = lax.all_gather(adapter_up_weight, ("fsdp", "tensor"), axis=1, tiled=True)
    weight_delta = jnp.dot(down_factor_matrix, up_factor_matrix, preferred_element_type=jnp.float32)
    combined_output_weight = (
        frozen_output_weight.astype(jnp.float32) + adapter_scale * weight_delta
    ).astype(jnp.bfloat16)
    query_rows, new_rows = (
        lax.all_to_all(queries, "tensor", split_axis=1, concat_axis=2, tiled=True),
        lax.all_to_all(decoded_key_value, "tensor", split_axis=1, concat_axis=2, tiled=True),
    )
    attended = attend(query_rows, cache, new_rows, lengths)
    head_major = lax.all_to_all(attended, "tensor", split_axis=2, concat_axis=1, tiled=True)
    steps_count, rows_dev, width_dev = head_major.shape
    partial_out = jnp.dot(
        head_major.reshape(steps_count * rows_dev, width_dev),
        combined_output_weight,
        preferred_element_type=jnp.float32,
    )
    partial_out = partial_out.reshape(steps_count, rows_dev, combined_output_weight.shape[1])
    own_rows = lax.psum_scatter(partial_out, "tensor", scatter_dimension=1, tiled=True)
    return own_rows.astype(jnp.bfloat16)


def solution(mesh):
    return jax.shard_map(
        shards,
        mesh=mesh,
        in_specs=(
            P(None, ("groups", "fsdp"), "tensor"),
            P(("groups", "fsdp", "tensor"), None, None, None, None),
            P(None, ("groups", "fsdp"), "tensor"),
            P(("groups", "fsdp", "tensor")),
            P("tensor", None),
            P("tensor", "fsdp"),
            P(None, ("fsdp", "tensor")),
        ),
        out_specs=P(None, ("groups", "fsdp", "tensor"), None),
        check_vma=False,
    )
```

profile of v0, /device:TPU:0, one launch (start us, length us, event | category | flops | bytes accessed | tf_op | source)
XLA Modules:
  0.0 140.8 jit_solution(7199129075134379574)
XLA Ops:
  6.5 1.5 %copy.26 = bf16[8,8,512]{2,0,1:T(8,128)(2,1)} copy(bf16[8,8,512]{2,1,0:T(8,128)(2,1)} %param.9) | data formatting | bytes 131072 | tf_op args[2]
  8.0 4.2 %all-to-all-start.1 = ((bf16[8,8,512]{2,0,1:T(8,128)(2,1)}), bf16[8,8,512]{2,0,1:T(8,128)(2,1)S(1)}, u32[]{:S(2)}, u32[]{:S(2)}) async-start(bf16[8,8,512]{2,0,1:T(8,128)(2,1)} %copy.26), calls=%async_computation.1 | async-start | bytes 131072 | tf_op jit(solution)/shard_map/all_to_all | solution.py:74
  12.2 0.7 all-gather.2.cloned.1.call-update
  13.0 1.8 %copy.22 = bf16[8,8,2048]{2,0,1:T(8,128)(2,1)} copy(bf16[8,8,2048]{2,1,0:T(8,128)(2,1)} %param.7) | data formatting | bytes 524288 | tf_op args[0]
  14.8 1.6 %all-to-all-done.1 = bf16[8,8,512]{2,0,1:T(8,128)(2,1)S(1)} async-done(((bf16[8,8,512]{2,0,1:T(8,128)(2,1)}), bf16[8,8,512]{2,0,1:T(8,128)(2,1)S(1)}, u32[]{:S(2)}, u32[]{:S(2)}) %all-to-all-start.1) | async-done | bytes 65568 | tf_op jit(solution)/shard_map/all_to_all | solution.py:74
  16.4 3.4 %all-to-all-start = ((bf16[8,8,2048]{2,0,1:T(8,128)(2,1)}), bf16[8,8,2048]{2,0,1:T(8,128)(2,1)S(1)}, u32[]{:S(2)}, u32[]{:S(2)}) async-start(bf16[8,8,2048]{2,0,1:T(8,128)(2,1)} %copy.22), calls=%async_computation | async-start | bytes 524288 | tf_op jit(solution)/shard_map/all_to_all | solution.py:73
  19.8 0.7 iota_compare_fusion.1
  20.5 5.3 %all-to-all-done = bf16[8,8,2048]{2,0,1:T(8,128)(2,1)S(1)} async-done(((bf16[8,8,2048]{2,0,1:T(8,128)(2,1)}), bf16[8,8,2048]{2,0,1:T(8,128)(2,1)S(1)}, u32[]{:S(2)}, u32[]{:S(2)}) %all-to-all-start) | async-done | bytes 262176 | tf_op jit(solution)/shard_map/all_to_all | solution.py:73
  25.8 0.2 copy.60
  26.0 0.2 reshape.57
  26.2 1.3 fusion.33
  27.4 0.0 copy-start
  27.5 2.7 %fusion.11 = (f32[2,8,8,8]{3,2,1,0:T(8,128)S(1)}, f32[2,8,8,8,512]{4,3,2,1,0:T(8,128)S(1)}) fusion(pred[2,512]{1,0:T(4,128)(4,1)S(1)} %iota_compare_fusion.1, bf16[2,2,8,512,128]{4,3,2,1,0:T(8,128)(2,1)} %param.8, bf16[8,2,8,8,128]{4,3,2,1,0:T(8,128)(2,1)S(1)} %reshape.57), kind=kOutput, calls=%fused_computation.12 | convolution fusion | flops 135789568 | bytes 4461568 | tf_op jit(solution)/shard_map/srkgd,rkcd->rksgc/dot_general | solution.py:30
  30.2 0.2 fusion.22
  30.4 0.7 fusion.12
  31.1 0.0 copy-done
  31.1 1.7 %fusion.5 = f32[2,8,8,8,128]{4,3,2,1,0:T(8,128)S(1)} fusion(bf16[2,2,8,512,128]{4,3,2,1,0:T(8,128)(2,1)S(1)} %copy-done, f32[2,8,8,8,512]{4,3,2,1,0:T(8,128)S(1)} %get-tuple-element.6, f32[2,8,8,8]{3,2,1,0:T(8,128)S(1)} %max.7, pred[2,512]{1,0:T(4,128)(4,1)S(1)} %iota_compare_fusion.1), kind=kOutput, calls=%fused_computation.4 | convolution fusion | flops 807403520 | bytes 4786176 | tf_op jit(solution)/shard_map/rksgc,rkcd->rksgd/dot_general | solution.py:47
  32.8 0.7 fusion.16
  33.5 4.6 %copy.45 = bf16[8,2,8,8,128]{0,1,4,3,2:T(2,128)(2,1)} copy(bf16[8,2,8,8,128]{4,3,0,2,1:T(8,128)(2,1)S(1)} %fusion.16) | data formatting | bytes 524288 | tf_op jit(solution)/shard_map/reshape | solution.py:54
  38.1 6.5 %reshape.66 = bf16[4,2,16384]{2,1,0:T(2,128)(2,1)} reshape(bf16[8192,2,8]{2,1,0:T(2,128)(2,1)} %bitcast.64) | data formatting | bytes 524288
  44.7 3.4 %all-to-all-start.2 = ((bf16[4,2,16384]{2,1,0:T(2,128)(2,1)}), bf16[4,2,16384]{2,1,0:T(2,128)(2,1)S(1)}, u32[]{:S(2)}, u32[]{:S(2)}) async-start(bf16[4,2,16384]{2,1,0:T(2,128)(2,1)} %reshape.66), calls=%async_computation.2 | async-start | bytes 524288 | tf_op jit(solution)/shard_map/all_to_all | solution.py:77
  48.1 0.0 reduce-scatter.2.cloned.1.call-start
  48.1 14.8 %all_gather.6 = bf16[2048,64]{0,1:T(8,128)(2,1)S(1)} all-gather(bf16[2048,16]{0,1:T(8,128)(2,1)S(1)} %copy-done.1), channel_id=1, replica_groups=mesh['groups'=2,'fsdp'=4,'tensor'=4] {'fsdp'}, dimensions={1}, use_global_device_ids=true | all-gather | bytes 327680 | tf_op jit(solution)/shard_map/all_gather | solution.py:66
  62.9 0.0 all-to-all-done.2
  62.9 5.9 %reshape.67 = bf16[8192,2,8]{2,1,0:T(2,128)(2,1)} reshape(bf16[4,2,16384]{2,1,0:T(2,128)(2,1)S(1)} %all-to-all-done.2) | data formatting | bytes 524288
  68.8 8.9 %copy.46 = bf16[8,4,2,2048]{3,0,2,1:T(8,128)(2,1)S(1)} copy(bf16[8,4,2,2048]{0,2,3,1:T(2,128)(2,1)} %bitcast.65) | data formatting | bytes 524288 | tf_op jit(solution)/shard_map/dot_general | solution.py:79
  77.7 0.0 all-gather.2.cloned.1.call-done
  77.7 20.8 %fusion.1 = f32[8,8,8192]{2,0,1:T(8,128)} fusion(bf16[8,8,2048]{2,0,1:T(8,128)(2,1)S(1)} %bitcast.68, bf16[2048,8192]{1,0:T(8,128)(2,1)} %param.11, bf16[2048,64]{0,1:T(8,128)(2,1)S(1)} %all_gather.6, bf16[64,8192]{1,0:T(8,128)(2,1)} %all-gather.2.cloned.1.call-done), kind=kOutput, calls=%fused_computation.2 | convolution fusion | flops 4362076160 | bytes 37224448 | tf_op jit(solution)/shard_map/dot_general | solution.py:79
  98.5 0.0 reduce-scatter.2.cloned.1.call-update
  98.5 33.4 %reduce-scatter.2.cloned.1.call-done = f32[8,2,8192]{2,0,1:T(8,128)} async-done(((f32[8,8,8192]{2,0,1:T(8,128)}), f32[8,2,8192]{2,0,1:T(8,128)}) %reduce-scatter.2.cloned.1.call-update) | async-done | bytes 524304 | tf_op jit(solution)/shard_map/reduce_scatter | solution.py:85
  131.9 1.1 convert_element_type.18
  133.0 1.0 copy.37
  (7 shorter events, 0.0 us)
Async XLA Ops:
  8.0 8.4 %all-to-all-start.1 = ((bf16[8,8,512]{2,0,1:T(8,128)(2,1)}), bf16[8,8,512]{2,0,1:T(8,128)(2,1)S(1)}, u32[]{:S(2)}, u32[]{:S(2)}) async-start(bf16[8,8,512]{2,0,1:T(8,128)(2,1)} %copy.26), calls=%async_computation.1 | async-start | bytes 131072 | tf_op jit(solution)/shard_map/all_to_all | solution.py:74
  12.2 65.5 %all-gather.2.cloned.1.call-start = ((), (), s32[]{:S(2)}) async-start(), calls=%async_computation.4 | async-start | bytes 1114112 | tf_op jit(solution)/shard_map/all_gather | solution.py:67
  16.4 9.4 %all-to-all-start = ((bf16[8,8,2048]{2,0,1:T(8,128)(2,1)}), bf16[8,8,2048]{2,0,1:T(8,128)(2,1)S(1)}, u32[]{:S(2)}, u32[]{:S(2)}) async-start(bf16[8,8,2048]{2,0,1:T(8,128)(2,1)} %copy.22), calls=%async_computation | async-start | bytes 524288 | tf_op jit(solution)/shard_map/all_to_all | solution.py:73
  27.4 3.6 %copy-start = (bf16[2,2,8,512,128]{4,3,2,1,0:T(8,128)(2,1)S(1)}, bf16[2,2,8,512,128]{4,3,2,1,0:T(8,128)(2,1)}, u32[]{:S(2)}) copy-start(bf16[2,2,8,512,128]{4,3,2,1,0:T(8,128)(2,1)} %param.8) | copy-start | bytes 12582916
  38.1 10.0 %copy-start.1 = (bf16[2048,16]{0,1:T(8,128)(2,1)S(1)}, bf16[2048,16]{0,1:T(8,128)(2,1)}, u32[]{:S(2)}) copy-start(bf16[2048,16]{0,1:T(8,128)(2,1)} %param.12) | copy-start | bytes 196612
  44.7 18.3 %all-to-all-start.2 = ((bf16[4,2,16384]{2,1,0:T(2,128)(2,1)}), bf16[4,2,16384]{2,1,0:T(2,128)(2,1)S(1)}, u32[]{:S(2)}, u32[]{:S(2)}) async-start(bf16[4,2,16384]{2,1,0:T(2,128)(2,1)} %reshape.66), calls=%async_computation.2 | async-start | bytes 524288 | tf_op jit(solution)/shard_map/all_to_all | solution.py:77
  48.1 83.9 %reduce-scatter.2.cloned.1.call-start = ((), (), s32[]{:S(2)}) async-start(), calls=%async_computation.5 | async-start | bytes 2621440 | tf_op jit(solution)/shard_map/reduce_scatter | solution.py:85
Sparse Core Ops, SparseCore 0:
  15.2 39.0 all-gather.1
  98.7 33.2 reduce-scatter.1
where the time goes:
time: 142 us; the launch traced here: 141 us
  waiting for transfers between devices  41 us (29%)
  local copies, waits for them, and re-layouts  30.6 us (22%)
  matrix products  27.2 us (19%)
  blocking collectives  14.8 us (10%)
  between operations  13.5 us (10%)
  starting transfers between devices  11.1 us (8%)
  other arithmetic  2.72 us (2%)
    reduce_scatter x1, waiting for transfers between devices, shards(): lax.psum_scatter(partial_out, 'tensor', scatter_dimension=1, tiled=True)  33.4 us
    dot_general x1, matrix products, shards(): jnp.dot(head_major.reshape(steps_count * rows_dev, width_dev), combined_o...  20.8 us
    unnamed x8, local copies, waits for them, and re-layouts  15.7 us
    all_gather x1, blocking collectives, shards(): lax.all_gather(adapter_down_weight, 'fsdp', axis=1, tiled=True)  14.8 us
    dot_general x1, local copies, waits for them, and re-layouts, shards(): jnp.dot(head_major.reshape(steps_count * rows_dev, width_dev), combined_o...  8.88 us
    all_to_all x1, waiting for transfers between devices, shards(): lax.all_to_all(queries, 'tensor', split_axis=1, concat_axis=2, tiled=True)  5.26 us
    reshape x1, local copies, waits for them, and re-layouts, attend(): jnp.transpose(result, (2, 0, 1, 3, 4))  4.6 us
    all_to_all x1, starting transfers between devices, shards(): lax.all_to_all(decoded_key_value, 'tensor', split_axis=1, concat_axis=2,...  4.24 us
  transfers between devices with their start and end apart: 5, of which 3 were waited for; matrix products, arithmetic and copies ran while one was open for 26% of the time, Pallas kernels for 0%

commit v1 on v0

v1 whole, which is shorter than its diff:
```python
import functools

import jax
import jax.numpy as jnp
from jax import lax
from jax.experimental import pallas as pl
from jax.experimental.pallas import tpu as pltpu
from jax.sharding import PartitionSpec as P

HEADS = 64
KV_HEADS = 8
HEAD_DIM = 128
GROUP = HEADS // KV_HEADS
RANK = 64
SCALE = 2.0
CHUNKS = 2
BF16 = jnp.bfloat16
F32 = jnp.float32
VMEM = pl.BlockSpec(memory_space=pltpu.VMEM)
SMEM = pl.BlockSpec(memory_space=pltpu.SMEM)
ROW_ROW = (((1,), (1,)), ((), ()))


def dot(a, b):
    return jnp.dot(a, b, preferred_element_type=F32)


def dot_rows(a, b):
    return lax.dot_general(a, b, ROW_ROW, preferred_element_type=F32)


def params(mib=24):
    return pltpu.CompilerParams(vmem_limit_bytes=mib * 2**20)


def split(x):
    high = x.astype(BF16)
    return high, (x - high.astype(F32)).astype(BF16)


def log2(n):
    return n.bit_length() - 1


def pack_kernel(query_ref, new_ref, down_ref, up_ref, *out_refs, parts, own, steps):
    *block_refs, factor_ref = out_refs
    me = lax.axis_index("tensor")
    rows = parts * own
    count = steps * rows
    i = lax.broadcasted_iota(jnp.int32, (count, count), 0)
    j = lax.broadcasted_iota(jnp.int32, (count, count), 1)
    step_out = i & (steps - 1)
    row_out = (i >> log2(steps)) & (own - 1)
    part_out = (i >> log2(steps * own)) ^ me
    source = step_out * rows + part_out * own + row_out
    select = jnp.where(source == j, 1.0, 0.0).astype(BF16)
    queries = query_ref[...].reshape(count, query_ref.shape[2])
    new = new_ref[...].reshape(count, new_ref.shape[2])
    queries = dot(select, queries)
    new = dot(select, new)
    heads = queries.shape[1] // HEAD_DIM
    pieces = new.shape[1] // HEAD_DIM
    tall = own * steps
    for k, block_ref in enumerate(block_refs):
        q = queries[k * tall : (k + 1) * tall]
        n = new[k * tall : (k + 1) * tall]
        tiles = [
            q[r * steps : (r + 1) * steps, h * HEAD_DIM : (h + 1) * HEAD_DIM]
            for r in range(own)
            for h in range(heads)
        ]
        tiles += [n[:, c * HEAD_DIM : (c + 1) * HEAD_DIM] for c in range(pieces)]
        block_ref[...] = jnp.concatenate(tiles, axis=0).astype(BF16)
    slot, depth = down_ref.shape[1], down_ref.shape[0]
    a = lax.broadcasted_iota(jnp.int32, (slot, slot), 0)
    b = lax.broadcasted_iota(jnp.int32, (slot, slot), 1)
    eye = jnp.where(a == b, 1.0, 0.0).astype(BF16)
    factor_ref[0:slot, :] = dot_rows(eye, down_ref[...]).astype(BF16)
    cut = up_ref.shape[1]
    per = depth // cut
    for c in range(per):
        lanes = slice(c * cut, (c + 1) * cut)
        tall = RANK // per
        factor_ref[slot + c * tall : slot + (c + 1) * tall, lanes] = up_ref[c * tall : (c + 1) * tall, :]


def attend_kernel(length_ref, *refs, parts, own, steps):
    block_refs = refs[:parts]
    cache_ref = refs[parts]
    out_refs = refs[parts + 1 : 2 * parts + 1]
    held_ref, attended_ref = refs[2 * parts + 1 :]
    me = lax.axis_index("tensor")
    for k in range(parts):
        held_ref[me ^ k] = block_refs[k][...]
    heads = HEADS // parts
    pieces = 2 * KV_HEADS // parts
    query_rows = own * heads * steps
    tall = own * steps
    slots = cache_ref.shape[3]
    together = min(heads, GROUP)
    scale = HEAD_DIM ** (-0.5)

    def piece(c):
        start = query_rows + (c % pieces) * tall
        return held_ref[c // pieces, start : start + tall, :]

    queries_count = GROUP * steps
    slot_ids = lax.broadcasted_iota(jnp.int32, (queries_count, slots), 1)
    step_ids = lax.broadcasted_iota(jnp.int32, (queries_count, tall), 0) & (steps - 1)
    new_ids = lax.broadcasted_iota(jnp.int32, (queries_count, tall), 1)
    for r in range(own):
        valid = slot_ids < length_ref[r]
        past = new_ids - r * steps
        causal = (past >= 0) & (past <= step_ids)
        for g in range(KV_HEADS):
            parts_q = []
            for first in range(g * GROUP, (g + 1) * GROUP, together):
                start = (r * heads + first % heads) * steps
                parts_q.append(held_ref[first // heads, start : start + together * steps, :])
            q = parts_q[0] if len(parts_q) == 1 else jnp.concatenate(parts_q, axis=0)
            old_scores = jnp.where(valid, dot_rows(q, cache_ref[r, 0, g]) * scale, -1e30)
            new_scores = jnp.where(causal, dot_rows(q, piece(g)) * scale, -1e30)
            highest = jnp.maximum(
                old_scores.max(-1, keepdims=True), new_scores.max(-1, keepdims=True)
            )
            old = jnp.exp(old_scores - highest)
            new = jnp.exp(new_scores - highest)
            total = old.sum(-1, keepdims=True) + new.sum(-1, keepdims=True)
            old = jnp.concatenate(split(old), axis=0)
            new = jnp.concatenate(split(new), axis=0)
            mixed = dot(old, cache_ref[r, 1, g]) + dot(new, piece(KV_HEADS + g))
            mixed = (mixed[:queries_count] + mixed[queries_count:]) / total
            for h in range(GROUP):
                head = g * GROUP + h
                lane = (head % heads) * HEAD_DIM
                attended_ref[
                    head // heads, r * steps : (r + 1) * steps, lane : lane + HEAD_DIM
                ] = mixed[h * steps : (h + 1) * steps]
    for k in range(parts):
        out_refs[k][...] = attended_ref[me ^ k].astype(BF16)


def collect_kernel(*refs, slot):
    factor_refs = refs[:-2]
    down_ref, up_ref = refs[-2:]
    me = lax.axis_index("fsdp")
    cut = up_ref.shape[2]
    per = down_ref.shape[1] // cut
    tall = RANK // per
    for k, factor_ref in enumerate(factor_refs):
        down_ref[pl.ds(pl.multiple_of((me ^ k) * slot, slot), slot), :] = factor_ref[0:slot, :]
        for c in range(per):
            up_ref[k, c * tall : (c + 1) * tall, :] = factor_ref[
                slot + c * tall : slot + (c + 1) * tall, c * cut : (c + 1) * cut
            ]


def project_kernel(*refs, parts, with_low):
    attended_refs = refs[:parts]
    weight_ref = refs[parts]
    rest = refs[parts + 1 :]
    if with_low:
        down_ref, rest = rest[0], rest[1:]
    keep_ref, send_ref = rest[0], rest[1]
    rows = jnp.concatenate([a[...] for a in attended_refs], axis=0)
    half = rows.shape[0] // 2
    out = dot(rows, weight_ref[...])
    keep_ref[...] = out[:half]
    send_ref[...] = out[half:].astype(BF16)
    if with_low:
        low_keep_ref, low_send_ref = rest[2], rest[3]

        @pl.when(pl.program_id(0) == 0)
        def _():
            low = dot_rows(rows, down_ref[...])
            low_keep_ref[...] = low[:half]
            high, rest_low = split(low[half:])
            low_send_ref[...] = jnp.concatenate([high, rest_low], axis=1)


def project(attended, weight, chunk, tile, down=None):
    parts = len(attended)
    tall, depth = attended[0].shape
    width = weight.shape[1] // CHUNKS
    half = parts * tall // 2
    tiles = width // tile
    out_shape = [
        jax.ShapeDtypeStruct((half, width), F32),
        jax.ShapeDtypeStruct((half, width), BF16),
    ]
    out_specs = [
        pl.BlockSpec((half, tile), lambda j: (0, j)),
        pl.BlockSpec((half, tile), lambda j: (0, j)),
    ]
    whole = lambda shape: pl.BlockSpec(shape, lambda j: (0, 0))
    in_specs = [whole((tall, depth))] * parts
    in_specs += [pl.BlockSpec((depth, tile), lambda j: (0, chunk * tiles + j))]
    args = [*attended, weight]
    if down is not None:
        in_specs += [whole(down.shape)]
        args += [down]
        out_shape += [
            jax.ShapeDtypeStruct((half, RANK), F32),
            jax.ShapeDtypeStruct((half, 2 * RANK), BF16),
        ]
        out_specs += [whole((half, RANK)), whole((half, 2 * RANK))]
    return pl.pallas_call(
        functools.partial(project_kernel, parts=parts, with_low=down is not None),
        grid=(tiles,),
        in_specs=in_specs,
        out_specs=out_specs,
        out_shape=out_shape,
        compiler_params=params(),
        name="project",
    )(*args)


def fold_low(keep, got):
    return keep + got[:, :RANK].astype(F32) + got[:, RANK:].astype(F32)


def finish_kernel(*refs, sets, cut, own, steps):
    sum_refs, refs = refs[: 2 * CHUNKS], refs[2 * CHUNKS :]
    low_keep_ref, low_got_ref, refs = refs[0], refs[1], refs[2:]
    *up_refs, out_ref, extra_ref = refs
    me, place = lax.axis_index("tensor"), lax.axis_index("fsdp")
    low = SCALE * fold_low(low_keep_ref[...], low_got_ref[...])
    tall = low.shape[0]
    low = jnp.concatenate(split(low), axis=0)
    if len(up_refs) == 1:
        both = dot(low, up_refs[0][...])
        extra_ref[...] = both[:tall] + both[tall:]
    else:
        for kt, up_ref in enumerate(up_refs):
            for kf in range(up_ref.shape[0]):
                both = dot(low, up_ref[kf])
                start = pl.multiple_of(((place ^ kf) * sets + (me ^ kt)) * cut, cut)
                extra_ref[:, pl.ds(start, cut)] = both[:tall] + both[tall:]
    width = sum_refs[0].shape[1]
    for c in range(CHUNKS):
        lanes = slice(c * width, (c + 1) * width)
        total = sum_refs[2 * c][...] + sum_refs[2 * c + 1][...].astype(F32) + extra_ref[:, lanes]
        total = total.astype(BF16)
        for r in range(own):
            out_ref[:, r, lanes] = total[r * steps : (r + 1) * steps]


def shards(queries, cache, new, lengths, weight, down, up):
    parts, spread = lax.axis_size("tensor"), lax.axis_size("fsdp")
    steps, rows, width = queries.shape
    own = rows // parts
    tall = own * steps
    depth, slot = down.shape
    cut = up.shape[1]
    heads, pieces = width // HEAD_DIM, new.shape[2] // HEAD_DIM
    swap = lambda x, axis, k: lax.ppermute(
        x, axis, [(i, i ^ k) for i in range(lax.axis_size(axis))]
    )

    block = jax.ShapeDtypeStruct((own * heads * steps + pieces * tall, HEAD_DIM), BF16)
    *blocks, factors = pl.pallas_call(
        functools.partial(pack_kernel, parts=parts, own=own, steps=steps),
        in_specs=[VMEM] * 4,
        out_specs=[VMEM] * (parts + 1),
        out_shape=[block] * parts + [jax.ShapeDtypeStruct((slot + RANK, depth), BF16)],
        compiler_params=params(),
        name="pack",
    )(queries, new, down, up)
    blocks = [blocks[0]] + [swap(blocks[k], "tensor", k) for k in range(1, parts)]
    factors = [factors] + [swap(factors, "fsdp", k) for k in range(1, spread)]

    attended = pl.pallas_call(
        functools.partial(attend_kernel, parts=parts, own=own, steps=steps),
        in_specs=[SMEM] + [VMEM] * (parts + 1),
        out_specs=[VMEM] * parts,
        out_shape=[jax.ShapeDtypeStruct((tall, width), BF16)] * parts,
        scratch_shapes=[
            pltpu.VMEM((parts,) + block.shape, BF16),
            pltpu.VMEM((parts, tall, width), F32),
        ],
        compiler_params=params(),
        name="attend",
    )(lengths, *blocks, cache)
    attended = [attended[0]] + [swap(attended[k], "tensor", k) for k in range(1, parts)]

    down_rows, ups = pl.pallas_call(
        functools.partial(collect_kernel, slot=slot),
        in_specs=[VMEM] * spread,
        out_specs=[VMEM] * 2,
        out_shape=[
            jax.ShapeDtypeStruct((RANK, depth), BF16),
            jax.ShapeDtypeStruct((spread, RANK, cut), BF16),
        ],
        compiler_params=params(),
        name="collect",
    )(*factors)
    if cut % HEAD_DIM:
        up_sets = {0: lax.all_gather(up, ("fsdp", "tensor"), axis=1, tiled=True)}
    else:
        up_sets = {0: ups}
        bit = parts // 2
        while bit:
            up_sets |= {k ^ bit: swap(u, "tensor", bit) for k, u in list(up_sets.items())}
            bit //= 2

    order = sorted(range(parts), key=lambda k: format(k, "08b")[::-1])
    attended = [attended[k] for k in order]
    sums = []
    low = None
    for c in range(CHUNKS):
        keep, send, *lows = project(
            attended, weight, c, min(512, weight.shape[1] // CHUNKS), down_rows if c == 0 else None
        )
        bit = 1
        while True:
            got = swap(send, "tensor", bit)
            if lows:
                low_keep, low_send = lows
                low_got = swap(low_send, "tensor", bit)
            bit *= 2
            if bit == parts:
                break
            both = keep + got.astype(F32)
            half = both.shape[0] // 2
            keep, send = both[:half], both[half:].astype(BF16)
            if lows:
                low_both = fold_low(low_keep, low_got)
                lows = low_both[:half], jnp.concatenate(split(low_both[half:]), axis=1)
        sums += [keep, got]
        if lows:
            low = [low_keep, low_got]

    return pl.pallas_call(
        functools.partial(finish_kernel, sets=parts, cut=cut, own=own, steps=steps),
        in_specs=[VMEM] * (2 * CHUNKS + 2 + len(up_sets)),
        out_specs=VMEM,
        out_shape=jax.ShapeDtypeStruct((steps, own, weight.shape[1]), BF16),
        scratch_shapes=[pltpu.VMEM((tall, weight.shape[1]), F32)],
        compiler_params=params(),
        name="finish",
    )(*sums, *low, *[up_sets[k] for k in range(len(up_sets))])


def solution(mesh):
    return jax.shard_map(
        shards,
        mesh=mesh,
        in_specs=(
            P(None, ("groups", "fsdp"), "tensor"),
            P(("groups", "fsdp", "tensor"), None, None, None, None),
            P(None, ("groups", "fsdp"), "tensor"),
            P(("groups", "fsdp", "tensor")),
            P("tensor", None),
            P("tensor", "fsdp"),
            P(None, ("fsdp", "tensor")),
        ),
        out_specs=P(None, ("groups", "fsdp", "tensor"), None),
        check_vma=False,
    )
```

time: 142 us -> 69.1 us (0.49)
  matrix products: 27.2 us -> 0 us
  Pallas kernels: 0 us -> 26.2 us
  local copies, waits for them, and re-layouts: 30.6 us -> 6.65 us
  waiting for transfers between devices: 41 us -> 17.7 us
  blocking collectives: 14.8 us -> 0 us
  between operations: 13.5 us -> 0.12 us
  starting transfers between devices: 11.1 us -> 17.8 us
  other arithmetic: 2.72 us -> 0.26 us
    reduce_scatter x1 -> x0, waiting for transfers between devices: 33.4 us -> none  [shards(): lax.psum_scatter(partial_out, 'tensor', scatter_dimension=1, tiled=True)]
    dot_general x5 -> x0, matrix products: 27.2 us -> none  [the longest x1 20.8 us: shards(): jnp.dot(head_major.reshape(steps_count * rows_dev, width_dev), combined_o...]
    pallas_call x0 -> x6, Pallas kernels: none -> 26.2 us  [the longest x2 19.2 us: project(): pl.pallas_call(functools.partial(project_kernel, parts=parts, with_low=do...]
    ppermute x0 -> x18, starting transfers between devices: none -> 17.8 us  [shards(): lax.ppermute(x, axis, [(i, i ^ k) for i in range(lax.axis_size(axis))])]
    ppermute x0 -> x18, waiting for transfers between devices: none -> 17.7 us  [shards(): lax.ppermute(x, axis, [(i, i ^ k) for i in range(lax.axis_size(axis))])]
    all_gather x1 -> x0, blocking collectives: 14.8 us -> none  [shards(): lax.all_gather(adapter_down_weight, 'fsdp', axis=1, tiled=True)]
    all_to_all x3 -> x0, starting transfers between devices: 11.1 us -> none  [the longest x1 4.24 us: shards(): lax.all_to_all(decoded_key_value, 'tensor', split_axis=1, concat_axis=2,...]
    unnamed x8 -> x11, local copies, waits for them, and re-layouts: 15.7 us -> 6.58 us
  transfers between devices with their start and end apart: 5 -> 18, of which waited for: 3 -> 7; matrix products, arithmetic and copies ran while one was open for 26% -> 0% of each run, Pallas kernels for 0% -> 36%
where the time goes in v1:
time: 69.1 us; the launch traced here: 68.7 us
  Pallas kernels  26.2 us (38%)
  starting transfers between devices  17.8 us (26%)
  waiting for transfers between devices  17.7 us (26%)
  local copies, waits for them, and re-layouts  6.65 us (10%)
    pallas_call x2, Pallas kernels, project(): pl.pallas_call(functools.partial(project_kernel, parts=parts, with_low=do...  19.2 us
    ppermute x18, starting transfers between devices, shards(): lax.ppermute(x, axis, [(i, i ^ k) for i in range(lax.axis_size(axis))])  17.8 us
    ppermute x18, waiting for transfers between devices, shards(): lax.ppermute(x, axis, [(i, i ^ k) for i in range(lax.axis_size(axis))])  17.7 us
    unnamed x11, local copies, waits for them, and re-layouts  6.58 us
    pallas_call x1, Pallas kernels, shards(): pl.pallas_call(functools.partial(attend_kernel, parts=parts, own=own, ste...  5.33 us
  transfers between devices with their start and end apart: 18, of which 7 were waited for; matrix products, arithmetic and copies ran while one was open for 0% of the time, Pallas kernels for 36%

profile of v1, /device:TPU:0, one launch (start us, length us, event | category | flops | bytes accessed | tf_op | source)
XLA Modules:
  0.0 68.7 jit_solution(2042831572468749530)
XLA Ops:
  0.0 1.1 %copy.8.down_ref = bf16[2048,16]{1,0:T(8,128)(2,1)S(1)} copy(bf16[2048,16]{0,1:T(8,128)(2,1)} %param.12) | data formatting | bytes 131072 | tf_op args[5]
  1.1 0.9 %copy-done.1 = bf16[8,8,2048]{2,1,0:T(8,128)(2,1)S(1)} copy-done((bf16[8,8,2048]{2,1,0:T(8,128)(2,1)S(1)}, bf16[8,8,2048]{2,1,0:T(8,128)(2,1)}, u32[]{:S(2)}) %copy-start.1) | copy-done | bytes 262168
  2.1 0.8 %copy-done.2 = bf16[8,8,512]{2,1,0:T(8,128)(2,1)S(1)} copy-done((bf16[8,8,512]{2,1,0:T(8,128)(2,1)S(1)}, bf16[8,8,512]{2,1,0:T(8,128)(2,1)}, u32[]{:S(2)}) %copy-start.2) | copy-done | bytes 65560
  2.9 0.8 %copy-done.3 = bf16[64,512]{1,0:T(8,128)(2,1)S(1)} copy-done((bf16[64,512]{1,0:T(8,128)(2,1)S(1)}, bf16[64,512]{1,0:T(8,128)(2,1)}, u32[]{:S(2)}) %copy-start.3) | copy-done | bytes 65560
  3.8 0.3 pack.1
  4.1 3.0 %collective-permute-start.6 = (bf16[80,2048]{1,0:T(8,128)(2,1)S(1)}, bf16[80,2048]{1,0:T(8,128)(2,1)S(1)}, u32[]{:S(2)}, u32[]{:S(2)}) collective-permute-start(bf16[80,2048]{1,0:T(8,128)(2,1)S(1)} %get-tuple-element.30.refs_0_), channel_id=1, source_target_pairs={{0,4},{4,0},{8,12},{12,8},{1,5},{5,1},{9,13},{13,9},{2,6},{6,2},{1... | collective-permute-start | bytes 983048 | tf_op jit(solution)/shard_map/ppermute | solution.py:256
  7.1 2.6 %collective-permute-start.7 = (bf16[80,2048]{1,0:T(8,128)(2,1)S(1)}, bf16[80,2048]{1,0:T(8,128)(2,1)S(1)}, u32[]{:S(2)}, u32[]{:S(2)}) collective-permute-start(bf16[80,2048]{1,0:T(8,128)(2,1)S(1)} %get-tuple-element.30.refs_0_), channel_id=1, source_target_pairs={{0,8},{4,12},{8,0},{12,4},{1,9},{5,13},{9,1},{13,5},{2,10},{6,14},... | collective-permute-start | bytes 983048 | tf_op jit(solution)/shard_map/ppermute | solution.py:256
  9.7 1.7 %collective-permute-start.1 = (bf16[320,128]{1,0:T(8,128)(2,1)S(1)}, bf16[320,128]{1,0:T(8,128)(2,1)S(1)}, u32[]{:S(2)}, u32[]{:S(2)}) collective-permute-start(bf16[320,128]{1,0:T(8,128)(2,1)S(1)} %get-tuple-element.24), channel_id=1, source_target_pairs={{0,2},{1,3},{2,0},{3,1},{4,6},{5,7},{6,4},{7,5},{8,10},{9,11},{10,... | collective-permute-start | bytes 245768 | tf_op jit(solution)/shard_map/ppermute | solution.py:256
  11.5 1.0 %collective-permute-start.2 = (bf16[320,128]{1,0:T(8,128)(2,1)S(1)}, bf16[320,128]{1,0:T(8,128)(2,1)S(1)}, u32[]{:S(2)}, u32[]{:S(2)}) collective-permute-start(bf16[320,128]{1,0:T(8,128)(2,1)S(1)} %get-tuple-element.25), channel_id=1, source_target_pairs={{0,3},{1,2},{2,1},{3,0},{4,7},{5,6},{6,5},{7,4},{8,11},{9,10},{10,... | collective-permute-start | bytes 245768 | tf_op jit(solution)/shard_map/ppermute | solution.py:256
  12.5 2.2 %collective-permute-done.1.refs_2_ = bf16[320,128]{1,0:T(8,128)(2,1)S(1)} collective-permute-done((bf16[320,128]{1,0:T(8,128)(2,1)S(1)}, bf16[320,128]{1,0:T(8,128)(2,1)S(1)}, u32[]{:S(2)}, u32[]{:S(2)}) %collective-permute-start.1) | collective-permute-done | bytes 81952 | tf_op jit(solution)/shard_map/ppermute | solution.py:256
  14.7 1.4 %collective-permute-done.2.refs_3_ = bf16[320,128]{1,0:T(8,128)(2,1)S(1)} collective-permute-done((bf16[320,128]{1,0:T(8,128)(2,1)S(1)}, bf16[320,128]{1,0:T(8,128)(2,1)S(1)}, u32[]{:S(2)}, u32[]{:S(2)}) %collective-permute-start.2) | collective-permute-done | bytes 81952 | tf_op jit(solution)/shard_map/ppermute | solution.py:256
  16.1 2.2 %copy-done = bf16[2,2,8,512,128]{4,3,2,1,0:T(8,128)(2,1)S(1)} copy-done((bf16[2,2,8,512,128]{4,3,2,1,0:T(8,128)(2,1)S(1)}, bf16[2,2,8,512,128]{4,3,2,1,0:T(8,128)(2,1)}, u32[]{:S(2)}) %copy-start) | copy-done | bytes 4194328
  18.3 0.7 copy-done.4
  18.9 5.3 %attend.1 = (bf16[16,2048]{1,0:T(8,128)(2,1)S(1)}, bf16[16,2048]{1,0:T(8,128)(2,1)S(1)}, bf16[16,2048]{1,0:T(8,128)(2,1)S(1)}, bf16[16,2048]{1,0:T(8,128)(2,1)S(1)}) custom-call(s32[2]{0:T(128)S(1)} %copy-done.4, bf16[320,128]{1,0:T(8,128)(2,1)S(1)} %get-tuple-element.22.refs_0_, bf16[320,128]{1,0:T(8,128)(2,1)S(1)} %collective-permute-done.refs_1_, ...), custom_call_target="tpu_custom_call" | custom-call | tf_op jit(solution)/shard_map/attend/pallas_call | solution.py:272
  24.3 1.7 %collective-permute-start.3 = (bf16[16,2048]{1,0:T(8,128)(2,1)S(1)}, bf16[16,2048]{1,0:T(8,128)(2,1)S(1)}, u32[]{:S(2)}, u32[]{:S(2)}) collective-permute-start(bf16[16,2048]{1,0:T(8,128)(2,1)S(1)} %get-tuple-element.27), channel_id=1, source_target_pairs={{0,2},{1,3},{2,0},{3,1},{4,6},{5,7},{6,4},{7,5},{8,10},{9,11},{10,... | collective-permute-start | bytes 196616 | tf_op jit(solution)/shard_map/ppermute | solution.py:256
  25.9 0.2 collective-permute-start.4
  26.2 2.5 %collective-permute-done.3.refs_1_ = bf16[16,2048]{1,0:T(8,128)(2,1)S(1)} collective-permute-done((bf16[16,2048]{1,0:T(8,128)(2,1)S(1)}, bf16[16,2048]{1,0:T(8,128)(2,1)S(1)}, u32[]{:S(2)}, u32[]{:S(2)}) %collective-permute-start.3) | collective-permute-done | bytes 65568 | tf_op jit(solution)/shard_map/ppermute | solution.py:256
  28.7 1.1 %collective-permute-start.5 = (bf16[16,2048]{1,0:T(8,128)(2,1)S(1)}, bf16[16,2048]{1,0:T(8,128)(2,1)S(1)}, u32[]{:S(2)}, u32[]{:S(2)}) collective-permute-start(bf16[16,2048]{1,0:T(8,128)(2,1)S(1)} %get-tuple-element.29), channel_id=1, source_target_pairs={{0,3},{1,2},{2,1},{3,0},{4,7},{5,6},{6,5},{7,4},{8,11},{9,10},{10,... | collective-permute-start | bytes 196616 | tf_op jit(solution)/shard_map/ppermute | solution.py:256
  29.8 3.0 %collective-permute-done.5.refs_3_ = bf16[16,2048]{1,0:T(8,128)(2,1)S(1)} collective-permute-done((bf16[16,2048]{1,0:T(8,128)(2,1)S(1)}, bf16[16,2048]{1,0:T(8,128)(2,1)S(1)}, u32[]{:S(2)}, u32[]{:S(2)}) %collective-permute-start.5) | collective-permute-done | bytes 65568 | tf_op jit(solution)/shard_map/ppermute | solution.py:256
  32.8 9.5 %project.3 = (f32[32,4096]{1,0:T(8,128)S(1)}, bf16[32,4096]{1,0:T(8,128)(2,1)S(1)}) custom-call(bf16[16,2048]{1,0:T(8,128)(2,1)S(1)} %get-tuple-element.26.refs_0_, bf16[16,2048]{1,0:T(8,128)(2,1)S(1)} %collective-permute-done.3.refs_1_, bf16[16,2048]{1,0:T(8,128)(2,1)S(1)} %collective-permute-done.4.refs_2_, ...), custom_call_target="tpu_custom_call" | custom-call | tf_op jit(solution)/shard_map/project/pallas_call | solution.py:207
  42.3 0.2 collective-permute-start.11
  42.5 9.7 %project.2 = (f32[32,4096]{1,0:T(8,128)S(1)}, bf16[32,4096]{1,0:T(8,128)(2,1)S(1)}, f32[32,64]{1,0:T(8,128)S(1)}, bf16[32,128]{1,0:T(8,128)(2,1)S(1)}) custom-call(bf16[16,2048]{1,0:T(8,128)(2,1)S(1)} %get-tuple-element.26.refs_0_, bf16[16,2048]{1,0:T(8,128)(2,1)S(1)} %collective-permute-done.3.refs_1_, bf16[16,2048]{1,0:T(8,128)(2,1)S(1)} %collective-permute-done.4.refs_2_, ...), custom_call_target="tpu_custom_call" | custom-call | tf_op jit(solution)/shard_map/project/pallas_call | solution.py:207
  52.3 0.5 collective-permute-start.13
  52.9 1.9 %collective-permute-start.16 = (bf16[4,64,512]{2,1,0:T(8,128)(2,1)S(1)}, bf16[4,64,512]{2,1,0:T(8,128)(2,1)S(1)}, u32[]{:S(2)}, u32[]{:S(2)}) collective-permute-start(bf16[4,64,512]{2,1,0:T(8,128)(2,1)S(1)} %get-tuple-element.38.refs_6_), channel_id=1, source_target_pairs={{0,2},{1,3},{2,0},{3,1},{4,6},{5,7},{6,4},{7,5},{8,10},{9,11},{10,... | collective-permute-start | bytes 786440 | tf_op jit(solution)/shard_map/ppermute | solution.py:256
  54.8 0.2 collective-permute-start.9
  55.1 0.6 collective-permute-start.12
  55.8 0.6 collective-permute-done.9
  56.4 0.9 %collective-permute-start.10 = (bf16[16,4096]{1,0:T(8,128)(2,1)S(1)}, bf16[16,4096]{1,0:T(8,128)(2,1)S(1)}, u32[]{:S(2)}, u32[]{:S(2)}) collective-permute-start(bf16[16,4096]{1,0:T(8,128)(2,1)S(1)} %slice.49), channel_id=1, source_target_pairs={{0,2},{1,3},{2,0},{3,1},{4,6},{5,7},{6,4},{7,5},{8,10},{9,11},{10,... | collective-permute-start | bytes 393224 | tf_op jit(solution)/shard_map/ppermute | solution.py:256
  57.4 4.6 %collective-permute-done.16.refs_8_ = bf16[4,64,512]{2,1,0:T(8,128)(2,1)S(1)} collective-permute-done((bf16[4,64,512]{2,1,0:T(8,128)(2,1)S(1)}, bf16[4,64,512]{2,1,0:T(8,128)(2,1)S(1)}, u32[]{:S(2)}, u32[]{:S(2)}) %collective-permute-start.16) | collective-permute-done | bytes 262176 | tf_op jit(solution)/shard_map/ppermute | solution.py:256
  62.1 1.9 %collective-permute-start.14 = (bf16[16,128]{1,0:T(8,128)(2,1)S(1)}, bf16[16,128]{1,0:T(8,128)(2,1)S(1)}, u32[]{:S(2)}, u32[]{:S(2)}) collective-permute-start(bf16[16,128]{1,0:T(8,128)(2,1)S(1)} %pad_maximum_fusion), channel_id=1, source_target_pairs={{0,2},{1,3},{2,0},{3,1},{4,6},{5,7},{6,4},{7,5},{8,10},{9,11},{10,... | collective-permute-start | bytes 12296 | tf_op jit(solution)/shard_map/ppermute | solution.py:256
  64.0 3.4 %collective-permute-done.14.refs_5_ = bf16[16,128]{1,0:T(8,128)(2,1)S(1)} collective-permute-done((bf16[16,128]{1,0:T(8,128)(2,1)S(1)}, bf16[16,128]{1,0:T(8,128)(2,1)S(1)}, u32[]{:S(2)}, u32[]{:S(2)}) %collective-permute-start.14) | collective-permute-done | bytes 4128 | tf_op jit(solution)/shard_map/ppermute | solution.py:256
  67.4 1.2 %finish.1 = bf16[8,2,8192]{2,1,0:T(2,128)(2,1)} custom-call(f32[16,4096]{1,0:T(8,128)S(1)} %slice.34.refs_0_, bf16[16,4096]{1,0:T(8,128)(2,1)S(1)} %collective-permute-done.10.refs_1_, f32[16,4096]{1,0:T(8,128)S(1)} %slice.36.refs_2_, bf16[16,4096]{1,0:T(8,128)(2,1)S(1)} %collective-permute-done.12.refs_3_, f32[16,64]{1,0:T(8,128)S(1)} %get-tuple-element.41.refs_4_, ...), custom_call_target="tpu_custom_call" | custom-call | tf_op jit(solution)/shard_map/finish/pallas_call | solution.py:333
  (30 shorter events, 0.5 us)
Async XLA Ops:
  1.1 1.0 %copy-start.1 = (bf16[8,8,2048]{2,1,0:T(8,128)(2,1)S(1)}, bf16[8,8,2048]{2,1,0:T(8,128)(2,1)}, u32[]{:S(2)}) copy-start(bf16[8,8,2048]{2,1,0:T(8,128)(2,1)} %query_ref.1) | copy-start | bytes 786436
  2.1 0.8 %copy-start.2 = (bf16[8,8,512]{2,1,0:T(8,128)(2,1)S(1)}, bf16[8,8,512]{2,1,0:T(8,128)(2,1)}, u32[]{:S(2)}) copy-start(bf16[8,8,512]{2,1,0:T(8,128)(2,1)} %new_ref.1) | copy-start | bytes 196612
  2.9 0.8 %copy-start.3 = (bf16[64,512]{1,0:T(8,128)(2,1)S(1)}, bf16[64,512]{1,0:T(8,128)(2,1)}, u32[]{:S(2)}) copy-start(bf16[64,512]{1,0:T(8,128)(2,1)} %up_ref.1) | copy-start | bytes 196612
  4.1 38.4 %collective-permute-start.6 = (bf16[80,2048]{1,0:T(8,128)(2,1)S(1)}, bf16[80,2048]{1,0:T(8,128)(2,1)S(1)}, u32[]{:S(2)}, u32[]{:S(2)}) collective-permute-start(bf16[80,2048]{1,0:T(8,128)(2,1)S(1)} %get-tuple-element.30.refs_0_), channel_id=1, source_target_pairs={{0,4},{4,0},{8,12},{12,8},{1,5},{5,1},{9,13},{13,9},{2,6},{6,2},{1... | collective-permute-start | bytes 983048 | tf_op jit(solution)/shard_map/ppermute | solution.py:256
  7.1 35.4 %collective-permute-start.7 = (bf16[80,2048]{1,0:T(8,128)(2,1)S(1)}, bf16[80,2048]{1,0:T(8,128)(2,1)S(1)}, u32[]{:S(2)}, u32[]{:S(2)}) collective-permute-start(bf16[80,2048]{1,0:T(8,128)(2,1)S(1)} %get-tuple-element.30.refs_0_), channel_id=1, source_target_pairs={{0,8},{4,12},{8,0},{12,4},{1,9},{5,13},{9,1},{13,5},{2,10},{6,14},... | collective-permute-start | bytes 983048 | tf_op jit(solution)/shard_map/ppermute | solution.py:256
  9.7 32.8 %collective-permute-start.8 = (bf16[80,2048]{1,0:T(8,128)(2,1)S(1)}, bf16[80,2048]{1,0:T(8,128)(2,1)S(1)}, u32[]{:S(2)}, u32[]{:S(2)}) collective-permute-start(bf16[80,2048]{1,0:T(8,128)(2,1)S(1)} %get-tuple-element.30.refs_0_), channel_id=1, source_target_pairs={{0,12},{4,8},{8,4},{12,0},{1,13},{5,9},{9,5},{13,1},{2,14},{6,10},... | collective-permute-start | bytes 983048 | tf_op jit(solution)/shard_map/ppermute | solution.py:256
  9.7 1.7 %collective-permute-start = (bf16[320,128]{1,0:T(8,128)(2,1)S(1)}, bf16[320,128]{1,0:T(8,128)(2,1)S(1)}, u32[]{:S(2)}, u32[]{:S(2)}) collective-permute-start(bf16[320,128]{1,0:T(8,128)(2,1)S(1)} %get-tuple-element.23), channel_id=1, source_target_pairs={{0,1},{1,0},{2,3},{3,2},{4,5},{5,4},{6,7},{7,6},{8,9},{9,8},{10,11... | collective-permute-start | bytes 245768 | tf_op jit(solution)/shard_map/ppermute | solution.py:256
  9.7 5.0 %collective-permute-start.1 = (bf16[320,128]{1,0:T(8,128)(2,1)S(1)}, bf16[320,128]{1,0:T(8,128)(2,1)S(1)}, u32[]{:S(2)}, u32[]{:S(2)}) collective-permute-start(bf16[320,128]{1,0:T(8,128)(2,1)S(1)} %get-tuple-element.24), channel_id=1, source_target_pairs={{0,2},{1,3},{2,0},{3,1},{4,6},{5,7},{6,4},{7,5},{8,10},{9,11},{10,... | collective-permute-start | bytes 245768 | tf_op jit(solution)/shard_map/ppermute | solution.py:256
  11.5 4.6 %collective-permute-start.2 = (bf16[320,128]{1,0:T(8,128)(2,1)S(1)}, bf16[320,128]{1,0:T(8,128)(2,1)S(1)}, u32[]{:S(2)}, u32[]{:S(2)}) collective-permute-start(bf16[320,128]{1,0:T(8,128)(2,1)S(1)} %get-tuple-element.25), channel_id=1, source_target_pairs={{0,3},{1,2},{2,1},{3,0},{4,7},{5,6},{6,5},{7,4},{8,11},{9,10},{10,... | collective-permute-start | bytes 245768 | tf_op jit(solution)/shard_map/ppermute | solution.py:256
  16.1 2.2 %copy-start = (bf16[2,2,8,512,128]{4,3,2,1,0:T(8,128)(2,1)S(1)}, bf16[2,2,8,512,128]{4,3,2,1,0:T(8,128)(2,1)}, u32[]{:S(2)}) copy-start(bf16[2,2,8,512,128]{4,3,2,1,0:T(8,128)(2,1)} %refs_4_.3) | copy-start | bytes 12582916
  18.3 0.7 copy-start.4
  24.3 4.5 %collective-permute-start.3 = (bf16[16,2048]{1,0:T(8,128)(2,1)S(1)}, bf16[16,2048]{1,0:T(8,128)(2,1)S(1)}, u32[]{:S(2)}, u32[]{:S(2)}) collective-permute-start(bf16[16,2048]{1,0:T(8,128)(2,1)S(1)} %get-tuple-element.27), channel_id=1, source_target_pairs={{0,2},{1,3},{2,0},{3,1},{4,6},{5,7},{6,4},{7,5},{8,10},{9,11},{10,... | collective-permute-start | bytes 196616 | tf_op jit(solution)/shard_map/ppermute | solution.py:256
  25.9 3.9 %collective-permute-start.4 = (bf16[16,2048]{1,0:T(8,128)(2,1)S(1)}, bf16[16,2048]{1,0:T(8,128)(2,1)S(1)}, u32[]{:S(2)}, u32[]{:S(2)}) collective-permute-start(bf16[16,2048]{1,0:T(8,128)(2,1)S(1)} %get-tuple-element.28), channel_id=1, source_target_pairs={{0,1},{1,0},{2,3},{3,2},{4,5},{5,4},{6,7},{7,6},{8,9},{9,8},{10,11... | collective-permute-start | bytes 196616 | tf_op jit(solution)/shard_map/ppermute | solution.py:256
  28.7 4.1 %collective-permute-start.5 = (bf16[16,2048]{1,0:T(8,128)(2,1)S(1)}, bf16[16,2048]{1,0:T(8,128)(2,1)S(1)}, u32[]{:S(2)}, u32[]{:S(2)}) collective-permute-start(bf16[16,2048]{1,0:T(8,128)(2,1)S(1)} %get-tuple-element.29), channel_id=1, source_target_pairs={{0,3},{1,2},{2,1},{3,0},{4,7},{5,6},{6,5},{7,4},{8,11},{9,10},{10,... | collective-permute-start | bytes 196616 | tf_op jit(solution)/shard_map/ppermute | solution.py:256
  42.3 12.7 %collective-permute-start.11 = (bf16[32,4096]{1,0:T(8,128)(2,1)S(1)}, bf16[32,4096]{1,0:T(8,128)(2,1)S(1)}, u32[]{:S(2)}, u32[]{:S(2)}) collective-permute-start(bf16[32,4096]{1,0:T(8,128)(2,1)S(1)} %get-tuple-element.35), channel_id=1, source_target_pairs={{0,1},{1,0},{2,3},{3,2},{4,5},{5,4},{6,7},{7,6},{8,9},{9,8},{10,11... | collective-permute-start | bytes 786440 | tf_op jit(solution)/shard_map/ppermute | solution.py:256
  52.3 2.7 %collective-permute-start.13 = (bf16[32,128]{1,0:T(8,128)(2,1)S(1)}, bf16[32,128]{1,0:T(8,128)(2,1)S(1)}, u32[]{:S(2)}, u32[]{:S(2)}) collective-permute-start(bf16[32,128]{1,0:T(8,128)(2,1)S(1)} %get-tuple-element.37), channel_id=1, source_target_pairs={{0,1},{1,0},{2,3},{3,2},{4,5},{5,4},{6,7},{7,6},{8,9},{9,8},{10,11... | collective-permute-start | bytes 24584 | tf_op jit(solution)/shard_map/ppermute | solution.py:256
  52.8 14.6 %collective-permute-start.15 = (bf16[4,64,512]{2,1,0:T(8,128)(2,1)S(1)}, bf16[4,64,512]{2,1,0:T(8,128)(2,1)S(1)}, u32[]{:S(2)}, u32[]{:S(2)}) collective-permute-start(bf16[4,64,512]{2,1,0:T(8,128)(2,1)S(1)} %get-tuple-element.38.refs_6_), channel_id=1, source_target_pairs={{0,1},{1,0},{2,3},{3,2},{4,5},{5,4},{6,7},{7,6},{8,9},{9,8},{10,11... | collective-permute-start | bytes 786440 | tf_op jit(solution)/shard_map/ppermute | solution.py:256
  52.9 9.1 %collective-permute-start.16 = (bf16[4,64,512]{2,1,0:T(8,128)(2,1)S(1)}, bf16[4,64,512]{2,1,0:T(8,128)(2,1)S(1)}, u32[]{:S(2)}, u32[]{:S(2)}) collective-permute-start(bf16[4,64,512]{2,1,0:T(8,128)(2,1)S(1)} %get-tuple-element.38.refs_6_), channel_id=1, source_target_pairs={{0,2},{1,3},{2,0},{3,1},{4,6},{5,7},{6,4},{7,5},{8,10},{9,11},{10,... | collective-permute-start | bytes 786440 | tf_op jit(solution)/shard_map/ppermute | solution.py:256
  54.8 1.5 %collective-permute-start.9 = (bf16[32,4096]{1,0:T(8,128)(2,1)S(1)}, bf16[32,4096]{1,0:T(8,128)(2,1)S(1)}, u32[]{:S(2)}, u32[]{:S(2)}) collective-permute-start(bf16[32,4096]{1,0:T(8,128)(2,1)S(1)} %get-tuple-element.33), channel_id=1, source_target_pairs={{0,1},{1,0},{2,3},{3,2},{4,5},{5,4},{6,7},{7,6},{8,9},{9,8},{10,11... | collective-permute-start | bytes 786440 | tf_op jit(solution)/shard_map/ppermute | solution.py:256
  55.1 12.3 %collective-permute-start.12 = (bf16[16,4096]{1,0:T(8,128)(2,1)S(1)}, bf16[16,4096]{1,0:T(8,128)(2,1)S(1)}, u32[]{:S(2)}, u32[]{:S(2)}) collective-permute-start(bf16[16,4096]{1,0:T(8,128)(2,1)S(1)} %slice.48), channel_id=1, source_target_pairs={{0,2},{1,3},{2,0},{3,1},{4,6},{5,7},{6,4},{7,5},{8,10},{9,11},{10,... | collective-permute-start | bytes 393224 | tf_op jit(solution)/shard_map/ppermute | solution.py:256
  56.4 11.0 %collective-permute-start.10 = (bf16[16,4096]{1,0:T(8,128)(2,1)S(1)}, bf16[16,4096]{1,0:T(8,128)(2,1)S(1)}, u32[]{:S(2)}, u32[]{:S(2)}) collective-permute-start(bf16[16,4096]{1,0:T(8,128)(2,1)S(1)} %slice.49), channel_id=1, source_target_pairs={{0,2},{1,3},{2,0},{3,1},{4,6},{5,7},{6,4},{7,5},{8,10},{9,11},{10,... | collective-permute-start | bytes 393224 | tf_op jit(solution)/shard_map/ppermute | solution.py:256
  62.0 5.4 %collective-permute-start.17 = (bf16[4,64,512]{2,1,0:T(8,128)(2,1)S(1)}, bf16[4,64,512]{2,1,0:T(8,128)(2,1)S(1)}, u32[]{:S(2)}, u32[]{:S(2)}) collective-permute-start(bf16[4,64,512]{2,1,0:T(8,128)(2,1)S(1)} %collective-permute-done.16.refs_8_), channel_id=1, source_target_pairs={{0,1},{1,0},{2,3},{3,2},{4,5},{5,4},{6,7},{7,6},{8,9},{9,8},{10,11... | collective-permute-start | bytes 786440 | tf_op jit(solution)/shard_map/ppermute | solution.py:256
  62.1 5.3 %collective-permute-start.14 = (bf16[16,128]{1,0:T(8,128)(2,1)S(1)}, bf16[16,128]{1,0:T(8,128)(2,1)S(1)}, u32[]{:S(2)}, u32[]{:S(2)}) collective-permute-start(bf16[16,128]{1,0:T(8,128)(2,1)S(1)} %pad_maximum_fusion), channel_id=1, source_target_pairs={{0,2},{1,3},{2,0},{3,1},{4,6},{5,7},{6,4},{7,5},{8,10},{9,11},{10,... | collective-permute-start | bytes 12296 | tf_op jit(solution)/shard_map/ppermute | solution.py:256

commit v2 on v1

v2 whole, which is shorter than its diff:
```python
import functools

import jax
import jax.numpy as jnp
from jax import lax
from jax.experimental import pallas as pl
from jax.experimental.pallas import tpu as pltpu
from jax.sharding import PartitionSpec as P

HEADS = 64
KV_HEADS = 8
HEAD_DIM = 128
GROUP = HEADS // KV_HEADS
RANK = 64
SCALE = 2.0
BF16 = jnp.bfloat16
F32 = jnp.float32
VMEM = pl.BlockSpec(memory_space=pltpu.VMEM)
ANY = pl.BlockSpec(memory_space=pl.ANY)
ROW_ROW = (((1,), (1,)), ((), ()))
shape_of = jax.ShapeDtypeStruct


def dot(a, b):
    return jnp.dot(a, b, preferred_element_type=F32)


def dot_rows(a, b):
    return lax.dot_general(a, b, ROW_ROW, preferred_element_type=F32)


def call(kernel, name, ins, outs, scratch=(), mib=16, cost=None):
    specs, args = zip(*ins)
    return pl.pallas_call(
        kernel,
        in_specs=list(specs),
        out_specs=[VMEM] * len(outs),
        out_shape=list(outs),
        scratch_shapes=list(scratch),
        compiler_params=pltpu.CompilerParams(vmem_limit_bytes=mib * 2**20),
        cost_estimate=cost,
        name=name,
    )(*args)


def split(x):
    high = x.astype(BF16)
    return high, (x - high.astype(F32)).astype(BF16)


def log2(n):
    return n.bit_length() - 1


def strip_copy(weight_ref, strip, own_half, index, into_ref, sem):
    width = into_ref.shape[1]
    top = lax.axis_index("tensor") >> (log2(lax.axis_size("tensor")) - 1)
    half = top if own_half else 1 - top
    start = pl.multiple_of((2 * strip + half) * width, width)
    return pltpu.make_async_copy(weight_ref.at[:, pl.ds(start, width)], into_ref, sem.at[index])


def pack_kernel(query_hbm, new_hbm, down_hbm, up_hbm, *refs, parts, own, steps):
    block_refs, factor_ref = refs[:parts], refs[parts]
    query_ref, new_ref, down_ref, up_ref, sem = refs[parts + 1 :]
    copies = [
        pltpu.make_async_copy(a, b, sem.at[i])
        for i, (a, b) in enumerate(
            [(query_hbm, query_ref), (new_hbm, new_ref), (down_hbm, down_ref), (up_hbm, up_ref)]
        )
    ]
    for copy in copies:
        copy.start()
    me = lax.axis_index("tensor")
    count = steps * parts * own
    i = lax.broadcasted_iota(jnp.int32, (count, count), 0)
    j = lax.broadcasted_iota(jnp.int32, (count, count), 1)
    step_out = i & (steps - 1)
    row_out = (i >> log2(steps)) & (own - 1)
    part_out = (i >> log2(steps * own)) ^ me
    source = step_out * (parts * own) + part_out * own + row_out
    select = jnp.where(source == j, 1.0, 0.0).astype(BF16)
    for copy in copies:
        copy.wait()
    queries = dot(select, query_ref[...].reshape(count, query_ref.shape[2]))
    new = dot(select, new_ref[...].reshape(count, new_ref.shape[2]))
    heads = queries.shape[1] // HEAD_DIM
    pieces = new.shape[1] // HEAD_DIM
    tall = own * steps
    for k, block_ref in enumerate(block_refs):
        q = queries[k * tall : (k + 1) * tall]
        n = new[k * tall : (k + 1) * tall]
        tiles = [
            q[r * steps : (r + 1) * steps, h * HEAD_DIM : (h + 1) * HEAD_DIM]
            for r in range(own)
            for h in range(heads)
        ]
        tiles += [n[:, c * HEAD_DIM : (c + 1) * HEAD_DIM] for c in range(pieces)]
        block_ref[...] = jnp.concatenate(tiles, axis=0).astype(BF16)
    slot, depth = down_ref.shape
    cut = up_ref.shape[1]
    per = depth // cut
    tall = RANK // per
    factor_ref[0:slot, :] = down_ref[...]
    for c in range(per):
        factor_ref[slot : slot + tall, c * cut : (c + 1) * cut] = up_ref[c * tall : (c + 1) * tall, :]


def attend_kernel(length_hbm, *refs, parts, own, steps, strips):
    block_refs, refs = refs[:parts], refs[parts:]
    cache_hbm, weight_hbm, refs = refs[0], refs[1], refs[2:]
    out_refs, refs = refs[:parts], refs[parts:]
    strip_refs, refs = refs[:strips], refs[strips:]
    cache_ref, length_ref, held_ref, attended_ref, cache_sem, sem = refs
    length_copy = pltpu.make_async_copy(length_hbm, length_ref, sem.at[strips])
    length_copy.start()
    pairs = KV_HEADS // 2

    def cache_copy(r, p, part):
        two = pl.ds(2 * p, 2)
        return pltpu.make_async_copy(
            cache_hbm.at[r, part, two], cache_ref.at[r, part, two], cache_sem.at[r, p, part]
        )

    for r in range(own):
        for p in range(pairs):
            cache_copy(r, p, 0).start()
            cache_copy(r, p, 1).start()
    weight_copies = [
        strip_copy(weight_hbm, i, False, i, strip_refs[i], sem) for i in range(strips)
    ]
    for copy in weight_copies:
        copy.start()

    me = lax.axis_index("tensor")
    for k in range(parts):
        held_ref[me ^ k] = block_refs[k][...]
    heads = HEADS // parts
    pieces = 2 * KV_HEADS // parts
    query_rows = own * heads * steps
    tall = own * steps
    slots = cache_ref.shape[3]
    together = min(heads, GROUP)
    scale = HEAD_DIM ** (-0.5)
    count = GROUP * steps

    def piece(c):
        start = query_rows + (c % pieces) * tall
        return held_ref[c // pieces, start : start + tall, :]

    def beside(a, b):
        return jnp.concatenate([a, b], axis=1)

    slot_ids = lax.broadcasted_iota(jnp.int32, (2 * count, slots), 1)
    step_ids = lax.broadcasted_iota(jnp.int32, (2 * count, tall), 0) & (steps - 1)
    new_ids = lax.broadcasted_iota(jnp.int32, (2 * count, tall), 1)
    blank = jnp.zeros((count, HEAD_DIM), BF16)
    length_copy.wait()
    for r in range(own):
        valid = slot_ids < length_ref[r]
        past = new_ids - r * steps
        causal = (past >= 0) & (past <= step_ids)
        for p in range(pairs):
            q = []
            for g in (2 * p, 2 * p + 1):
                found = []
                for first in range(g * GROUP, (g + 1) * GROUP, together):
                    start = (r * heads + first % heads) * steps
                    found.append(held_ref[first // heads, start : start + together * steps, :])
                q.append(found[0] if len(found) == 1 else jnp.concatenate(found, axis=0))
            q = jnp.concatenate([beside(q[0], blank), beside(blank, q[1])], axis=0)
            cache_copy(r, p, 0).wait()
            keys = beside(cache_ref[r, 0, 2 * p], cache_ref[r, 0, 2 * p + 1])
            new_keys = beside(piece(2 * p), piece(2 * p + 1))
            old_scores = jnp.where(valid, dot_rows(q, keys) * scale, -1e30)
            new_scores = jnp.where(causal, dot_rows(q, new_keys) * scale, -1e30)
            highest = jnp.maximum(
                old_scores.max(-1, keepdims=True), new_scores.max(-1, keepdims=True)
            )
            old = jnp.exp(old_scores - highest)
            new = jnp.exp(new_scores - highest)
            total = old.sum(-1, keepdims=True) + new.sum(-1, keepdims=True)
            old = jnp.concatenate(split(old), axis=0)
            new = jnp.concatenate(split(new), axis=0)
            cache_copy(r, p, 1).wait()
            values = beside(cache_ref[r, 1, 2 * p], cache_ref[r, 1, 2 * p + 1])
            new_values = beside(piece(KV_HEADS + 2 * p), piece(KV_HEADS + 2 * p + 1))
            mixed = dot(old, values) + dot(new, new_values)
            mixed = (mixed[: 2 * count] + mixed[2 * count :]) / total
            for side in range(2):
                for h in range(GROUP):
                    head = (2 * p + side) * GROUP + h
                    lane = (head % heads) * HEAD_DIM
                    row = side * count + h * steps
                    attended_ref[
                        head // heads, r * steps : (r + 1) * steps, lane : lane + HEAD_DIM
                    ] = mixed[row : row + steps, side * HEAD_DIM : (side + 1) * HEAD_DIM]
    for k in range(parts):
        out_refs[k][...] = attended_ref[me ^ k].astype(BF16)
    for copy in weight_copies:
        copy.wait()


def collect_kernel(*refs, slot):
    *factor_refs, down_ref, up_ref = refs
    me = lax.axis_index("fsdp")
    cut = up_ref.shape[2]
    per = down_ref.shape[1] // cut
    tall = RANK // per
    for k, factor_ref in enumerate(factor_refs):
        down_ref[pl.ds(pl.multiple_of((me ^ k) * slot, slot), slot), :] = factor_ref[0:slot, :]
        for c in range(per):
            up_ref[k, c * tall : (c + 1) * tall, :] = factor_ref[
                slot : slot + tall, c * cut : (c + 1) * cut
            ]


def fetch_kernel(after_ref, weight_hbm, *refs, first):
    *strip_refs, sem = refs
    copies = [
        strip_copy(weight_hbm, first + i, False, i, strip_ref, sem)
        for i, strip_ref in enumerate(strip_refs)
    ]
    for copy in copies:
        copy.start()
    for copy in copies:
        copy.wait()


def project_kernel(*refs, parts, held, ahead, late, first, with_low):
    attended_refs, refs = refs[:parts], refs[parts:]
    held_refs, refs = refs[:held], refs[held:]
    weight_hbm, refs = refs[0], refs[1:]
    if with_low:
        down_ref, refs = refs[0], refs[1:]
    keep_ref, send_ref, refs = refs[0], refs[1], refs[2:]
    if with_low:
        low_keep_ref, low_send_ref, refs = refs[0], refs[1], refs[2:]
    ahead_refs, refs = refs[:ahead], refs[ahead:]
    late_refs, sem = refs[:late], refs[-1]
    copies = [
        strip_copy(weight_hbm, first + i, True, i, ref, sem)
        for i, ref in enumerate([*late_refs, *ahead_refs])
    ]
    for copy in copies:
        copy.start()
    rows = jnp.concatenate([a[...] for a in attended_refs], axis=0)
    half = rows.shape[0] // 2
    if with_low:
        low = dot_rows(rows, down_ref[...])
        low_keep_ref[...] = low[:half]
        low_send_ref[...] = jnp.concatenate(split(low[half:]), axis=1)
    for i, strip_ref in enumerate([*held_refs, *late_refs]):
        if i >= held:
            copies[i - held].wait()
        width = strip_ref.shape[1]
        lanes = slice(i * width, (i + 1) * width)
        out = dot(rows, strip_ref[...])
        keep_ref[:, lanes] = out[:half]
        send_ref[:, lanes] = out[half:].astype(BF16)
    for copy in copies[late:]:
        copy.wait()


def project(attended, held, weight, wide, ahead=0, late=0, first=0, down=None):
    parts = len(attended)
    tall, depth = attended[0].shape
    half = parts * tall // 2
    width = wide * (len(held) + late)
    outs = [shape_of((half, width), F32), shape_of((half, width), BF16)]
    ins = [(VMEM, a) for a in attended] + [(VMEM, h) for h in held] + [(ANY, weight)]
    if down is not None:
        ins += [(VMEM, down)]
        outs += [shape_of((half, RANK), F32), shape_of((half, 2 * RANK), BF16)]
    strip = pltpu.VMEM((depth, wide), BF16)
    outs += [strip] * ahead
    scratch = [strip] * late + [pltpu.SemaphoreType.DMA((max(ahead + late, 1),))]
    kernel = functools.partial(
        project_kernel,
        parts=parts,
        held=len(held),
        ahead=ahead,
        late=late,
        first=first,
        with_low=down is not None,
    )
    cost = pl.CostEstimate(
        flops=2 * parts * tall * depth * width, bytes_accessed=2 * depth * width, transcendentals=0
    )
    return call(kernel, "project", ins, outs, scratch, cost=cost)


def fold_low(keep, got):
    return keep + got[:, :RANK].astype(F32) + got[:, RANK:].astype(F32)


def adapt_kernel(*refs, pieces, sets, ordered):
    low_ref, low_got_ref, refs = refs[0], refs[1], refs[2:]
    keep_refs, refs = refs[:pieces], refs[pieces:]
    got_refs, refs = refs[:pieces], refs[pieces:]
    up_refs, (own_ref, send_ref, extra_ref) = refs[:sets], refs[sets:]
    me, place = lax.axis_index("tensor"), lax.axis_index("fsdp")
    half = low_ref.shape[0] // 2
    got = low_got_ref[...]
    got = jnp.concatenate([got[:, : 2 * RANK], got[:, 2 * RANK :]], axis=0)
    low = SCALE * fold_low(low_ref[...], got)
    low = jnp.concatenate(split(low), axis=0)
    if ordered:
        both = dot(low, up_refs[0][...])
        extra_ref[...] = both[: 2 * half] + both[2 * half :]
    else:
        cut = up_refs[0].shape[2]
        for kt, up_ref in enumerate(up_refs):
            for kf in range(up_ref.shape[0]):
                both = dot(low, up_ref[kf])
                column = (place ^ kf) * sets + ((me ^ kt) & (sets - 1))
                start = pl.multiple_of(column * cut, cut)
                extra_ref[:, pl.ds(start, cut)] = both[: 2 * half] + both[2 * half :]
    first = 0
    for keep_ref, got_ref in zip(keep_refs, got_refs):
        lanes = slice(first, first + keep_ref.shape[1])
        first += keep_ref.shape[1]
        total = keep_ref[...] + got_ref[...].astype(F32) + extra_ref[:, lanes]
        own_ref[:, lanes] = total[:half]
        send_ref[:, lanes] = total[half:].astype(BF16)


def finish_kernel(far_ref, far_got_ref, near_ref, near_got_ref, out_ref, *, own, steps, strips):
    top = lax.axis_index("tensor") >> (log2(lax.axis_size("tensor")) - 1)
    wide = near_ref.shape[1] // strips
    for keep_ref, got_ref, half in ((near_ref, near_got_ref, top), (far_ref, far_got_ref, 1 - top)):
        for i in range(strips):
            lanes = slice(i * wide, (i + 1) * wide)
            total = (keep_ref[:, lanes] + got_ref[:, lanes].astype(F32)).astype(BF16)
            start = pl.multiple_of((2 * i + half) * wide, wide)
            for r in range(own):
                out_ref[:, r, pl.ds(start, wide)] = total[r * steps : (r + 1) * steps]


def shards(queries, cache, new, lengths, weight, down, up):
    parts, spread = lax.axis_size("tensor"), lax.axis_size("fsdp")
    steps, rows, width = queries.shape
    own = rows // parts
    tall = own * steps
    depth, slot = down.shape
    cut = up.shape[1]
    heads, pieces = width // HEAD_DIM, new.shape[2] // HEAD_DIM
    sets = parts // 2
    wide = sets * cut
    half_width = spread * wide
    swap = lambda x, axis, k: lax.ppermute(
        x, axis, [(i, i ^ k) for i in range(lax.axis_size(axis))]
    )

    block = shape_of((own * heads * steps + pieces * tall, HEAD_DIM), BF16)
    per = depth // cut
    sources = (queries, new, down.T, up)
    *blocks, factors = call(
        functools.partial(pack_kernel, parts=parts, own=own, steps=steps),
        "pack",
        [(ANY, a) for a in sources],
        [block] * parts + [shape_of((slot + RANK // per, depth), BF16)],
        [pltpu.VMEM(a.shape, BF16) for a in sources] + [pltpu.SemaphoreType.DMA((4,))],
    )
    got = {k: swap(blocks[k], "tensor", k) for k in range(parts - 1, 0, -1)}
    blocks = [blocks[0]] + [got[k] for k in range(1, parts)]
    factors, blocks[1] = lax.optimization_barrier((factors, blocks[1]))
    factors = [factors] + [swap(factors, "fsdp", k) for k in range(1, spread)]

    strip = pltpu.VMEM((depth, wide), BF16)
    early = spread // 2
    attended, fetched = None, None
    outs = call(
        functools.partial(attend_kernel, parts=parts, own=own, steps=steps, strips=early),
        "attend",
        [(ANY, lengths)] + [(VMEM, b) for b in blocks] + [(ANY, cache), (ANY, weight)],
        [shape_of((tall, width), BF16)] * parts + [strip] * early,
        [
            pltpu.VMEM(cache.shape, BF16),
            pltpu.SMEM(lengths.shape, jnp.int32),
            pltpu.VMEM((parts,) + block.shape, BF16),
            pltpu.VMEM((parts, tall, width), F32),
            pltpu.SemaphoreType.DMA((own, KV_HEADS // 2, 2)),
            pltpu.SemaphoreType.DMA((early + 1,)),
        ],
    )
    attended, far_strips = outs[:parts], outs[parts:]
    far_strips += call(
        functools.partial(fetch_kernel, first=early),
        "fetch",
        [(ANY, attended[0]), (ANY, weight)],
        [strip] * (spread - early),
        [pltpu.SemaphoreType.DMA((spread - early,))],
        cost=pl.CostEstimate(
            flops=0, bytes_accessed=2 * (spread - early) * depth * wide, transcendentals=0
        ),
    )
    got = {k: swap(attended[k], "tensor", k) for k in range(parts - 1, 0, -1)}
    attended = [attended[0]] + [got[k] for k in range(1, parts)]

    down_rows, ups = call(
        functools.partial(collect_kernel, slot=slot),
        "collect",
        [(VMEM, f) for f in factors],
        [shape_of((RANK, depth), BF16), shape_of((spread, RANK, cut), BF16)],
    )
    ordered = cut % HEAD_DIM != 0
    if ordered:
        ups = lax.all_gather(up, ("fsdp", "tensor"), axis=1, tiled=True)
        ups = ups.reshape(RANK, spread, 2, wide)
        top = lax.axis_index("tensor") // sets
        ups = lax.dynamic_index_in_dim(ups, top, 2, keepdims=False)
        up_sets = {0: ups.reshape(RANK, half_width)}
    else:
        up_sets = {0: ups}
        bit = sets // 2
        while bit:
            up_sets |= {k ^ bit: swap(u, "tensor", bit) for k, u in list(up_sets.items())}
            bit //= 2

    order = sorted(range(parts), key=lambda k: format(k, "08b")[::-1])
    attended = [attended[k] for k in order]

    def reduce(keep, send):
        bit = 1
        while True:
            got = swap(send, "tensor", bit)
            bit *= 2
            if bit == sets:
                return keep, got
            both = keep + got.astype(F32)
            half = both.shape[0] // 2
            keep, send = both[:half], both[half:].astype(BF16)

    def reduce_low(keep, send):
        bit = 1
        while True:
            both = fold_low(keep, swap(send, "tensor", bit))
            bit *= 2
            if bit == sets:
                return both
            half = both.shape[0] // 2
            keep, send = both[:half], jnp.concatenate(split(both[half:]), axis=1)

    near = spread // 2
    middle = spread // 4
    keep, send, low_keep, low_send, *near_strips = project(
        attended, far_strips, weight, wide, ahead=near, down=down_rows
    )
    far_keep, far_got = reduce(keep, send)
    low = reduce_low(low_keep, low_send)
    keep_a, send_a, *later_strips = project(
        attended, near_strips, weight, wide, ahead=middle, first=near
    )
    keep_a, got_a = reduce(keep_a, send_a)
    keep_b, send_b = project(
        attended, later_strips, weight, wide, late=spread - near - middle, first=near + middle
    )
    keep_b, got_b = reduce(keep_b, send_b)

    far = far_keep + far_got.astype(F32)
    low_parts = jnp.concatenate(split(low), axis=1)
    message = jnp.concatenate([far[tall:].astype(BF16), low_parts[tall:], low_parts[:tall]], axis=1)
    message = swap(message, "tensor", sets)
    near_got, low_got = message[:, :half_width], message[:, half_width:]

    ups = [up_sets[k] for k in range(len(up_sets))]
    near_keep, near_send = call(
        functools.partial(adapt_kernel, pieces=2, sets=len(ups), ordered=ordered),
        "adapt",
        [(VMEM, a) for a in (low, low_got, keep_a, keep_b, got_a, got_b, *ups)],
        [shape_of((tall, half_width), F32), shape_of((tall, half_width), BF16)],
        [pltpu.VMEM((2 * tall, half_width), F32)],
    )
    far_got = swap(near_send, "tensor", sets)

    return call(
        functools.partial(finish_kernel, own=own, steps=steps, strips=spread),
        "finish",
        [(VMEM, a) for a in (far[:tall], far_got, near_keep, near_got)],
        [shape_of((steps, own, weight.shape[1]), BF16)],
    )[0]


def solution(mesh):
    return jax.shard_map(
        shards,
        mesh=mesh,
        in_specs=(
            P(None, ("groups", "fsdp"), "tensor"),
            P(("groups", "fsdp", "tensor"), None, None, None, None),
            P(None, ("groups", "fsdp"), "tensor"),
            P(("groups", "fsdp", "tensor")),
            P("tensor", None),
            P("tensor", "fsdp"),
            P(None, ("fsdp", "tensor")),
        ),
        out_specs=P(None, ("groups", "fsdp", "tensor"), None),
        check_vma=False,
    )
```

time: 69.1 us -> 65.1 us (0.942)
  local copies, waits for them, and re-layouts: 6.65 us -> 16.9 us
  waiting for transfers between devices: 17.7 us -> 8.71 us
  starting transfers between devices: 17.8 us -> 13.3 us
  Pallas kernels: 26.2 us -> 25.3 us
    unnamed x11 -> x14, local copies, waits for them, and re-layouts: 6.58 us -> 16.9 us
    ppermute x18 -> x16, waiting for transfers between devices: 17.7 us -> 8.71 us  [shards(): lax.ppermute(x, axis, [(i, i ^ k) for i in range(lax.axis_size(axis))])]
    ppermute x18 -> x16, starting transfers between devices: 17.8 us -> 13.3 us  [shards(): lax.ppermute(x, axis, [(i, i ^ k) for i in range(lax.axis_size(axis))])]
    pallas_call x6 -> x9, Pallas kernels: 26.2 us -> 25.3 us  [call(): pl.pallas_call(kernel, in_specs=list(specs), out_specs=[VMEM] * len(outs)...]
  transfers between devices with their start and end apart: 18 -> 16, of which waited for: 7 -> 6; matrix products, arithmetic and copies ran while one was open for 0% -> 1% of each run, Pallas kernels for 36% -> 26%
where the time goes in v2:
time: 65.1 us; the launch traced here: 64.7 us
  Pallas kernels  25.3 us (39%)
  local copies, waits for them, and re-layouts  16.9 us (26%)
  starting transfers between devices  13.3 us (20%)
  waiting for transfers between devices  8.71 us (13%)
    pallas_call x9, Pallas kernels, call(): pl.pallas_call(kernel, in_specs=list(specs), out_specs=[VMEM] * len(outs)...  25.3 us
    unnamed x14, local copies, waits for them, and re-layouts  16.9 us
    ppermute x16, starting transfers between devices, shards(): lax.ppermute(x, axis, [(i, i ^ k) for i in range(lax.axis_size(axis))])  13.3 us
    ppermute x16, waiting for transfers between devices, shards(): lax.ppermute(x, axis, [(i, i ^ k) for i in range(lax.axis_size(axis))])  8.71 us
  transfers between devices with their start and end apart: 16, of which 6 were waited for; matrix products, arithmetic and copies ran while one was open for 1% of the time, Pallas kernels for 26%

profile of v2, /device:TPU:0, one launch (start us, length us, event | category | flops | bytes accessed | tf_op | source)
XLA Modules:
  0.0 64.7 jit_solution(7475503873895110728)
XLA Ops:
  0.0 0.9 %copy-done.2 = bf16[8,8,2048]{2,1,0:T(8,128)(2,1)S(1)} copy-done((bf16[8,8,2048]{2,1,0:T(8,128)(2,1)S(1)}, bf16[8,8,2048]{2,1,0:T(8,128)(2,1)}, u32[]{:S(2)}) %copy-start.2) | copy-done | bytes 262168
  1.0 0.8 %copy-done.3 = bf16[8,8,512]{2,1,0:T(8,128)(2,1)S(1)} copy-done((bf16[8,8,512]{2,1,0:T(8,128)(2,1)S(1)}, bf16[8,8,512]{2,1,0:T(8,128)(2,1)}, u32[]{:S(2)}) %copy-start.3) | copy-done | bytes 65560
  1.8 0.8 %copy-done.4 = bf16[2048,16]{0,1:T(8,128)(2,1)S(1)} copy-done((bf16[2048,16]{0,1:T(8,128)(2,1)S(1)}, bf16[2048,16]{0,1:T(8,128)(2,1)}, u32[]{:S(2)}) %copy-start.4) | copy-done | bytes 65560
  2.6 0.8 %copy-done.5 = bf16[64,512]{1,0:T(8,128)(2,1)S(1)} copy-done((bf16[64,512]{1,0:T(8,128)(2,1)S(1)}, bf16[64,512]{1,0:T(8,128)(2,1)}, u32[]{:S(2)}) %copy-start.5) | copy-done | bytes 65560
  3.5 0.6 pack.1
  4.0 0.5 collective-permute-start
  4.6 0.9 %collective-permute-done.refs_1_ = bf16[320,128]{1,0:T(8,128)(2,1)S(1)} collective-permute-done((bf16[320,128]{1,0:T(8,128)(2,1)S(1)}, bf16[320,128]{1,0:T(8,128)(2,1)S(1)}, u32[]{:S(2)}, u32[]{:S(2)}) %collective-permute-start) | collective-permute-done | bytes 81952 | tf_op jit(solution)/shard_map/ppermute | solution.py:351
  5.5 2.9 %collective-permute-start.6 = (bf16[32,2048]{1,0:T(8,128)(2,1)S(1)}, bf16[32,2048]{1,0:T(8,128)(2,1)S(1)}, u32[]{:S(2)}, u32[]{:S(2)}) collective-permute-start(bf16[32,2048]{1,0:T(8,128)(2,1)S(1)} %get-tuple-element.49.refs_0_), channel_id=1, source_target_pairs={{0,4},{4,0},{8,12},{12,8},{1,5},{5,1},{9,13},{13,9},{2,6},{6,2},{1... | collective-permute-start | bytes 393224 | tf_op jit(solution)/shard_map/ppermute | solution.py:351
  8.4 1.5 %collective-permute-start.1 = (bf16[320,128]{1,0:T(8,128)(2,1)S(1)}, bf16[320,128]{1,0:T(8,128)(2,1)S(1)}, u32[]{:S(2)}, u32[]{:S(2)}) collective-permute-start(bf16[320,128]{1,0:T(8,128)(2,1)S(1)} %get-tuple-element.39), channel_id=1, source_target_pairs={{0,2},{1,3},{2,0},{3,1},{4,6},{5,7},{6,4},{7,5},{8,10},{9,11},{10,... | collective-permute-start | bytes 245768 | tf_op jit(solution)/shard_map/ppermute | solution.py:351
  9.9 2.6 %collective-permute-start.7 = (bf16[32,2048]{1,0:T(8,128)(2,1)S(1)}, bf16[32,2048]{1,0:T(8,128)(2,1)S(1)}, u32[]{:S(2)}, u32[]{:S(2)}) collective-permute-start(bf16[32,2048]{1,0:T(8,128)(2,1)S(1)} %get-tuple-element.49.refs_0_), channel_id=1, source_target_pairs={{0,8},{4,12},{8,0},{12,4},{1,9},{5,13},{9,1},{13,5},{2,10},{6,14},... | collective-permute-start | bytes 393224 | tf_op jit(solution)/shard_map/ppermute | solution.py:351
  12.5 0.2 collective-permute-start.8
  12.8 1.8 %collective-permute-done.2.refs_3_ = bf16[320,128]{1,0:T(8,128)(2,1)S(1)} collective-permute-done((bf16[320,128]{1,0:T(8,128)(2,1)S(1)}, bf16[320,128]{1,0:T(8,128)(2,1)S(1)}, u32[]{:S(2)}, u32[]{:S(2)}) %collective-permute-start.2) | collective-permute-done | bytes 81952 | tf_op jit(solution)/shard_map/ppermute | solution.py:351
  14.6 2.2 %copy-done.1 = bf16[2,2,8,512,128]{4,3,2,1,0:T(8,128)(2,1)S(1)} copy-done((bf16[2,2,8,512,128]{4,3,2,1,0:T(8,128)(2,1)S(1)}, bf16[2,2,8,512,128]{4,3,2,1,0:T(8,128)(2,1)}, u32[]{:S(2)}) %copy-start.1) | copy-done | bytes 4194328
  16.8 0.7 %copy-done.6 = s32[2]{0:T(128)S(1)} copy-done((s32[2]{0:T(128)S(1)}, s32[2]{0:T(128)}, u32[]{:S(2)}) %copy-start.6) | copy-done | bytes 32
  17.4 7.4 %attend.1 = (bf16[16,2048]{1,0:T(8,128)(2,1)S(1)}, bf16[16,2048]{1,0:T(8,128)(2,1)S(1)}, bf16[16,2048]{1,0:T(8,128)(2,1)S(1)}, bf16[16,2048]{1,0:T(8,128)(2,1)S(...) custom-call(s32[2]{0:T(128)S(1)} %copy-done.6, bf16[320,128]{1,0:T(8,128)(2,1)S(1)} %get-tuple-element.35.refs_0_, ...), custom_call_target="tpu_custom_call" | custom-call | tf_op jit(solution)/shard_map/attend/pallas_call | solution.py:34
  24.9 0.6 %collective-permute-start.3 = (bf16[16,2048]{1,0:T(8,128)(2,1)S(1)}, bf16[16,2048]{1,0:T(8,128)(2,1)S(1)}, u32[]{:S(2)}, u32[]{:S(2)}) collective-permute-start(bf16[16,2048]{1,0:T(8,128)(2,1)S(1)} %get-tuple-element.42), channel_id=1, source_target_pairs={{0,2},{1,3},{2,0},{3,1},{4,6},{5,7},{6,4},{7,5},{8,10},{9,11},{10,... | collective-permute-start | bytes 196616 | tf_op jit(solution)/shard_map/ppermute | solution.py:351
  25.5 0.7 %collective-permute-start.4 = (bf16[16,2048]{1,0:T(8,128)(2,1)S(1)}, bf16[16,2048]{1,0:T(8,128)(2,1)S(1)}, u32[]{:S(2)}, u32[]{:S(2)}) collective-permute-start(bf16[16,2048]{1,0:T(8,128)(2,1)S(1)} %get-tuple-element.43), channel_id=1, source_target_pairs={{0,1},{1,0},{2,3},{3,2},{4,5},{5,4},{6,7},{7,6},{8,9},{9,8},{10,11... | collective-permute-start | bytes 196616 | tf_op jit(solution)/shard_map/ppermute | solution.py:351
  26.2 0.8 %collective-permute-start.5 = (bf16[16,2048]{1,0:T(8,128)(2,1)S(1)}, bf16[16,2048]{1,0:T(8,128)(2,1)S(1)}, u32[]{:S(2)}, u32[]{:S(2)}) collective-permute-start(bf16[16,2048]{1,0:T(8,128)(2,1)S(1)} %get-tuple-element.44), channel_id=1, source_target_pairs={{0,3},{1,2},{2,1},{3,0},{4,7},{5,6},{6,5},{7,4},{8,11},{9,10},{10,... | collective-permute-start | bytes 196616 | tf_op jit(solution)/shard_map/ppermute | solution.py:351
  27.1 3.5 %fetch.1 = (bf16[2048,1024]{1,0:T(8,128)(2,1)S(1)}, bf16[2048,1024]{1,0:T(8,128)(2,1)S(1)}) custom-call(bf16[16,2048]{1,0:T(8,128)(2,1)S(1)} %get-tuple-element.41.after_ref.refs_0_, bf16[2048,8192]{1,0:T(8,128)(2,1)} %refs_5_.3), custom_call_target="tpu_custom_call" | custom-call | bytes 8388608 | tf_op jit(solution)/shard_map/fetch/pallas_call | solution.py:34
  30.7 6.5 %project.3 = (f32[32,4096]{1,0:T(8,128)S(1)}, bf16[32,4096]{1,0:T(8,128)(2,1)S(1)}, f32[32,64]{1,0:T(8,128)S(1)}, bf16[32,128]{1,0:T(8,128)(2,1)S(1)}, bf16[2048...) custom-call(bf16[16,2048]{1,0:T(8,128)(2,1)S(1)} %get-tuple-element.41.after_ref.refs_0_, ...), custom_call_target="tpu_custom_call" | custom-call | flops 1073741824 | bytes 16777216 | tf_op jit(solution)/shard_map/project/pallas_call | solution.py:34
  37.2 0.5 collective-permute-start.9
  37.8 3.6 %project.4 = (f32[32,2048]{1,0:T(8,128)S(1)}, bf16[32,2048]{1,0:T(8,128)(2,1)S(1)}, bf16[2048,1024]{1,0:T(8,128)(2,1)S(1)}) custom-call(bf16[16,2048]{1,0:T(8,128)(2,1)S(1)} %get-tuple-element.41.after_ref.refs_0_, bf16[16,2048]{1,0:T(8,128)(2,1)S(1)} %collective-permute-done.3.refs_1_, bf16[16,2048]{1,0:T(8,128)(2,1)S(1)} %collective-permute-done.4.refs_2_, ...), custom_call_target="tpu_custom_call" | custom-call | flops 536870912 | bytes 8388608 | tf_op jit(solution)/shard_map/project/pallas_call | solution.py:34
  41.8 1.2 %collective-permute-start.11 = (bf16[16,4352]{1,0:T(8,128)(2,1)S(1)}, bf16[16,4352]{1,0:T(8,128)(2,1)S(1)}, u32[]{:S(2)}, u32[]{:S(2)}) collective-permute-start(bf16[16,4352]{1,0:T(8,128)(2,1)S(1)} %fusion), channel_id=1, source_target_pairs={{0,2},{1,3},{2,0},{3,1},{4,6},{5,7},{6,4},{7,5},{8,10},{9,11},{10,... | collective-permute-start | bytes 417800 | tf_op jit(solution)/shard_map/ppermute | solution.py:351
  43.0 10.5 %copy-done = bf16[2048,8192]{1,0:T(8,128)(2,1)S(1)} copy-done((bf16[2048,8192]{1,0:T(8,128)(2,1)S(1)}, bf16[2048,8192]{1,0:T(8,128)(2,1)}, u32[]{:S(2)}) %copy-start) | copy-done | bytes 33554456
  53.5 2.5 %project.5 = (f32[32,2048]{1,0:T(8,128)S(1)}, bf16[32,2048]{1,0:T(8,128)(2,1)S(1)}) custom-call(bf16[16,2048]{1,0:T(8,128)(2,1)S(1)} %get-tuple-element.41.after_ref.refs_0_, bf16[16,2048]{1,0:T(8,128)(2,1)S(1)} %collective-permute-done.3.refs_1_, bf16[16,2048]{1,0:T(8,128)(2,1)S(1)} %collective-permute-done.4.refs_2_, ...), custom_call_target="tpu_custom_call" | custom-call | flops 536870912 | bytes 8388608 | tf_op jit(solution)/shard_map/project/pallas_call | solution.py:34
  56.1 0.5 collective-permute-start.12
  56.6 0.8 %collective-permute-done.13.refs_5_ = bf16[32,2048]{1,0:T(8,128)(2,1)S(1)} collective-permute-done((bf16[32,2048]{1,0:T(8,128)(2,1)S(1)}, bf16[32,2048]{1,0:T(8,128)(2,1)S(1)}, u32[]{:S(2)}, u32[]{:S(2)}) %collective-permute-start.13) | collective-permute-done | bytes 131104 | tf_op jit(solution)/shard_map/ppermute | solution.py:351
  57.5 0.2 collective-permute-done.12.refs_4_
  57.7 0.4 adapt.1
  58.1 0.9 %collective-permute-start.15 = (bf16[16,4096]{1,0:T(8,128)(2,1)S(1)}, bf16[16,4096]{1,0:T(8,128)(2,1)S(1)}, u32[]{:S(2)}, u32[]{:S(2)}) collective-permute-start(bf16[16,4096]{1,0:T(8,128)(2,1)S(1)} %get-tuple-element.63), channel_id=1, source_target_pairs={{0,2},{1,3},{2,0},{3,1},{4,6},{5,7},{6,4},{7,5},{8,10},{9,11},{10,... | collective-permute-start | bytes 393224 | tf_op jit(solution)/shard_map/ppermute | solution.py:351
  59.0 4.9 %collective-permute-done.15.far_got_ref = bf16[16,4096]{1,0:T(8,128)(2,1)S(1)} collective-permute-done((bf16[16,4096]{1,0:T(8,128)(2,1)S(1)}, bf16[16,4096]{1,0:T(8,128)(2,1)S(1)}, u32[]{:S(2)}, u32[]{:S(2)}) %collective-permute-start.15) | collective-permute-done | bytes 131104 | tf_op jit(solution)/shard_map/ppermute | solution.py:351
  63.9 0.8 %finish.1 = bf16[8,2,8192]{2,1,0:T(2,128)(2,1)} custom-call(f32[16,4096]{1,0:T(8,128)S(1)} %slice.33.far_ref, bf16[16,4096]{1,0:T(8,128)(2,1)S(1)} %collective-permute-done.15.far_got_ref, f32[16,4096]{1,0:T(8,128)S(1)} %get-tuple-element.64.near_ref, bf16[16,4096]{1,0:T(8,128)(2,1)S(1)} %slice.40.near_got_ref), custom_call_target="tpu_custom_call" | custom-call | tf_op jit(solution)/shard_map/finish/pallas_call | solution.py:34
  (31 shorter events, 0.7 us)
Async XLA Ops:
  0.0 0.9 %copy-start.2 = (bf16[8,8,2048]{2,1,0:T(8,128)(2,1)S(1)}, bf16[8,8,2048]{2,1,0:T(8,128)(2,1)}, u32[]{:S(2)}) copy-start(bf16[8,8,2048]{2,1,0:T(8,128)(2,1)} %query_hbm.1) | copy-start | bytes 786436
  1.0 0.8 %copy-start.3 = (bf16[8,8,512]{2,1,0:T(8,128)(2,1)S(1)}, bf16[8,8,512]{2,1,0:T(8,128)(2,1)}, u32[]{:S(2)}) copy-start(bf16[8,8,512]{2,1,0:T(8,128)(2,1)} %new_hbm.1) | copy-start | bytes 196612
  1.8 0.8 %copy-start.4 = (bf16[2048,16]{0,1:T(8,128)(2,1)S(1)}, bf16[2048,16]{0,1:T(8,128)(2,1)}, u32[]{:S(2)}) copy-start(bf16[2048,16]{0,1:T(8,128)(2,1)} %param.12) | copy-start | bytes 196612
  2.6 0.8 %copy-start.5 = (bf16[64,512]{1,0:T(8,128)(2,1)S(1)}, bf16[64,512]{1,0:T(8,128)(2,1)}, u32[]{:S(2)}) copy-start(bf16[64,512]{1,0:T(8,128)(2,1)} %up_hbm.1) | copy-start | bytes 196612
  4.0 1.4 %collective-permute-start = (bf16[320,128]{1,0:T(8,128)(2,1)S(1)}, bf16[320,128]{1,0:T(8,128)(2,1)S(1)}, u32[]{:S(2)}, u32[]{:S(2)}) collective-permute-start(bf16[320,128]{1,0:T(8,128)(2,1)S(1)} %get-tuple-element.37), channel_id=1, source_target_pairs={{0,1},{1,0},{2,3},{3,2},{4,5},{5,4},{6,7},{7,6},{8,9},{9,8},{10,11... | collective-permute-start | bytes 245768 | tf_op jit(solution)/shard_map/ppermute | solution.py:351
  5.5 20.8 %collective-permute-start.6 = (bf16[32,2048]{1,0:T(8,128)(2,1)S(1)}, bf16[32,2048]{1,0:T(8,128)(2,1)S(1)}, u32[]{:S(2)}, u32[]{:S(2)}) collective-permute-start(bf16[32,2048]{1,0:T(8,128)(2,1)S(1)} %get-tuple-element.49.refs_0_), channel_id=1, source_target_pairs={{0,4},{4,0},{8,12},{12,8},{1,5},{5,1},{9,13},{13,9},{2,6},{6,2},{1... | collective-permute-start | bytes 393224 | tf_op jit(solution)/shard_map/ppermute | solution.py:351
  8.4 4.4 %collective-permute-start.1 = (bf16[320,128]{1,0:T(8,128)(2,1)S(1)}, bf16[320,128]{1,0:T(8,128)(2,1)S(1)}, u32[]{:S(2)}, u32[]{:S(2)}) collective-permute-start(bf16[320,128]{1,0:T(8,128)(2,1)S(1)} %get-tuple-element.39), channel_id=1, source_target_pairs={{0,2},{1,3},{2,0},{3,1},{4,6},{5,7},{6,4},{7,5},{8,10},{9,11},{10,... | collective-permute-start | bytes 245768 | tf_op jit(solution)/shard_map/ppermute | solution.py:351
  9.9 4.7 %collective-permute-start.2 = (bf16[320,128]{1,0:T(8,128)(2,1)S(1)}, bf16[320,128]{1,0:T(8,128)(2,1)S(1)}, u32[]{:S(2)}, u32[]{:S(2)}) collective-permute-start(bf16[320,128]{1,0:T(8,128)(2,1)S(1)} %get-tuple-element.40), channel_id=1, source_target_pairs={{0,3},{1,2},{2,1},{3,0},{4,7},{5,6},{6,5},{7,4},{8,11},{9,10},{10,... | collective-permute-start | bytes 245768 | tf_op jit(solution)/shard_map/ppermute | solution.py:351
  9.9 20.7 %collective-permute-start.7 = (bf16[32,2048]{1,0:T(8,128)(2,1)S(1)}, bf16[32,2048]{1,0:T(8,128)(2,1)S(1)}, u32[]{:S(2)}, u32[]{:S(2)}) collective-permute-start(bf16[32,2048]{1,0:T(8,128)(2,1)S(1)} %get-tuple-element.49.refs_0_), channel_id=1, source_target_pairs={{0,8},{4,12},{8,0},{12,4},{1,9},{5,13},{9,1},{13,5},{2,10},{6,14},... | collective-permute-start | bytes 393224 | tf_op jit(solution)/shard_map/ppermute | solution.py:351
  12.5 18.1 %collective-permute-start.8 = (bf16[32,2048]{1,0:T(8,128)(2,1)S(1)}, bf16[32,2048]{1,0:T(8,128)(2,1)S(1)}, u32[]{:S(2)}, u32[]{:S(2)}) collective-permute-start(bf16[32,2048]{1,0:T(8,128)(2,1)S(1)} %get-tuple-element.49.refs_0_), channel_id=1, source_target_pairs={{0,12},{4,8},{8,4},{12,0},{1,13},{5,9},{9,5},{13,1},{2,14},{6,10},... | collective-permute-start | bytes 393224 | tf_op jit(solution)/shard_map/ppermute | solution.py:351
  14.6 2.2 %copy-start.1 = (bf16[2,2,8,512,128]{4,3,2,1,0:T(8,128)(2,1)S(1)}, bf16[2,2,8,512,128]{4,3,2,1,0:T(8,128)(2,1)}, u32[]{:S(2)}) copy-start(bf16[2,2,8,512,128]{4,3,2,1,0:T(8,128)(2,1)} %refs_4_.1) | copy-start | bytes 12582916
  16.8 0.7 %copy-start.6 = (s32[2]{0:T(128)S(1)}, s32[2]{0:T(128)}, u32[]{:S(2)}) copy-start(s32[2]{0:T(128)} %length_hbm.1) | copy-start | bytes 28
  24.9 5.8 %collective-permute-start.3 = (bf16[16,2048]{1,0:T(8,128)(2,1)S(1)}, bf16[16,2048]{1,0:T(8,128)(2,1)S(1)}, u32[]{:S(2)}, u32[]{:S(2)}) collective-permute-start(bf16[16,2048]{1,0:T(8,128)(2,1)S(1)} %get-tuple-element.42), channel_id=1, source_target_pairs={{0,2},{1,3},{2,0},{3,1},{4,6},{5,7},{6,4},{7,5},{8,10},{9,11},{10,... | collective-permute-start | bytes 196616 | tf_op jit(solution)/shard_map/ppermute | solution.py:351
  25.5 5.1 %collective-permute-start.4 = (bf16[16,2048]{1,0:T(8,128)(2,1)S(1)}, bf16[16,2048]{1,0:T(8,128)(2,1)S(1)}, u32[]{:S(2)}, u32[]{:S(2)}) collective-permute-start(bf16[16,2048]{1,0:T(8,128)(2,1)S(1)} %get-tuple-element.43), channel_id=1, source_target_pairs={{0,1},{1,0},{2,3},{3,2},{4,5},{5,4},{6,7},{7,6},{8,9},{9,8},{10,11... | collective-permute-start | bytes 196616 | tf_op jit(solution)/shard_map/ppermute | solution.py:351
  26.2 4.4 %collective-permute-start.5 = (bf16[16,2048]{1,0:T(8,128)(2,1)S(1)}, bf16[16,2048]{1,0:T(8,128)(2,1)S(1)}, u32[]{:S(2)}, u32[]{:S(2)}) collective-permute-start(bf16[16,2048]{1,0:T(8,128)(2,1)S(1)} %get-tuple-element.44), channel_id=1, source_target_pairs={{0,3},{1,2},{2,1},{3,0},{4,7},{5,6},{6,5},{7,4},{8,11},{9,10},{10,... | collective-permute-start | bytes 196616 | tf_op jit(solution)/shard_map/ppermute | solution.py:351
  37.1 4.3 %collective-permute-start.10 = (bf16[32,128]{1,0:T(8,128)(2,1)S(1)}, bf16[32,128]{1,0:T(8,128)(2,1)S(1)}, u32[]{:S(2)}, u32[]{:S(2)}) collective-permute-start(bf16[32,128]{1,0:T(8,128)(2,1)S(1)} %get-tuple-element.54), channel_id=1, source_target_pairs={{0,1},{1,0},{2,3},{3,2},{4,5},{5,4},{6,7},{7,6},{8,9},{9,8},{10,11... | collective-permute-start | bytes 24584 | tf_op jit(solution)/shard_map/ppermute | solution.py:351
  37.2 4.4 %collective-permute-start.9 = (bf16[32,4096]{1,0:T(8,128)(2,1)S(1)}, bf16[32,4096]{1,0:T(8,128)(2,1)S(1)}, u32[]{:S(2)}, u32[]{:S(2)}) collective-permute-start(bf16[32,4096]{1,0:T(8,128)(2,1)S(1)} %get-tuple-element.52), channel_id=1, source_target_pairs={{0,1},{1,0},{2,3},{3,2},{4,5},{5,4},{6,7},{7,6},{8,9},{9,8},{10,11... | collective-permute-start | bytes 786440 | tf_op jit(solution)/shard_map/ppermute | solution.py:351
  37.7 19.9 %collective-permute-start.14 = (bf16[4,64,512]{2,1,0:T(8,128)(2,1)S(1)}, bf16[4,64,512]{2,1,0:T(8,128)(2,1)S(1)}, u32[]{:S(2)}, u32[]{:S(2)}) collective-permute-start(bf16[4,64,512]{2,1,0:T(8,128)(2,1)S(1)} %get-tuple-element.62.refs_6_), channel_id=1, source_target_pairs={{0,1},{1,0},{2,3},{3,2},{4,5},{5,4},{6,7},{7,6},{8,9},{9,8},{10,11... | collective-permute-start | bytes 786440 | tf_op jit(solution)/shard_map/ppermute | solution.py:351
  41.8 14.9 %collective-permute-start.11 = (bf16[16,4352]{1,0:T(8,128)(2,1)S(1)}, bf16[16,4352]{1,0:T(8,128)(2,1)S(1)}, u32[]{:S(2)}, u32[]{:S(2)}) collective-permute-start(bf16[16,4352]{1,0:T(8,128)(2,1)S(1)} %fusion), channel_id=1, source_target_pairs={{0,2},{1,3},{2,0},{3,1},{4,6},{5,7},{6,4},{7,5},{8,10},{9,11},{10,... | collective-permute-start | bytes 417800 | tf_op jit(solution)/shard_map/ppermute | solution.py:351
  43.0 10.5 %copy-start = (bf16[2048,8192]{1,0:T(8,128)(2,1)S(1)}, bf16[2048,8192]{1,0:T(8,128)(2,1)}, u32[]{:S(2)}) copy-start(bf16[2048,8192]{1,0:T(8,128)(2,1)} %refs_5_.3) | copy-start | bytes 100663296
  56.1 1.4 %collective-permute-start.13 = (bf16[32,2048]{1,0:T(8,128)(2,1)S(1)}, bf16[32,2048]{1,0:T(8,128)(2,1)S(1)}, u32[]{:S(2)}, u32[]{:S(2)}) collective-permute-start(bf16[32,2048]{1,0:T(8,128)(2,1)S(1)} %get-tuple-element.61), channel_id=1, source_target_pairs={{0,1},{1,0},{2,3},{3,2},{4,5},{5,4},{6,7},{7,6},{8,9},{9,8},{10,11... | collective-permute-start | bytes 393224 | tf_op jit(solution)/shard_map/ppermute | solution.py:351
  56.1 1.5 %collective-permute-start.12 = (bf16[32,2048]{1,0:T(8,128)(2,1)S(1)}, bf16[32,2048]{1,0:T(8,128)(2,1)S(1)}, u32[]{:S(2)}, u32[]{:S(2)}) collective-permute-start(bf16[32,2048]{1,0:T(8,128)(2,1)S(1)} %get-tuple-element.60), channel_id=1, source_target_pairs={{0,1},{1,0},{2,3},{3,2},{4,5},{5,4},{6,7},{7,6},{8,9},{9,8},{10,11... | collective-permute-start | bytes 393224 | tf_op jit(solution)/shard_map/ppermute | solution.py:351
  58.1 5.8 %collective-permute-start.15 = (bf16[16,4096]{1,0:T(8,128)(2,1)S(1)}, bf16[16,4096]{1,0:T(8,128)(2,1)S(1)}, u32[]{:S(2)}, u32[]{:S(2)}) collective-permute-start(bf16[16,4096]{1,0:T(8,128)(2,1)S(1)} %get-tuple-element.63), channel_id=1, source_target_pairs={{0,2},{1,3},{2,0},{3,1},{4,6},{5,7},{6,4},{7,5},{8,10},{9,11},{10,... | collective-permute-start | bytes 393224 | tf_op jit(solution)/shard_map/ppermute | solution.py:351

commit v3 on v2

v3 whole, which is shorter than its diff:
```python
import functools

import jax
import jax.numpy as jnp
from jax import lax
from jax.experimental import pallas as pl
from jax.experimental.pallas import tpu as pltpu
from jax.sharding import PartitionSpec as P

HEADS = 64
KV_HEADS = 8
HEAD_DIM = 128
GROUP = HEADS // KV_HEADS
RANK = 64
LOG2_E = 1.4426950408889634
SCALE = 2.0
BF16 = jnp.bfloat16
F32 = jnp.float32
VMEM = pl.BlockSpec(memory_space=pltpu.VMEM)
ANY = pl.BlockSpec(memory_space=pl.ANY)
HBM = pl.BlockSpec(memory_space=pltpu.HBM)
ROW_ROW = (((1,), (1,)), ((), ()))
shape_of = jax.ShapeDtypeStruct


def dot(a, b):
    return jnp.dot(a, b, preferred_element_type=F32)


def dot_rows(a, b):
    return lax.dot_general(a, b, ROW_ROW, preferred_element_type=F32)


def call(kernel, name, ins, outs, scratch=(), mib=6, cost=None, alias=None):
    specs, args = zip(*ins)
    args = [
        pltpu.with_memory_space_constraint(a, pltpu.HBM) if s is HBM else a for s, a in ins
    ]
    return pl.pallas_call(
        kernel,
        in_specs=list(specs),
        out_specs=[VMEM] * len(outs),
        out_shape=list(outs),
        scratch_shapes=list(scratch),
        input_output_aliases=alias or {},
        compiler_params=pltpu.CompilerParams(vmem_limit_bytes=mib * 2**20),
        cost_estimate=cost,
        name=name,
    )(*args)


def split(x):
    high = x.astype(BF16)
    return high, (x - high.astype(F32)).astype(BF16)


def log2(n):
    return n.bit_length() - 1


def strip_copies(weight_hbm, strips_ref, sem, first):
    count, _, wide = strips_ref.shape
    spread = weight_hbm.shape[1] // (2 * wide)
    top = lax.axis_index("tensor") >> (log2(lax.axis_size("tensor")) - 1)
    copies = []
    for i in range(count):
        half = top if first + i >= spread else 1 - top
        start = pl.multiple_of((2 * ((first + i) % spread) + half) * wide, wide)
        copies.append(
            pltpu.make_async_copy(
                weight_hbm.at[:, pl.ds(start, wide)], strips_ref.at[i], sem.at[i]
            )
        )
    return copies


def pack_kernel(query_hbm, new_hbm, *refs, parts, own, steps):
    *block_refs, query_ref, new_ref, sem = refs
    copies = [
        pltpu.make_async_copy(query_hbm, query_ref, sem.at[0]),
        pltpu.make_async_copy(new_hbm, new_ref, sem.at[1]),
    ]
    for copy in copies:
        copy.start()
    me = lax.axis_index("tensor")
    count = steps * parts * own
    i = lax.broadcasted_iota(jnp.int32, (count, count), 0)
    j = lax.broadcasted_iota(jnp.int32, (count, count), 1)
    step_out = i & (steps - 1)
    row_out = (i >> log2(steps)) & (own - 1)
    part_out = (i >> log2(steps * own)) ^ me
    source = step_out * (parts * own) + part_out * own + row_out
    select = jnp.where(source == j, 1.0, 0.0).astype(BF16)
    for copy in copies:
        copy.wait()
    queries = dot(select, query_ref[...].reshape(count, query_ref.shape[2]))
    new = dot(select, new_ref[...].reshape(count, new_ref.shape[2]))
    heads = queries.shape[1] // HEAD_DIM
    pieces = new.shape[1] // HEAD_DIM
    tall = own * steps
    for k in range(parts):
        q = queries[k * tall : (k + 1) * tall]
        n = new[k * tall : (k + 1) * tall]
        tiles = [
            q[r * steps : (r + 1) * steps, h * HEAD_DIM : (h + 1) * HEAD_DIM]
            for r in range(own)
            for h in range(heads)
        ]
        tiles += [n[:, c * HEAD_DIM : (c + 1) * HEAD_DIM] for c in range(pieces)]
        block = jnp.concatenate(tiles, axis=0).astype(BF16)
        if k < parts // 2:
            block_refs[k][...] = block
        else:
            block_refs[-1][k - parts // 2] = block


def stage_kernel(after_ref, cache_hbm, down_hbm, up_hbm, cache_ref, factor_ref, up_ref, sem):
    slot, depth = down_hbm.shape
    copies = [
        pltpu.make_async_copy(up_hbm, up_ref, sem.at[0]),
        pltpu.make_async_copy(down_hbm, factor_ref.at[pl.ds(0, slot)], sem.at[1]),
    ]
    slots = pl.ds(0, cache_hbm.shape[3])
    for r in range(cache_hbm.shape[0]):
        for part in range(2):
            copies.append(
                pltpu.make_async_copy(
                    cache_hbm.at[r, part],
                    cache_ref.at[r, part, :, slots],
                    sem.at[2 + 2 * r + part],
                )
            )
    for copy in copies:
        copy.start()
    cut = up_ref.shape[1]
    per = depth // cut
    tall = RANK // per
    copies[0].wait()
    for c in range(per):
        factor_ref[slot : slot + tall, c * cut : (c + 1) * cut] = up_ref[c * tall : (c + 1) * tall, :]
    for copy in copies[1:]:
        copy.wait()


def attend_kernel(length_hbm, *refs, parts, own, steps):
    block_refs, refs = refs[:parts], refs[parts:]
    weight_hbm, refs = refs[0], refs[2:]
    out_refs, refs = refs[:parts], refs[parts:]
    strips_ref, cache_ref, length_ref, held_ref, attended_ref = refs[:5]
    scores_ref, weights_ref, length_sem, sem = refs[5:]
    length_copy = pltpu.make_async_copy(length_hbm, length_ref, length_sem)
    length_copy.start()
    heads = HEADS // parts
    pieces = 2 * KV_HEADS // parts
    query_rows = own * heads * steps
    tall = own * steps
    slots = cache_ref.shape[3] - tall
    count = GROUP * steps
    turns = own * KV_HEADS
    weight_copies = strip_copies(weight_hbm, strips_ref, sem, 0)
    for copy in weight_copies:
        copy.start()

    me = lax.axis_index("tensor")
    for k, block_ref in enumerate(block_refs):
        held_ref[me ^ k] = block_ref[0:query_rows, :]
        for c in range(pieces):
            piece = (me ^ k) * pieces + c
            start = query_rows + c * tall
            for r in range(own):
                cache_ref[r, piece >> log2(KV_HEADS), piece & (KV_HEADS - 1), slots : slots + tall, :] = (
                    block_ref[start : start + tall, :]
                )

    def queries(r, g):
        if heads >= GROUP:
            groups = heads // GROUP
            start = (r * heads + (g & (groups - 1)) * GROUP) * steps
            return held_ref[g >> log2(groups), pl.ds(pl.multiple_of(start, count), count), :]
        span = GROUP // heads
        start = pl.multiple_of(r * heads * steps, heads * steps)
        found = [held_ref[g * span + i, pl.ds(start, heads * steps), :] for i in range(span)]
        return jnp.concatenate(found, axis=0)

    slot = lax.broadcasted_iota(jnp.int32, (count, slots + tall), 1)
    step = lax.broadcasted_iota(jnp.int32, (count, slots + tall), 0) & (steps - 1)
    ones = jnp.ones((slots + tall, HEAD_DIM), BF16)
    length_copy.wait()

    def turn(j, _):
        scored = jnp.minimum(j, turns - 1)
        r, g = scored >> log2(KV_HEADS), scored & (KV_HEADS - 1)
        summed = jnp.maximum(j - 2, 0)
        r_out, g_out = summed >> log2(KV_HEADS), summed & (KV_HEADS - 1)

        fresh = slot - slots - r * steps
        valid = (slot < length_ref[r]) | ((fresh >= 0) & (fresh <= step))
        scores = dot_rows(queries(r, g), cache_ref[r, 0, g]) * (HEAD_DIM**-0.5 * LOG2_E)
        before = scores_ref[(j + 1) & 1]
        weights = jnp.exp2(before - before.max(-1, keepdims=True))
        values = jnp.concatenate([cache_ref[r_out, 1, g_out], ones], axis=1)
        mixed = dot(weights_ref[j & 1], values)
        mixed = mixed[:count] + mixed[count:]
        mixed = mixed[:, :HEAD_DIM] / mixed[:, HEAD_DIM:]

        high, rest = split(weights)
        weights_ref[(j + 1) & 1, 0:count, :] = high
        weights_ref[(j + 1) & 1, count : 2 * count, :] = rest
        scores_ref[j & 1] = jnp.where(valid, scores, -1e30)
        row = pl.ds(pl.multiple_of(r_out * steps, steps), steps)
        for h in range(GROUP):
            head = g_out * GROUP + h
            attended_ref[head >> log2(heads), head & (heads - 1), row, :] = mixed[
                h * steps : (h + 1) * steps
            ]
        return 0

    lax.fori_loop(0, turns + 2, turn, 0, unroll=2)
    for k in range(parts):
        for h in range(heads):
            out_refs[k][:, h * HEAD_DIM : (h + 1) * HEAD_DIM] = attended_ref[me ^ k, h].astype(BF16)
    for copy in weight_copies:
        copy.wait()


def collect_kernel(*refs, slot):
    _, *factor_refs, down_ref, up_ref = refs
    me = lax.axis_index("fsdp")
    cut = up_ref.shape[2]
    per = down_ref.shape[1] // cut
    tall = RANK // per
    for k, factor_ref in enumerate(factor_refs):
        down_ref[pl.ds(pl.multiple_of((me ^ k) * slot, slot), slot), :] = factor_ref[0:slot, :]
        for c in range(per):
            up_ref[k, c * tall : (c + 1) * tall, :] = factor_ref[
                slot : slot + tall, c * cut : (c + 1) * cut
            ]


def fetch_kernel(after_ref, weight_hbm, strips_ref, sem, *, first):
    copies = strip_copies(weight_hbm, strips_ref, sem, first)
    for copy in copies:
        copy.start()
    for copy in copies:
        copy.wait()


def project_kernel(*refs, parts, spans, ahead, first):
    attended_refs, refs = refs[:parts], refs[parts:]
    held_refs, refs = refs[: len(spans)], refs[len(spans) :]
    weight_hbm, keep_ref, send_ref, refs = refs[0], refs[1], refs[2], refs[3:]
    copies = []
    if ahead:
        ahead_ref, rows_ref, sem = refs
        copies = strip_copies(weight_hbm, ahead_ref, sem, first)
    else:
        rows_ref = refs[0]
    for copy in copies:
        copy.start()
    tall = attended_refs[0].shape[0]
    for k, attended_ref in enumerate(attended_refs):
        rows_ref[k * tall : (k + 1) * tall, :] = attended_ref[...]
    half = rows_ref.shape[0] // 2
    place = 0
    for strips_ref, (low, high) in zip(held_refs, spans):
        wide = strips_ref.shape[2]

        @pl.loop(low, high)
        def _(i, strips_ref=strips_ref, place=place - low):
            out = dot(rows_ref[...], strips_ref[i])
            lanes = pl.ds(pl.multiple_of((place + i) * wide, wide), wide)
            keep_ref[:, lanes] = out[:half]
            send_ref[:, lanes] = out[half:].astype(BF16)

        place += high - low
    for copy in copies:
        copy.wait()


def project(attended, weight, buffers, low, high, ahead=0):
    parts = len(attended)
    tall, depth = attended[0].shape
    half = parts * tall // 2
    held, spans = [], []
    for first, buffer in buffers:
        a, b = max(low - first, 0), min(high - first, buffer.shape[0])
        if a < b:
            held.append(buffer)
            spans.append((a, b))
    wide = held[0].shape[2]
    width = wide * (high - low)
    next_strip = buffers[-1][0] + buffers[-1][1].shape[0]
    outs = [shape_of((half, width), F32), shape_of((half, width), BF16)]
    ins = [(VMEM, a) for a in attended] + [(VMEM, h) for h in held] + [(HBM, weight)]
    scratch = [pltpu.VMEM((parts * tall, depth), BF16)]
    if ahead:
        outs += [pltpu.VMEM((ahead, depth, wide), BF16)]
        scratch += [pltpu.SemaphoreType.DMA((ahead,))]
    kernel = functools.partial(
        project_kernel, parts=parts, spans=spans, ahead=ahead, first=next_strip
    )
    cost = pl.CostEstimate(
        flops=2 * parts * tall * depth * width, bytes_accessed=2 * depth * width, transcendentals=0
    )
    keep, send, *rest = call(kernel, "project", ins, outs, scratch, cost=cost)
    return keep, send, buffers + [(next_strip, rest[0])] if ahead else buffers


def lower_kernel(*refs):
    *attended_refs, down_ref, keep_ref, send_ref = refs
    half = len(attended_refs) // 2
    for first, last in ((0, half), (half, 2 * half)):
        rows = jnp.concatenate([a[...] for a in attended_refs[first:last]], axis=0)
        low = dot_rows(rows, down_ref[...])
        if first:
            send_ref[...] = jnp.concatenate(split(low), axis=1)
        else:
            keep_ref[...] = low


def fold_low(keep, got):
    return keep + got[:, :RANK].astype(F32) + got[:, RANK:].astype(F32)


def adapt_kernel(*refs, pieces, sets, ordered):
    low_ref, low_got_ref, refs = refs[0], refs[1], refs[2:]
    keep_refs, refs = refs[:pieces], refs[pieces:]
    got_refs, refs = refs[:pieces], refs[pieces:]
    up_refs, (own_ref, send_ref, extra_ref) = refs[:sets], refs[sets:]
    me, place = lax.axis_index("tensor"), lax.axis_index("fsdp")
    half = low_ref.shape[0] // 2
    got = low_got_ref[...]
    got = jnp.concatenate([got[:, : 2 * RANK], got[:, 2 * RANK :]], axis=0)
    low = SCALE * fold_low(low_ref[...], got)
    low = jnp.concatenate(split(low), axis=0)
    if ordered:
        both = dot(low, up_refs[0][...])
        extra_ref[...] = both[: 2 * half] + both[2 * half :]
    else:
        cut = up_refs[0].shape[2]
        for kt, up_ref in enumerate(up_refs):
            for kf in range(up_ref.shape[0]):
                both = dot(low, up_ref[kf])
                column = (place ^ kf) * sets + ((me ^ kt) & (sets - 1))
                start = pl.multiple_of(column * cut, cut)
                extra_ref[:, pl.ds(start, cut)] = both[: 2 * half] + both[2 * half :]
    first = 0
    for keep_ref, got_ref in zip(keep_refs, got_refs):
        lanes = slice(first, first + keep_ref.shape[1])
        first += keep_ref.shape[1]
        total = keep_ref[...] + got_ref[...].astype(F32) + extra_ref[:, lanes]
        own_ref[:, lanes] = total[:half]
        send_ref[:, lanes] = total[half:].astype(BF16)


def finish_kernel(far_ref, far_got_ref, near_ref, near_got_ref, out_ref, *, own, steps, strips):
    top = lax.axis_index("tensor") >> (log2(lax.axis_size("tensor")) - 1)
    wide = near_ref.shape[1] // strips
    for keep_ref, got_ref, half in ((near_ref, near_got_ref, top), (far_ref, far_got_ref, 1 - top)):
        for i in range(strips):
            lanes = slice(i * wide, (i + 1) * wide)
            total = (keep_ref[:, lanes] + got_ref[:, lanes].astype(F32)).astype(BF16)
            start = pl.multiple_of((2 * i + half) * wide, wide)
            for r in range(own):
                out_ref[:, r, pl.ds(start, wide)] = total[r * steps : (r + 1) * steps]


def shards(queries, cache, new, lengths, weight, down, up):
    parts, spread = lax.axis_size("tensor"), lax.axis_size("fsdp")
    steps, rows, width = queries.shape
    own = rows // parts
    tall = own * steps
    depth, slot = down.shape
    cut = up.shape[1]
    heads, pieces = width // HEAD_DIM, new.shape[2] // HEAD_DIM
    sets = parts // 2
    wide = sets * cut
    half_width = spread * wide
    swap = lambda x, axis, k: lax.ppermute(
        x, axis, [(i, i ^ k) for i in range(lax.axis_size(axis))]
    )

    block = shape_of((own * heads * steps + pieces * tall, HEAD_DIM), BF16)
    per = depth // cut
    *blocks, cross = call(
        functools.partial(pack_kernel, parts=parts, own=own, steps=steps),
        "pack",
        [(HBM, queries), (HBM, new)],
        [block] * sets + [shape_of((sets,) + block.shape, BF16)],
        [pltpu.VMEM(queries.shape, BF16), pltpu.VMEM(new.shape, BF16), pltpu.SemaphoreType.DMA((2,))],
    )
    cache, factors = call(
        stage_kernel,
        "stage",
        [(ANY, blocks[0]), (HBM, cache), (HBM, down.T), (HBM, up)],
        [
            pltpu.VMEM(cache.shape[:3] + (cache.shape[3] + tall, HEAD_DIM), BF16),
            shape_of((slot + RANK // per, depth), BF16),
        ],
        [pltpu.VMEM(up.shape, BF16), pltpu.SemaphoreType.DMA((2 + 2 * own,))],
        cost=pl.CostEstimate(flops=0, bytes_accessed=2 * cache.size, transcendentals=0),
    )
    cross = swap(cross, "tensor", sets)
    blocks = blocks[:1] + [swap(blocks[k], "tensor", k) for k in range(1, sets)]
    blocks += [cross[0]] + [swap(cross[k], "tensor", k) for k in range(1, sets)]
    factors = {0: factors}
    bit = spread // 2
    while bit > 1:
        factors |= {k ^ bit: swap(v, "fsdp", bit) for k, v in list(factors.items())}
        bit //= 2
    near_factors, blocks[sets] = lax.optimization_barrier((factors[0], blocks[sets]))

    half, quarter = spread // 2, spread // 4
    early = half + quarter
    fetched = quarter
    attended = call(
        functools.partial(attend_kernel, parts=parts, own=own, steps=steps),
        "attend",
        [(HBM, lengths)] + [(VMEM, b) for b in blocks] + [(HBM, weight), (VMEM, cache)],
        [shape_of((tall, width), BF16)] * parts
        + [pltpu.VMEM((early, depth, wide), BF16), pltpu.VMEM(cache.shape, BF16)],
        [
            pltpu.SMEM(lengths.shape, jnp.int32),
            pltpu.VMEM((parts, own * heads * steps, HEAD_DIM), BF16),
            pltpu.VMEM((parts, heads, tall, HEAD_DIM), F32),
            pltpu.VMEM((2, GROUP * steps, cache.shape[3]), F32),
            pltpu.VMEM((2, 2 * GROUP * steps, cache.shape[3]), BF16),
            pltpu.SemaphoreType.DMA(()),
            pltpu.SemaphoreType.DMA((early,)),
        ],
        alias={parts + 2: parts + 1},
    )
    attended, buffers = attended[:parts], [(0, attended[parts])]
    buffers += [
        (
            early,
            call(
                functools.partial(fetch_kernel, first=early),
                "fetch",
                [(ANY, attended[0]), (HBM, weight)],
                [pltpu.VMEM((fetched, depth, wide), BF16)],
                [pltpu.SemaphoreType.DMA((fetched,))],
                cost=pl.CostEstimate(
                    flops=0, bytes_accessed=2 * fetched * depth * wide, transcendentals=0
                ),
            )[0],
        )
    ]
    factors[1] = swap(near_factors, "fsdp", 1)
    attended, factors = lax.optimization_barrier((list(attended), factors))
    factors |= {k ^ 1: swap(v, "fsdp", 1) for k, v in list(factors.items()) if k > 1}
    got = {k: swap(attended[k], "tensor", k) for k in range(parts - 1, 0, -1)}
    attended = [attended[0]] + [got[k] for k in range(1, parts)]

    order = sorted(range(parts), key=lambda k: format(k, "08b")[::-1])
    attended = [attended[k] for k in order]

    def reduce(keep, send):
        bit = 1
        while True:
            got = swap(send, "tensor", bit)
            bit *= 2
            if bit == sets:
                return keep, got
            both = keep + got.astype(F32)
            half = both.shape[0] // 2
            keep, send = both[:half], both[half:].astype(BF16)

    def reduce_low(keep, send):
        bit = 1
        while True:
            both = fold_low(keep, swap(send, "tensor", bit))
            bit *= 2
            if bit == sets:
                return both
            half = both.shape[0] // 2
            keep, send = both[:half], jnp.concatenate(split(both[half:]), axis=1)

    keep, send, buffers = project(attended, weight, buffers, 0, spread, half)
    far_keep, far_got = reduce(keep, send)

    down_rows, ups = call(
        functools.partial(collect_kernel, slot=slot),
        "collect",
        [(ANY, keep)] + [(VMEM, factors[k]) for k in range(spread)],
        [shape_of((RANK, depth), BF16), shape_of((spread, RANK, cut), BF16)],
    )
    low_keep, low_send = call(
        lower_kernel,
        "lower",
        [(VMEM, a) for a in (*attended, down_rows)],
        [shape_of((sets * tall, RANK), F32), shape_of((sets * tall, 2 * RANK), BF16)],
    )
    low = reduce_low(low_keep, low_send)
    ordered = cut % HEAD_DIM != 0
    if ordered:
        ups = lax.all_gather(up, ("fsdp", "tensor"), axis=1, tiled=True)
        ups = ups.reshape(RANK, spread, 2, wide)
        top = lax.axis_index("tensor") // sets
        ups = lax.dynamic_index_in_dim(ups, top, 2, keepdims=False)
        up_sets = {0: ups.reshape(RANK, half_width)}
    else:
        up_sets = {0: ups}
        bit = sets // 2
        while bit:
            up_sets |= {k ^ bit: swap(u, "tensor", bit) for k, u in list(up_sets.items())}
            bit //= 2

    middle = spread + half
    keep_a, send_a, buffers = project(attended, weight, buffers, spread, middle, half)
    keep_a, got_a = reduce(keep_a, send_a)
    keep_b, send_b, _ = project(attended, weight, buffers, middle, 2 * spread)
    keep_b, got_b = reduce(keep_b, send_b)

    far = far_keep + far_got.astype(F32)
    low_parts = jnp.concatenate(split(low), axis=1)
    message = jnp.concatenate([far[tall:].astype(BF16), low_parts[tall:], low_parts[:tall]], axis=1)
    message = swap(message, "tensor", sets)
    near_got, low_got = message[:, :half_width], message[:, half_width:]

    ups = [up_sets[k] for k in range(len(up_sets))]
    near_keep, near_send = call(
        functools.partial(adapt_kernel, pieces=2, sets=len(ups), ordered=ordered),
        "adapt",
        [(VMEM, a) for a in (low, low_got, keep_a, keep_b, got_a, got_b, *ups)],
        [shape_of((tall, half_width), F32), shape_of((tall, half_width), BF16)],
        [pltpu.VMEM((2 * tall, half_width), F32)],
    )
    far_got = swap(near_send, "tensor", sets)

    return call(
        functools.partial(finish_kernel, own=own, steps=steps, strips=spread),
        "finish",
        [(VMEM, a) for a in (far[:tall], far_got, near_keep, near_got)],
        [shape_of((steps, own, weight.shape[1]), BF16)],
    )[0]


def solution(mesh):
    return jax.shard_map(
        shards,
        mesh=mesh,
        in_specs=(
            P(None, ("groups", "fsdp"), "tensor"),
            P(("groups", "fsdp", "tensor"), None, None, None, None),
            P(None, ("groups", "fsdp"), "tensor"),
            P(("groups", "fsdp", "tensor")),
            P("tensor", None),
            P("tensor", "fsdp"),
            P(None, ("fsdp", "tensor")),
        ),
        out_specs=P(None, ("groups", "fsdp", "tensor"), None),
        check_vma=False,
    )
```

time: 65.1 us -> 43.7 us (0.67)
  local copies, waits for them, and re-layouts: 16.9 us -> 0.06 us
  Pallas kernels: 25.3 us -> 21 us
  starting transfers between devices: 13.3 us -> 14.3 us
  waiting for transfers between devices: 8.71 us -> 7.72 us
    unnamed x14 -> x0, local copies, waits for them, and re-layouts: 16.9 us -> none
    pallas_call x9 -> x11, Pallas kernels: 25.3 us -> 21 us  [call(): pl.pallas_call(kernel, in_specs=list(specs), out_specs=[VMEM] * len(outs)...]
    ppermute x16, starting transfers between devices: 13.3 us -> 14.3 us  [shards(): lax.ppermute(x, axis, [(i, i ^ k) for i in range(lax.axis_size(axis))])]
    ppermute x16, waiting for transfers between devices: 8.71 us -> 7.72 us  [shards(): lax.ppermute(x, axis, [(i, i ^ k) for i in range(lax.axis_size(axis))])]
  transfers between devices with their start and end apart: 16 -> 16, of which waited for: 6 -> 5; matrix products, arithmetic and copies ran while one was open for 1% -> 1% of each run, Pallas kernels for 26% -> 43%
where the time goes in v3:
time: 43.7 us; the launch traced here: 43.5 us
  Pallas kernels  21 us (48%)
  starting transfers between devices  14.3 us (33%)
  waiting for transfers between devices  7.72 us (18%)
    pallas_call x11, Pallas kernels, call(): pl.pallas_call(kernel, in_specs=list(specs), out_specs=[VMEM] * len(outs)...  21 us
    ppermute x16, starting transfers between devices, shards(): lax.ppermute(x, axis, [(i, i ^ k) for i in range(lax.axis_size(axis))])  14.3 us
    ppermute x16, waiting for transfers between devices, shards(): lax.ppermute(x, axis, [(i, i ^ k) for i in range(lax.axis_size(axis))])  7.72 us
  transfers between devices with their start and end apart: 16, of which 5 were waited for; matrix products, arithmetic and copies ran while one was open for 1% of the time, Pallas kernels for 43%

profile of v3, /device:TPU:0, one launch (start us, length us, event | category | flops | bytes accessed | tf_op | source)
XLA Modules:
  0.0 43.5 jit_solution(4202000162599821082)
XLA Ops:
  0.0 1.2 %pack.1 = (bf16[320,128]{1,0:T(8,128)(2,1)S(1)}, bf16[320,128]{1,0:T(8,128)(2,1)S(1)}, bf16[2,320,128]{2,1,0:T(8,128)(2,1)S(1)}) custom-call(bf16[8,8,2048]{2,1,0:T(8,128)(2,1)} %query_hbm.1, bf16[8,8,512]{2,1,0:T(8,128)(2,1)} %new_hbm.1), custom_call_target="tpu_custom_call" | custom-call | tf_op jit(solution)/shard_map/pack/pallas_call | solution.py:39
  1.2 3.0 %collective-permute-start.1 = (bf16[2,320,128]{2,1,0:T(8,128)(2,1)S(1)}, bf16[2,320,128]{2,1,0:T(8,128)(2,1)S(1)}, u32[]{:S(2)}, u32[]{:S(2)}) collective-permute-start(bf16[2,320,128]{2,1,0:T(8,128)(2,1)S(1)} %get-tuple-element.41), channel_id=1, source_target_pairs={{0,2},{1,3},{2,0},{3,1},{4,6},{5,7},{6,4},{7,5},{8,10},{9,11},{10,... | collective-permute-start | bytes 491528 | tf_op jit(solution)/shard_map/ppermute | solution.py:379
  4.2 2.3 %stage.1 = (bf16[2,2,8,528,128]{4,3,2,1,0:T(8,128)(2,1)S(1)}, bf16[32,2048]{1,0:T(8,128)(2,1)S(1)}) custom-call(bf16[320,128]{1,0:T(8,128)(2,1)S(1)} %get-tuple-element.38.after_ref.refs_0_, bf16[2,2,8,512,128]{4,3,2,1,0:T(8,128)(2,1)} %cache_hbm.1, bf16[16,2048]{1,0:T(8,128)(2,1)} %bitcast.5, bf16[64,512]{1,0:T(8,128)(2,1)} %up_hbm.1), custom_call_target="tpu_custom_call" | custom-call | bytes 4194304 | tf_op jit(solution)/shard_map/stage/pallas_call | solution.py:39
  6.5 2.6 %collective-permute-start.4 = (bf16[32,2048]{1,0:T(8,128)(2,1)S(1)}, bf16[32,2048]{1,0:T(8,128)(2,1)S(1)}, u32[]{:S(2)}, u32[]{:S(2)}) collective-permute-start(bf16[32,2048]{1,0:T(8,128)(2,1)S(1)} %get-tuple-element.56.refs_1_), channel_id=1, source_target_pairs={{0,8},{4,12},{8,0},{12,4},{1,9},{5,13},{9,1},{13,5},{2,10},{6,14},... | collective-permute-start | bytes 393224 | tf_op jit(solution)/shard_map/ppermute | solution.py:379
  9.2 1.6 %collective-permute-start.3 = (bf16[32,2048]{1,0:T(8,128)(2,1)S(1)}, bf16[32,2048]{1,0:T(8,128)(2,1)S(1)}, u32[]{:S(2)}, u32[]{:S(2)}) collective-permute-start(bf16[32,2048]{1,0:T(8,128)(2,1)S(1)} %get-tuple-element.56.refs_1_), channel_id=1, source_target_pairs={{0,4},{4,0},{8,12},{12,8},{1,5},{5,1},{9,13},{13,9},{2,6},{6,2},{1... | collective-permute-start | bytes 393224 | tf_op jit(solution)/shard_map/ppermute | solution.py:379
  10.9 0.5 %collective-permute-start.2 = (bf16[320,128]{1,0:T(8,128)(2,1)S(1)}, bf16[320,128]{1,0:T(8,128)(2,1)S(1)}, u32[]{:S(2)}, u32[]{:S(2)}) collective-permute-start(bf16[320,128]{1,0:T(8,128)(2,1)S(1)} %get-tuple-element.74), channel_id=1, source_target_pairs={{0,1},{1,0},{2,3},{3,2},{4,5},{5,4},{6,7},{7,6},{8,9},{9,8},{10,11... | collective-permute-start | bytes 245768 | tf_op jit(solution)/shard_map/ppermute | solution.py:379
  11.4 0.8 %collective-permute-done.refs_1_ = bf16[320,128]{1,0:T(8,128)(2,1)S(1)} collective-permute-done((bf16[320,128]{1,0:T(8,128)(2,1)S(1)}, bf16[320,128]{1,0:T(8,128)(2,1)S(1)}, u32[]{:S(2)}, u32[]{:S(2)}) %collective-permute-start) | collective-permute-done | bytes 81952 | tf_op jit(solution)/shard_map/ppermute | solution.py:379
  12.1 0.2 collective-permute-done.2.refs_3_
  12.3 4.9 %attend.1 = (bf16[16,2048]{1,0:T(8,128)(2,1)S(1)}, bf16[16,2048]{1,0:T(8,128)(2,1)S(1)}, bf16[16,2048]{1,0:T(8,128)(2,1)S(1)}, bf16[16,2048]{1,0:T(8,128)(2,1)S(...) custom-call(s32[2]{0:T(128)} %length_hbm.1, ...), custom_call_target="tpu_custom_call", output_to_operand_aliasing={{5}: (6, {})} | custom-call | tf_op jit(solution)/shard_map/attend/pallas_call | solution.py:39
  17.3 1.1 %collective-permute-start.5 = (bf16[16,2048]{1,0:T(8,128)(2,1)S(1)}, bf16[16,2048]{1,0:T(8,128)(2,1)S(1)}, u32[]{:S(2)}, u32[]{:S(2)}) collective-permute-start(bf16[16,2048]{1,0:T(8,128)(2,1)S(1)} %get-tuple-element.50), channel_id=1, source_target_pairs={{0,2},{1,3},{2,0},{3,1},{4,6},{5,7},{6,4},{7,5},{8,10},{9,11},{10,... | collective-permute-start | bytes 196616 | tf_op jit(solution)/shard_map/ppermute | solution.py:379
  18.3 0.1 collective-permute-start.6
  18.4 1.1 %collective-permute-start.7 = (bf16[16,2048]{1,0:T(8,128)(2,1)S(1)}, bf16[16,2048]{1,0:T(8,128)(2,1)S(1)}, u32[]{:S(2)}, u32[]{:S(2)}) collective-permute-start(bf16[16,2048]{1,0:T(8,128)(2,1)S(1)} %get-tuple-element.52), channel_id=1, source_target_pairs={{0,3},{1,2},{2,1},{3,0},{4,7},{5,6},{6,5},{7,4},{8,11},{9,10},{10,... | collective-permute-start | bytes 196616 | tf_op jit(solution)/shard_map/ppermute | solution.py:379
  19.5 0.4 %collective-permute-start.9 = (bf16[32,2048]{1,0:T(8,128)(2,1)S(1)}, bf16[32,2048]{1,0:T(8,128)(2,1)S(1)}, u32[]{:S(2)}, u32[]{:S(2)}) collective-permute-start(bf16[32,2048]{1,0:T(8,128)(2,1)S(1)} %collective-permute-done.4.refs_3_), channel_id=1, source_target_pairs={{0,4},{4,0},{8,12},{12,8},{1,5},{5,1},{9,13},{13,9},{2,6},{6,2},{1... | collective-permute-start | bytes 393224 | tf_op jit(solution)/shard_map/ppermute | solution.py:379
  19.9 2.2 %fetch.1.refs_5_ = bf16[1,2048,1024]{2,1,0:T(8,128)(2,1)S(1)} custom-call(bf16[16,2048]{1,0:T(8,128)(2,1)S(1)} %get-tuple-element.49.after_ref.refs_0_, bf16[2048,8192]{1,0:T(8,128)(2,1)} %refs_5_.3), custom_call_target="tpu_custom_call" | custom-call | bytes 4194304 | tf_op jit(solution)/shard_map/fetch/pallas_call | solution.py:39
  22.1 0.5 %collective-permute-done.7.refs_3_ = bf16[16,2048]{1,0:T(8,128)(2,1)S(1)} collective-permute-done((bf16[16,2048]{1,0:T(8,128)(2,1)S(1)}, bf16[16,2048]{1,0:T(8,128)(2,1)S(1)}, u32[]{:S(2)}, u32[]{:S(2)}) %collective-permute-start.7) | collective-permute-done | bytes 65568 | tf_op jit(solution)/shard_map/ppermute | solution.py:379
  22.7 3.5 %project.3 = (f32[32,4096]{1,0:T(8,128)S(1)}, bf16[32,4096]{1,0:T(8,128)(2,1)S(1)}, bf16[2,2048,1024]{2,1,0:T(8,128)(2,1)S(1)}) custom-call(bf16[16,2048]{1,0:T(8,128)(2,1)S(1)} %get-tuple-element.49.after_ref.refs_0_, bf16[16,2048]{1,0:T(8,128)(2,1)S(1)} %collective-permute-done.5.refs_1_, bf16[16,2048]{1,0:T(8,128)(2,1)S(1)} %collective-permute-done.6.refs_2_, ...), custom_call_target="tpu_custom_call" | custom-call | flops 1073741824 | bytes 16777216 | tf_op jit(solution)/shard_map/project/pallas_call | solution.py:39
  26.2 0.6 %collective-permute-start.8 = (bf16[32,4096]{1,0:T(8,128)(2,1)S(1)}, bf16[32,4096]{1,0:T(8,128)(2,1)S(1)}, u32[]{:S(2)}, u32[]{:S(2)}) collective-permute-start(bf16[32,4096]{1,0:T(8,128)(2,1)S(1)} %get-tuple-element.55), channel_id=1, source_target_pairs={{0,1},{1,0},{2,3},{3,2},{4,5},{5,4},{6,7},{7,6},{8,9},{9,8},{10,11... | collective-permute-start | bytes 786440 | tf_op jit(solution)/shard_map/ppermute | solution.py:379
  26.8 0.3 lower.1
  27.2 3.5 %project.4 = (f32[32,2048]{1,0:T(8,128)S(1)}, bf16[32,2048]{1,0:T(8,128)(2,1)S(1)}, bf16[2,2048,1024]{2,1,0:T(8,128)(2,1)S(1)}) custom-call(bf16[16,2048]{1,0:T(8,128)(2,1)S(1)} %get-tuple-element.49.after_ref.refs_0_, bf16[16,2048]{1,0:T(8,128)(2,1)S(1)} %collective-permute-done.5.refs_1_, bf16[16,2048]{1,0:T(8,128)(2,1)S(1)} %collective-permute-done.6.refs_2_, ...), custom_call_target="tpu_custom_call" | custom-call | flops 536870912 | bytes 8388608 | tf_op jit(solution)/shard_map/project/pallas_call | solution.py:39
  30.7 0.5 %collective-permute-start.14 = (bf16[4,64,512]{2,1,0:T(8,128)(2,1)S(1)}, bf16[4,64,512]{2,1,0:T(8,128)(2,1)S(1)}, u32[]{:S(2)}, u32[]{:S(2)}) collective-permute-start(bf16[4,64,512]{2,1,0:T(8,128)(2,1)S(1)} %get-tuple-element.68.refs_6_), channel_id=1, source_target_pairs={{0,1},{1,0},{2,3},{3,2},{4,5},{5,4},{6,7},{7,6},{8,9},{9,8},{10,11... | collective-permute-start | bytes 786440 | tf_op jit(solution)/shard_map/ppermute | solution.py:379
  31.3 0.1 subtract_convert_fusion
  31.3 0.1 fusion.1
  31.5 0.1 fusion
  31.6 1.0 %collective-permute-start.11 = (bf16[16,4352]{1,0:T(8,128)(2,1)S(1)}, bf16[16,4352]{1,0:T(8,128)(2,1)S(1)}, u32[]{:S(2)}, u32[]{:S(2)}) collective-permute-start(bf16[16,4352]{1,0:T(8,128)(2,1)S(1)} %fusion), channel_id=1, source_target_pairs={{0,2},{1,3},{2,0},{3,1},{4,6},{5,7},{6,4},{7,5},{8,10},{9,11},{10,... | collective-permute-start | bytes 417800 | tf_op jit(solution)/shard_map/ppermute | solution.py:379
  32.6 1.7 %project.5 = (f32[32,2048]{1,0:T(8,128)S(1)}, bf16[32,2048]{1,0:T(8,128)(2,1)S(1)}) custom-call(bf16[16,2048]{1,0:T(8,128)(2,1)S(1)} %get-tuple-element.49.after_ref.refs_0_, bf16[16,2048]{1,0:T(8,128)(2,1)S(1)} %collective-permute-done.5.refs_1_, bf16[16,2048]{1,0:T(8,128)(2,1)S(1)} %collective-permute-done.6.refs_2_, ...), custom_call_target="tpu_custom_call" | custom-call | flops 536870912 | bytes 8388608 | tf_op jit(solution)/shard_map/project/pallas_call | solution.py:39
  34.3 0.1 collective-permute-start.13
  34.4 0.5 %collective-permute-start.12 = (bf16[32,2048]{1,0:T(8,128)(2,1)S(1)}, bf16[32,2048]{1,0:T(8,128)(2,1)S(1)}, u32[]{:S(2)}, u32[]{:S(2)}) collective-permute-start(bf16[32,2048]{1,0:T(8,128)(2,1)S(1)} %get-tuple-element.66), channel_id=1, source_target_pairs={{0,1},{1,0},{2,3},{3,2},{4,5},{5,4},{6,7},{7,6},{8,9},{9,8},{10,11... | collective-permute-start | bytes 393224 | tf_op jit(solution)/shard_map/ppermute | solution.py:379
  34.9 2.3 %collective-permute-done.11 = bf16[16,4352]{1,0:T(8,128)(2,1)S(1)} collective-permute-done((bf16[16,4352]{1,0:T(8,128)(2,1)S(1)}, bf16[16,4352]{1,0:T(8,128)(2,1)S(1)}, u32[]{:S(2)}, u32[]{:S(2)}) %collective-permute-start.11) | collective-permute-done | bytes 139296 | tf_op jit(solution)/shard_map/ppermute | solution.py:379
  37.2 0.4 adapt.1
  37.6 1.1 %collective-permute-start.15 = (bf16[16,4096]{1,0:T(8,128)(2,1)S(1)}, bf16[16,4096]{1,0:T(8,128)(2,1)S(1)}, u32[]{:S(2)}, u32[]{:S(2)}) collective-permute-start(bf16[16,4096]{1,0:T(8,128)(2,1)S(1)} %get-tuple-element.69), channel_id=1, source_target_pairs={{0,2},{1,3},{2,0},{3,1},{4,6},{5,7},{6,4},{7,5},{8,10},{9,11},{10,... | collective-permute-start | bytes 393224 | tf_op jit(solution)/shard_map/ppermute | solution.py:379
  38.8 3.9 %collective-permute-done.15.far_got_ref = bf16[16,4096]{1,0:T(8,128)(2,1)S(1)} collective-permute-done((bf16[16,4096]{1,0:T(8,128)(2,1)S(1)}, bf16[16,4096]{1,0:T(8,128)(2,1)S(1)}, u32[]{:S(2)}, u32[]{:S(2)}) %collective-permute-start.15) | collective-permute-done | bytes 131104 | tf_op jit(solution)/shard_map/ppermute | solution.py:379
  42.7 0.8 %finish.1 = bf16[8,2,8192]{2,1,0:T(2,128)(2,1)} custom-call(f32[16,4096]{1,0:T(8,128)S(1)} %slice.43.far_ref, bf16[16,4096]{1,0:T(8,128)(2,1)S(1)} %collective-permute-done.15.far_got_ref, f32[16,4096]{1,0:T(8,128)S(1)} %get-tuple-element.70.near_ref, bf16[16,4096]{1,0:T(8,128)(2,1)S(1)} %slice.50.near_got_ref), custom_call_target="tpu_custom_call" | custom-call | tf_op jit(solution)/shard_map/finish/pallas_call | solution.py:39
  (20 shorter events, 0.2 us)
Async XLA Ops:
  1.2 8.0 %collective-permute-start.1 = (bf16[2,320,128]{2,1,0:T(8,128)(2,1)S(1)}, bf16[2,320,128]{2,1,0:T(8,128)(2,1)S(1)}, u32[]{:S(2)}, u32[]{:S(2)}) collective-permute-start(bf16[2,320,128]{2,1,0:T(8,128)(2,1)S(1)} %get-tuple-element.41), channel_id=1, source_target_pairs={{0,2},{1,3},{2,0},{3,1},{4,6},{5,7},{6,4},{7,5},{8,10},{9,11},{10,... | collective-permute-start | bytes 491528 | tf_op jit(solution)/shard_map/ppermute | solution.py:379
  6.5 10.7 %collective-permute-start.4 = (bf16[32,2048]{1,0:T(8,128)(2,1)S(1)}, bf16[32,2048]{1,0:T(8,128)(2,1)S(1)}, u32[]{:S(2)}, u32[]{:S(2)}) collective-permute-start(bf16[32,2048]{1,0:T(8,128)(2,1)S(1)} %get-tuple-element.56.refs_1_), channel_id=1, source_target_pairs={{0,8},{4,12},{8,0},{12,4},{1,9},{5,13},{9,1},{13,5},{2,10},{6,14},... | collective-permute-start | bytes 393224 | tf_op jit(solution)/shard_map/ppermute | solution.py:379
  9.2 8.0 %collective-permute-start.3 = (bf16[32,2048]{1,0:T(8,128)(2,1)S(1)}, bf16[32,2048]{1,0:T(8,128)(2,1)S(1)}, u32[]{:S(2)}, u32[]{:S(2)}) collective-permute-start(bf16[32,2048]{1,0:T(8,128)(2,1)S(1)} %get-tuple-element.56.refs_1_), channel_id=1, source_target_pairs={{0,4},{4,0},{8,12},{12,8},{1,5},{5,1},{9,13},{13,9},{2,6},{6,2},{1... | collective-permute-start | bytes 393224 | tf_op jit(solution)/shard_map/ppermute | solution.py:379
  10.9 1.3 %collective-permute-start = (bf16[320,128]{1,0:T(8,128)(2,1)S(1)}, bf16[320,128]{1,0:T(8,128)(2,1)S(1)}, u32[]{:S(2)}, u32[]{:S(2)}) collective-permute-start(bf16[320,128]{1,0:T(8,128)(2,1)S(1)} %get-tuple-element.39), channel_id=1, source_target_pairs={{0,1},{1,0},{2,3},{3,2},{4,5},{5,4},{6,7},{7,6},{8,9},{9,8},{10,11... | collective-permute-start | bytes 245768 | tf_op jit(solution)/shard_map/ppermute | solution.py:379
  10.9 1.4 %collective-permute-start.2 = (bf16[320,128]{1,0:T(8,128)(2,1)S(1)}, bf16[320,128]{1,0:T(8,128)(2,1)S(1)}, u32[]{:S(2)}, u32[]{:S(2)}) collective-permute-start(bf16[320,128]{1,0:T(8,128)(2,1)S(1)} %get-tuple-element.74), channel_id=1, source_target_pairs={{0,1},{1,0},{2,3},{3,2},{4,5},{5,4},{6,7},{7,6},{8,9},{9,8},{10,11... | collective-permute-start | bytes 245768 | tf_op jit(solution)/shard_map/ppermute | solution.py:379
  17.3 4.9 %collective-permute-start.5 = (bf16[16,2048]{1,0:T(8,128)(2,1)S(1)}, bf16[16,2048]{1,0:T(8,128)(2,1)S(1)}, u32[]{:S(2)}, u32[]{:S(2)}) collective-permute-start(bf16[16,2048]{1,0:T(8,128)(2,1)S(1)} %get-tuple-element.50), channel_id=1, source_target_pairs={{0,2},{1,3},{2,0},{3,1},{4,6},{5,7},{6,4},{7,5},{8,10},{9,11},{10,... | collective-permute-start | bytes 196616 | tf_op jit(solution)/shard_map/ppermute | solution.py:379
  18.3 3.8 %collective-permute-start.6 = (bf16[16,2048]{1,0:T(8,128)(2,1)S(1)}, bf16[16,2048]{1,0:T(8,128)(2,1)S(1)}, u32[]{:S(2)}, u32[]{:S(2)}) collective-permute-start(bf16[16,2048]{1,0:T(8,128)(2,1)S(1)} %get-tuple-element.51), channel_id=1, source_target_pairs={{0,1},{1,0},{2,3},{3,2},{4,5},{5,4},{6,7},{7,6},{8,9},{9,8},{10,11... | collective-permute-start | bytes 196616 | tf_op jit(solution)/shard_map/ppermute | solution.py:379
  18.4 4.3 %collective-permute-start.7 = (bf16[16,2048]{1,0:T(8,128)(2,1)S(1)}, bf16[16,2048]{1,0:T(8,128)(2,1)S(1)}, u32[]{:S(2)}, u32[]{:S(2)}) collective-permute-start(bf16[16,2048]{1,0:T(8,128)(2,1)S(1)} %get-tuple-element.52), channel_id=1, source_target_pairs={{0,3},{1,2},{2,1},{3,0},{4,7},{5,6},{6,5},{7,4},{8,11},{9,10},{10,... | collective-permute-start | bytes 196616 | tf_op jit(solution)/shard_map/ppermute | solution.py:379
  19.5 7.3 %collective-permute-start.9 = (bf16[32,2048]{1,0:T(8,128)(2,1)S(1)}, bf16[32,2048]{1,0:T(8,128)(2,1)S(1)}, u32[]{:S(2)}, u32[]{:S(2)}) collective-permute-start(bf16[32,2048]{1,0:T(8,128)(2,1)S(1)} %collective-permute-done.4.refs_3_), channel_id=1, source_target_pairs={{0,4},{4,0},{8,12},{12,8},{1,5},{5,1},{9,13},{13,9},{2,6},{6,2},{1... | collective-permute-start | bytes 393224 | tf_op jit(solution)/shard_map/ppermute | solution.py:379
  26.2 5.2 %collective-permute-start.8 = (bf16[32,4096]{1,0:T(8,128)(2,1)S(1)}, bf16[32,4096]{1,0:T(8,128)(2,1)S(1)}, u32[]{:S(2)}, u32[]{:S(2)}) collective-permute-start(bf16[32,4096]{1,0:T(8,128)(2,1)S(1)} %get-tuple-element.55), channel_id=1, source_target_pairs={{0,1},{1,0},{2,3},{3,2},{4,5},{5,4},{6,7},{7,6},{8,9},{9,8},{10,11... | collective-permute-start | bytes 786440 | tf_op jit(solution)/shard_map/ppermute | solution.py:379
  27.1 4.1 %collective-permute-start.10 = (bf16[32,128]{1,0:T(8,128)(2,1)S(1)}, bf16[32,128]{1,0:T(8,128)(2,1)S(1)}, u32[]{:S(2)}, u32[]{:S(2)}) collective-permute-start(bf16[32,128]{1,0:T(8,128)(2,1)S(1)} %get-tuple-element.61), channel_id=1, source_target_pairs={{0,1},{1,0},{2,3},{3,2},{4,5},{5,4},{6,7},{7,6},{8,9},{9,8},{10,11... | collective-permute-start | bytes 24584 | tf_op jit(solution)/shard_map/ppermute | solution.py:379
  30.7 6.5 %collective-permute-start.14 = (bf16[4,64,512]{2,1,0:T(8,128)(2,1)S(1)}, bf16[4,64,512]{2,1,0:T(8,128)(2,1)S(1)}, u32[]{:S(2)}, u32[]{:S(2)}) collective-permute-start(bf16[4,64,512]{2,1,0:T(8,128)(2,1)S(1)} %get-tuple-element.68.refs_6_), channel_id=1, source_target_pairs={{0,1},{1,0},{2,3},{3,2},{4,5},{5,4},{6,7},{7,6},{8,9},{9,8},{10,11... | collective-permute-start | bytes 786440 | tf_op jit(solution)/shard_map/ppermute | solution.py:379
  31.6 5.6 %collective-permute-start.11 = (bf16[16,4352]{1,0:T(8,128)(2,1)S(1)}, bf16[16,4352]{1,0:T(8,128)(2,1)S(1)}, u32[]{:S(2)}, u32[]{:S(2)}) collective-permute-start(bf16[16,4352]{1,0:T(8,128)(2,1)S(1)} %fusion), channel_id=1, source_target_pairs={{0,2},{1,3},{2,0},{3,1},{4,6},{5,7},{6,4},{7,5},{8,10},{9,11},{10,... | collective-permute-start | bytes 417800 | tf_op jit(solution)/shard_map/ppermute | solution.py:379
  34.3 2.9 %collective-permute-start.13 = (bf16[32,2048]{1,0:T(8,128)(2,1)S(1)}, bf16[32,2048]{1,0:T(8,128)(2,1)S(1)}, u32[]{:S(2)}, u32[]{:S(2)}) collective-permute-start(bf16[32,2048]{1,0:T(8,128)(2,1)S(1)} %get-tuple-element.67), channel_id=1, source_target_pairs={{0,1},{1,0},{2,3},{3,2},{4,5},{5,4},{6,7},{7,6},{8,9},{9,8},{10,11... | collective-permute-start | bytes 393224 | tf_op jit(solution)/shard_map/ppermute | solution.py:379
  34.4 2.8 %collective-permute-start.12 = (bf16[32,2048]{1,0:T(8,128)(2,1)S(1)}, bf16[32,2048]{1,0:T(8,128)(2,1)S(1)}, u32[]{:S(2)}, u32[]{:S(2)}) collective-permute-start(bf16[32,2048]{1,0:T(8,128)(2,1)S(1)} %get-tuple-element.66), channel_id=1, source_target_pairs={{0,1},{1,0},{2,3},{3,2},{4,5},{5,4},{6,7},{7,6},{8,9},{9,8},{10,11... | collective-permute-start | bytes 393224 | tf_op jit(solution)/shard_map/ppermute | solution.py:379
  37.6 5.0 %collective-permute-start.15 = (bf16[16,4096]{1,0:T(8,128)(2,1)S(1)}, bf16[16,4096]{1,0:T(8,128)(2,1)S(1)}, u32[]{:S(2)}, u32[]{:S(2)}) collective-permute-start(bf16[16,4096]{1,0:T(8,128)(2,1)S(1)} %get-tuple-element.69), channel_id=1, source_target_pairs={{0,2},{1,3},{2,0},{3,1},{4,6},{5,7},{6,4},{7,5},{8,10},{9,11},{10,... | collective-permute-start | bytes 393224 | tf_op jit(solution)/shard_map/ppermute | solution.py:379

commit v4 on v3

--- a/solution.py
+++ b/solution.py
@@ -74,12 +74,22 @@
     return copies
 
 
-def pack_kernel(query_hbm, new_hbm, *refs, parts, own, steps):
-    *block_refs, query_ref, new_ref, sem = refs
-    copies = [
-        pltpu.make_async_copy(query_hbm, query_ref, sem.at[0]),
-        pltpu.make_async_copy(new_hbm, new_ref, sem.at[1]),
+def pack_kernel(query_hbm, new_hbm, cache_hbm, down_hbm, up_hbm, *refs, parts, own, steps):
+    *block_refs, cache_ref, factor_ref, query_ref, new_ref, up_ref, sem = refs
+    slot, depth = down_hbm.shape
+    pairs = [
+        (query_hbm, query_ref),
+        (new_hbm, new_ref),
+        (up_hbm, up_ref),
+        (down_hbm, factor_ref.at[pl.ds(0, slot)]),
     ]
+    slots = pl.ds(0, cache_hbm.shape[3])
+    pairs += [
+        (cache_hbm.at[r, part], cache_ref.at[r, part, :, slots])
+        for r in range(own)
+        for part in range(2)
+    ]
+    copies = [pltpu.make_async_copy(*pair, sem.at[i]) for i, pair in enumerate(pairs)]
     for copy in copies:
         copy.start()
     me = lax.axis_index("tensor")
@@ -91,7 +101,7 @@
     part_out = (i >> log2(steps * own)) ^ me
     source = step_out * (parts * own) + part_out * own + row_out
     select = jnp.where(source == j, 1.0, 0.0).astype(BF16)
-    for copy in copies:
+    for copy in copies[:3]:
         copy.wait()
     queries = dot(select, query_ref[...].reshape(count, query_ref.shape[2]))
     new = dot(select, new_ref[...].reshape(count, new_ref.shape[2]))
@@ -112,33 +122,12 @@
             block_refs[k][...] = block
         else:
             block_refs[-1][k - parts // 2] = block
-
-
-def stage_kernel(after_ref, cache_hbm, down_hbm, up_hbm, cache_ref, factor_ref, up_ref, sem):
-    slot, depth = down_hbm.shape
-    copies = [
-        pltpu.make_async_copy(up_hbm, up_ref, sem.at[0]),
-        pltpu.make_async_copy(down_hbm, factor_ref.at[pl.ds(0, slot)], sem.at[1]),
-    ]
-    slots = pl.ds(0, cache_hbm.shape[3])
-    for r in range(cache_hbm.shape[0]):
-        for part in range(2):
-            copies.append(
-                pltpu.make_async_copy(
-                    cache_hbm.at[r, part],
-                    cache_ref.at[r, part, :, slots],
-                    sem.at[2 + 2 * r + part],
-                )
-            )
-    for copy in copies:
-        copy.start()
     cut = up_ref.shape[1]
     per = depth // cut
     tall = RANK // per
-    copies[0].wait()
     for c in range(per):
         factor_ref[slot : slot + tall, c * cut : (c + 1) * cut] = up_ref[c * tall : (c + 1) * tall, :]
-    for copy in copies[1:]:
+    for copy in copies[3:]:
         copy.wait()
 
 
@@ -147,7 +136,7 @@
     weight_hbm, refs = refs[0], refs[2:]
     out_refs, refs = refs[:parts], refs[parts:]
     strips_ref, cache_ref, length_ref, held_ref, attended_ref = refs[:5]
-    scores_ref, weights_ref, length_sem, sem = refs[5:]
+    scores_ref, weights_ref, mask_ref, length_sem, sem = refs[5:]
     length_copy = pltpu.make_async_copy(length_hbm, length_ref, length_sem)
     length_copy.start()
     heads = HEADS // parts
@@ -156,7 +145,6 @@
     tall = own * steps
     slots = cache_ref.shape[3] - tall
     count = GROUP * steps
-    turns = own * KV_HEADS
     weight_copies = strip_copies(weight_hbm, strips_ref, sem, 0)
     for copy in weight_copies:
         copy.start()
@@ -184,38 +172,40 @@
 
     slot = lax.broadcasted_iota(jnp.int32, (count, slots + tall), 1)
     step = lax.broadcasted_iota(jnp.int32, (count, slots + tall), 0) & (steps - 1)
-    ones = jnp.ones((slots + tall, HEAD_DIM), BF16)
     length_copy.wait()
-
-    def turn(j, _):
-        scored = jnp.minimum(j, turns - 1)
-        r, g = scored >> log2(KV_HEADS), scored & (KV_HEADS - 1)
-        summed = jnp.maximum(j - 2, 0)
-        r_out, g_out = summed >> log2(KV_HEADS), summed & (KV_HEADS - 1)
-
+    for r in range(own):
         fresh = slot - slots - r * steps
         valid = (slot < length_ref[r]) | ((fresh >= 0) & (fresh <= step))
-        scores = dot_rows(queries(r, g), cache_ref[r, 0, g]) * (HEAD_DIM**-0.5 * LOG2_E)
-        before = scores_ref[(j + 1) & 1]
-        weights = jnp.exp2(before - before.max(-1, keepdims=True))
-        values = jnp.concatenate([cache_ref[r_out, 1, g_out], ones], axis=1)
-        mixed = dot(weights_ref[j & 1], values)
-        mixed = mixed[:count] + mixed[count:]
-        mixed = mixed[:, :HEAD_DIM] / mixed[:, HEAD_DIM:]
-
-        high, rest = split(weights)
-        weights_ref[(j + 1) & 1, 0:count, :] = high
-        weights_ref[(j + 1) & 1, count : 2 * count, :] = rest
-        scores_ref[j & 1] = jnp.where(valid, scores, -1e30)
-        row = pl.ds(pl.multiple_of(r_out * steps, steps), steps)
-        for h in range(GROUP):
-            head = g_out * GROUP + h
-            attended_ref[head >> log2(heads), head & (heads - 1), row, :] = mixed[
-                h * steps : (h + 1) * steps
-            ]
+        mask_ref[r] = jnp.where(valid, 0.0, -1e30)
+    ones = jnp.ones((slots + tall, HEAD_DIM), BF16)
+
+    def turn(i, _):
+        scored = jnp.minimum(i, KV_HEADS - 1)
+        summed = jnp.maximum(i - 2, 0)
+        rows = range(own)
+        mixed = [
+            dot(weights_ref[r], jnp.concatenate([cache_ref[r, 1, summed], ones], axis=1)) for r in rows
+        ]
+        before = [scores_ref[r] for r in rows]
+        weights = [jnp.exp2(b - b.max(-1, keepdims=True)) for b in before]
+        scores = [
+            dot_rows(queries(r, scored), cache_ref[r, 0, scored]) * (HEAD_DIM**-0.5 * LOG2_E)
+            + mask_ref[r]
+            for r in rows
+        ]
+        for r in rows:
+            weights_ref[r] = jnp.concatenate(split(weights[r]), axis=0)
+            scores_ref[r] = scores[r]
+            total = mixed[r][:count] + mixed[r][count:]
+            total = total[:, :HEAD_DIM] / total[:, HEAD_DIM:]
+            for h in range(GROUP):
+                head = summed * GROUP + h
+                attended_ref[
+                    head >> log2(heads), head & (heads - 1), r * steps : (r + 1) * steps, :
+                ] = total[h * steps : (h + 1) * steps]
         return 0
 
-    lax.fori_loop(0, turns + 2, turn, 0, unroll=2)
+    lax.fori_loop(0, KV_HEADS + 2, turn, 0, unroll=2)
     for k in range(parts):
         for h in range(heads):
             out_refs[k][:, h * HEAD_DIM : (h + 1) * HEAD_DIM] = attended_ref[me ^ k, h].astype(BF16)
@@ -265,7 +255,7 @@
     for strips_ref, (low, high) in zip(held_refs, spans):
         wide = strips_ref.shape[2]
 
-        @pl.loop(low, high)
+        @pl.loop(low, high + jnp.minimum(lax.axis_index("tensor"), 0))
         def _(i, strips_ref=strips_ref, place=place - low):
             out = dot(rows_ref[...], strips_ref[i])
             lanes = pl.ds(pl.multiple_of((place + i) * wide, wide), wide)
@@ -382,23 +372,22 @@
 
     block = shape_of((own * heads * steps + pieces * tall, HEAD_DIM), BF16)
     per = depth // cut
-    *blocks, cross = call(
+    *blocks, cross, cache, factors = call(
         functools.partial(pack_kernel, parts=parts, own=own, steps=steps),
         "pack",
-        [(HBM, queries), (HBM, new)],
-        [block] * sets + [shape_of((sets,) + block.shape, BF16)],
-        [pltpu.VMEM(queries.shape, BF16), pltpu.VMEM(new.shape, BF16), pltpu.SemaphoreType.DMA((2,))],
-    )
-    cache, factors = call(
-        stage_kernel,
-        "stage",
-        [(ANY, blocks[0]), (HBM, cache), (HBM, down.T), (HBM, up)],
-        [
+        [(HBM, a) for a in (queries, new, cache, down.T, up)],
+        [block] * sets
+        + [
+            shape_of((sets,) + block.shape, BF16),
             pltpu.VMEM(cache.shape[:3] + (cache.shape[3] + tall, HEAD_DIM), BF16),
             shape_of((slot + RANK // per, depth), BF16),
         ],
-        [pltpu.VMEM(up.shape, BF16), pltpu.SemaphoreType.DMA((2 + 2 * own,))],
-        cost=pl.CostEstimate(flops=0, bytes_accessed=2 * cache.size, transcendentals=0),
+        [
+            pltpu.VMEM(queries.shape, BF16),
+            pltpu.VMEM(new.shape, BF16),
+            pltpu.VMEM(up.shape, BF16),
+            pltpu.SemaphoreType.DMA((4 + 2 * own,)),
+        ],
     )
     cross = swap(cross, "tensor", sets)
     blocks = blocks[:1] + [swap(blocks[k], "tensor", k) for k in range(1, sets)]
@@ -408,7 +397,7 @@
     while bit > 1:
         factors |= {k ^ bit: swap(v, "fsdp", bit) for k, v in list(factors.items())}
         bit //= 2
-    near_factors, blocks[sets] = lax.optimization_barrier((factors[0], blocks[sets]))
+    near_factors, blocks[1] = lax.optimization_barrier((factors[0], blocks[1]))
 
     half, quarter = spread // 2, spread // 4
     early = half + quarter
@@ -423,8 +412,9 @@
             pltpu.SMEM(lengths.shape, jnp.int32),
             pltpu.VMEM((parts, own * heads * steps, HEAD_DIM), BF16),
             pltpu.VMEM((parts, heads, tall, HEAD_DIM), F32),
-            pltpu.VMEM((2, GROUP * steps, cache.shape[3]), F32),
-            pltpu.VMEM((2, 2 * GROUP * steps, cache.shape[3]), BF16),
+            pltpu.VMEM((own, GROUP * steps, cache.shape[3]), F32),
+            pltpu.VMEM((own, 2 * GROUP * steps, cache.shape[3]), BF16),
+            pltpu.VMEM((own, GROUP * steps, cache.shape[3]), F32),
             pltpu.SemaphoreType.DMA(()),
             pltpu.SemaphoreType.DMA((early,)),
         ],
@@ -506,23 +496,29 @@
             up_sets |= {k ^ bit: swap(u, "tensor", bit) for k, u in list(up_sets.items())}
             bit //= 2
 
-    middle = spread + half
-    keep_a, send_a, buffers = project(attended, weight, buffers, spread, middle, half)
-    keep_a, got_a = reduce(keep_a, send_a)
-    keep_b, send_b, _ = project(attended, weight, buffers, middle, 2 * spread)
-    keep_b, got_b = reduce(keep_b, send_b)
-
     far = far_keep + far_got.astype(F32)
     low_parts = jnp.concatenate(split(low), axis=1)
     message = jnp.concatenate([far[tall:].astype(BF16), low_parts[tall:], low_parts[:tall]], axis=1)
+    near = []
+
+    def add_near(low, high, ahead):
+        nonlocal buffers
+        keep, send, buffers = project(attended, weight, buffers, low, high, ahead)
+        near.append(reduce(keep, send))
+
+    a, b = spread + quarter, 2 * spread - quarter
+    add_near(spread, a, quarter)
+    message, attended = lax.optimization_barrier((message, attended))
     message = swap(message, "tensor", sets)
+    add_near(a, b, quarter)
+    add_near(b, 2 * spread, 0)
     near_got, low_got = message[:, :half_width], message[:, half_width:]
 
     ups = [up_sets[k] for k in range(len(up_sets))]
     near_keep, near_send = call(
-        functools.partial(adapt_kernel, pieces=2, sets=len(ups), ordered=ordered),
+        functools.partial(adapt_kernel, pieces=len(near), sets=len(ups), ordered=ordered),
         "adapt",
-        [(VMEM, a) for a in (low, low_got, keep_a, keep_b, got_a, got_b, *ups)],
+        [(VMEM, a) for a in (low, low_got, *[k for k, _ in near], *[g for _, g in near], *ups)],
         [shape_of((tall, half_width), F32), shape_of((tall, half_width), BF16)],
         [pltpu.VMEM((2 * tall, half_width), F32)],
     )

time: 43.7 us -> 42.8 us (0.979)
  Pallas kernels: 21 us -> 19.8 us
  starting transfers between devices: 14.3 us -> 15.5 us
  waiting for transfers between devices: 7.72 us -> 6.82 us
    ppermute x16 -> x17, starting transfers between devices: 14.3 us -> 15.5 us  [shards(): lax.ppermute(x, axis, [(i, i ^ k) for i in range(lax.axis_size(axis))])]
    pallas_call x11, Pallas kernels: 21 us -> 19.8 us  [call(): pl.pallas_call(kernel, in_specs=list(specs), out_specs=[VMEM] * len(outs)...]
    ppermute x16 -> x17, waiting for transfers between devices: 7.72 us -> 6.82 us  [shards(): lax.ppermute(x, axis, [(i, i ^ k) for i in range(lax.axis_size(axis))])]
  transfers between devices with their start and end apart: 16 -> 17, of which waited for: 5 -> 4; matrix products, arithmetic and copies ran while one was open for 1% -> 1% of each run, Pallas kernels for 43% -> 38%
where the time goes in v4:
time: 42.8 us; the launch traced here: 42.6 us
  Pallas kernels  19.8 us (46%)
  starting transfers between devices  15.5 us (36%)
  waiting for transfers between devices  6.82 us (16%)
    pallas_call x11, Pallas kernels, call(): pl.pallas_call(kernel, in_specs=list(specs), out_specs=[VMEM] * len(outs)...  19.8 us
    ppermute x17, starting transfers between devices, shards(): lax.ppermute(x, axis, [(i, i ^ k) for i in range(lax.axis_size(axis))])  15.5 us
    ppermute x17, waiting for transfers between devices, shards(): lax.ppermute(x, axis, [(i, i ^ k) for i in range(lax.axis_size(axis))])  6.82 us
  transfers between devices with their start and end apart: 17, of which 4 were waited for; matrix products, arithmetic and copies ran while one was open for 1% of the time, Pallas kernels for 38%

profile of v4, /device:TPU:0, one launch (start us, length us, event | category | flops | bytes accessed | tf_op | source)
XLA Modules:
  0.0 42.6 jit_solution(2666814289605641792)
XLA Ops:
  0.0 2.4 %pack.1 = (bf16[320,128]{1,0:T(8,128)(2,1)S(1)}, bf16[320,128]{1,0:T(8,128)(2,1)S(1)}, bf16[2,320,128]{2,1,0:T(8,128)(2,1)S(1)}, bf16[2,2,8,528,128]{4,3,2,1,0:T(8,128)(2,1)S(1)}, bf16[32,2048]{1,0:T(8,128)(2,1)S(1)}) custom-call(bf16[8,8,2048]{2,1,0:T(8,128)(2,1)} %query_hbm.1, bf16[8,8,512]{2,1,0:T(8,128)(2,1)} %new_hbm.1, ...), custom_call_target="tpu_custom_call" | custom-call | tf_op jit(solution)/shard_map/pack/pallas_call | solution.py:39
  2.4 3.0 %collective-permute-start.1 = (bf16[2,320,128]{2,1,0:T(8,128)(2,1)S(1)}, bf16[2,320,128]{2,1,0:T(8,128)(2,1)S(1)}, u32[]{:S(2)}, u32[]{:S(2)}) collective-permute-start(bf16[2,320,128]{2,1,0:T(8,128)(2,1)S(1)} %get-tuple-element.50), channel_id=1, source_target_pairs={{0,2},{1,3},{2,0},{3,1},{4,6},{5,7},{6,4},{7,5},{8,10},{9,11},{10,... | collective-permute-start | bytes 491528 | tf_op jit(solution)/shard_map/ppermute | solution.py:369
  5.5 2.6 %collective-permute-start.4 = (bf16[32,2048]{1,0:T(8,128)(2,1)S(1)}, bf16[32,2048]{1,0:T(8,128)(2,1)S(1)}, u32[]{:S(2)}, u32[]{:S(2)}) collective-permute-start(bf16[32,2048]{1,0:T(8,128)(2,1)S(1)} %get-tuple-element.64.refs_1_), channel_id=1, source_target_pairs={{0,8},{4,12},{8,0},{12,4},{1,9},{5,13},{9,1},{13,5},{2,10},{6,14},... | collective-permute-start | bytes 393224 | tf_op jit(solution)/shard_map/ppermute | solution.py:369
  8.1 1.6 %collective-permute-start.3 = (bf16[32,2048]{1,0:T(8,128)(2,1)S(1)}, bf16[32,2048]{1,0:T(8,128)(2,1)S(1)}, u32[]{:S(2)}, u32[]{:S(2)}) collective-permute-start(bf16[32,2048]{1,0:T(8,128)(2,1)S(1)} %get-tuple-element.64.refs_1_), channel_id=1, source_target_pairs={{0,4},{4,0},{8,12},{12,8},{1,5},{5,1},{9,13},{13,9},{2,6},{6,2},{1... | collective-permute-start | bytes 393224 | tf_op jit(solution)/shard_map/ppermute | solution.py:369
  9.7 0.1 collective-permute-start.2
  9.8 1.3 %collective-permute-done.2.refs_3_ = bf16[320,128]{1,0:T(8,128)(2,1)S(1)} collective-permute-done((bf16[320,128]{1,0:T(8,128)(2,1)S(1)}, bf16[320,128]{1,0:T(8,128)(2,1)S(1)}, u32[]{:S(2)}, u32[]{:S(2)}) %collective-permute-start.2) | collective-permute-done | bytes 81952 | tf_op jit(solution)/shard_map/ppermute | solution.py:369
  11.0 4.8 %attend.1 = (bf16[16,2048]{1,0:T(8,128)(2,1)S(1)}, bf16[16,2048]{1,0:T(8,128)(2,1)S(1)}, bf16[16,2048]{1,0:T(8,128)(2,1)S(1)}, bf16[16,2048]{1,0:T(8,128)(2,1)S(...) custom-call(s32[2]{0:T(128)} %length_hbm.1, ...), custom_call_target="tpu_custom_call", output_to_operand_aliasing={{5}: (6, {})} | custom-call | tf_op jit(solution)/shard_map/attend/pallas_call | solution.py:39
  15.8 1.8 %collective-permute-start.5 = (bf16[16,2048]{1,0:T(8,128)(2,1)S(1)}, bf16[16,2048]{1,0:T(8,128)(2,1)S(1)}, u32[]{:S(2)}, u32[]{:S(2)}) collective-permute-start(bf16[16,2048]{1,0:T(8,128)(2,1)S(1)} %get-tuple-element.58), channel_id=1, source_target_pairs={{0,2},{1,3},{2,0},{3,1},{4,6},{5,7},{6,4},{7,5},{8,10},{9,11},{10,... | collective-permute-start | bytes 196616 | tf_op jit(solution)/shard_map/ppermute | solution.py:369
  17.6 0.4 collective-permute-start.7
  18.0 1.8 %collective-permute-start.9 = (bf16[32,2048]{1,0:T(8,128)(2,1)S(1)}, bf16[32,2048]{1,0:T(8,128)(2,1)S(1)}, u32[]{:S(2)}, u32[]{:S(2)}) collective-permute-start(bf16[32,2048]{1,0:T(8,128)(2,1)S(1)} %collective-permute-done.4.refs_3_), channel_id=1, source_target_pairs={{0,4},{4,0},{8,12},{12,8},{1,5},{5,1},{9,13},{13,9},{2,6},{6,2},{1... | collective-permute-start | bytes 393224 | tf_op jit(solution)/shard_map/ppermute | solution.py:369
  19.8 2.2 %fetch.1.refs_5_ = bf16[1,2048,1024]{2,1,0:T(8,128)(2,1)S(1)} custom-call(bf16[16,2048]{1,0:T(8,128)(2,1)S(1)} %get-tuple-element.73.after_ref.refs_0_, bf16[2048,8192]{1,0:T(8,128)(2,1)} %refs_5_.3), custom_call_target="tpu_custom_call" | custom-call | bytes 4194304 | tf_op jit(solution)/shard_map/fetch/pallas_call | solution.py:39
  22.1 3.5 %project.4 = (f32[32,4096]{1,0:T(8,128)S(1)}, bf16[32,4096]{1,0:T(8,128)(2,1)S(1)}, bf16[2,2048,1024]{2,1,0:T(8,128)(2,1)S(1)}) custom-call(bf16[16,2048]{1,0:T(8,128)(2,1)S(1)} %get-tuple-element.73.after_ref.refs_0_, bf16[16,2048]{1,0:T(8,128)(2,1)S(1)} %collective-permute-done.5.refs_1_, bf16[16,2048]{1,0:T(8,128)(2,1)S(1)} %collective-permute-done.6.refs_2_, ...), custom_call_target="tpu_custom_call" | custom-call | flops 1073741824 | bytes 16777216 | tf_op jit(solution)/shard_map/project/pallas_call | solution.py:39
  25.6 0.1 collective-permute-start.8
  25.8 0.3 lower.1
  26.1 0.5 %collective-permute-start.10 = (bf16[32,128]{1,0:T(8,128)(2,1)S(1)}, bf16[32,128]{1,0:T(8,128)(2,1)S(1)}, u32[]{:S(2)}, u32[]{:S(2)}) collective-permute-start(bf16[32,128]{1,0:T(8,128)(2,1)S(1)} %get-tuple-element.69), channel_id=1, source_target_pairs={{0,1},{1,0},{2,3},{3,2},{4,5},{5,4},{6,7},{7,6},{8,9},{9,8},{10,11... | collective-permute-start | bytes 24584 | tf_op jit(solution)/shard_map/ppermute | solution.py:369
  26.6 2.2 %project.5 = (f32[32,1024]{1,0:T(8,128)S(1)}, bf16[32,1024]{1,0:T(8,128)(2,1)S(1)}, bf16[1,2048,1024]{2,1,0:T(8,128)(2,1)S(1)}) custom-call(bf16[16,2048]{1,0:T(8,128)(2,1)S(1)} %get-tuple-element.73.after_ref.refs_0_, bf16[16,2048]{1,0:T(8,128)(2,1)S(1)} %collective-permute-done.5.refs_1_, bf16[16,2048]{1,0:T(8,128)(2,1)S(1)} %collective-permute-done.6.refs_2_, ...), custom_call_target="tpu_custom_call" | custom-call | flops 268435456 | bytes 4194304 | tf_op jit(solution)/shard_map/project/pallas_call | solution.py:39
  28.8 0.1 collective-permute-start.15
  28.9 0.1 subtract_convert_fusion
  29.0 0.1 fusion.1
  29.2 0.1 fusion
  29.2 1.5 %collective-permute-start.11 = (bf16[16,4352]{1,0:T(8,128)(2,1)S(1)}, bf16[16,4352]{1,0:T(8,128)(2,1)S(1)}, u32[]{:S(2)}, u32[]{:S(2)}) collective-permute-start(bf16[16,4352]{1,0:T(8,128)(2,1)S(1)} %fusion), channel_id=1, source_target_pairs={{0,2},{1,3},{2,0},{3,1},{4,6},{5,7},{6,4},{7,5},{8,10},{9,11},{10,... | collective-permute-start | bytes 417800 | tf_op jit(solution)/shard_map/ppermute | solution.py:369
  30.7 2.2 %project.6 = (f32[32,2048]{1,0:T(8,128)S(1)}, bf16[32,2048]{1,0:T(8,128)(2,1)S(1)}, bf16[1,2048,1024]{2,1,0:T(8,128)(2,1)S(1)}) custom-call(bf16[16,2048]{1,0:T(8,128)(2,1)S(1)} %get-tuple-element.73.after_ref.refs_0_, bf16[16,2048]{1,0:T(8,128)(2,1)S(1)} %collective-permute-done.5.refs_1_, bf16[16,2048]{1,0:T(8,128)(2,1)S(1)} %collective-permute-done.6.refs_2_, ...), custom_call_target="tpu_custom_call" | custom-call | flops 536870912 | bytes 8388608 | tf_op jit(solution)/shard_map/project/pallas_call | solution.py:39
  32.9 0.3 collective-permute-start.13
  33.2 0.3 collective-permute-start.12
  33.5 0.9 %project.7 = (f32[32,1024]{1,0:T(8,128)S(1)}, bf16[32,1024]{1,0:T(8,128)(2,1)S(1)}) custom-call(bf16[16,2048]{1,0:T(8,128)(2,1)S(1)} %get-tuple-element.73.after_ref.refs_0_, bf16[16,2048]{1,0:T(8,128)(2,1)S(1)} %collective-permute-done.5.refs_1_, bf16[16,2048]{1,0:T(8,128)(2,1)S(1)} %collective-permute-done.6.refs_2_, ...), custom_call_target="tpu_custom_call" | custom-call | flops 268435456 | bytes 4194304 | tf_op jit(solution)/shard_map/project/pallas_call | solution.py:39
  34.4 0.3 collective-permute-start.14
  34.6 0.6 %collective-permute-done.11 = bf16[16,4352]{1,0:T(8,128)(2,1)S(1)} collective-permute-done((bf16[16,4352]{1,0:T(8,128)(2,1)S(1)}, bf16[16,4352]{1,0:T(8,128)(2,1)S(1)}, u32[]{:S(2)}, u32[]{:S(2)}) %collective-permute-start.11) | collective-permute-done | bytes 139296 | tf_op jit(solution)/shard_map/ppermute | solution.py:369
  35.3 0.4 %collective-permute-done.14.refs_7_ = bf16[32,1024]{1,0:T(8,128)(2,1)S(1)} collective-permute-done((bf16[32,1024]{1,0:T(8,128)(2,1)S(1)}, bf16[32,1024]{1,0:T(8,128)(2,1)S(1)}, u32[]{:S(2)}, u32[]{:S(2)}) %collective-permute-start.14) | collective-permute-done | bytes 65568 | tf_op jit(solution)/shard_map/ppermute | solution.py:369
  35.7 0.4 adapt.1
  36.1 1.2 %collective-permute-start.16 = (bf16[16,4096]{1,0:T(8,128)(2,1)S(1)}, bf16[16,4096]{1,0:T(8,128)(2,1)S(1)}, u32[]{:S(2)}, u32[]{:S(2)}) collective-permute-start(bf16[16,4096]{1,0:T(8,128)(2,1)S(1)} %get-tuple-element.85), channel_id=1, source_target_pairs={{0,2},{1,3},{2,0},{3,1},{4,6},{5,7},{6,4},{7,5},{8,10},{9,11},{10,... | collective-permute-start | bytes 393224 | tf_op jit(solution)/shard_map/ppermute | solution.py:369
  37.3 4.5 %collective-permute-done.16.far_got_ref = bf16[16,4096]{1,0:T(8,128)(2,1)S(1)} collective-permute-done((bf16[16,4096]{1,0:T(8,128)(2,1)S(1)}, bf16[16,4096]{1,0:T(8,128)(2,1)S(1)}, u32[]{:S(2)}, u32[]{:S(2)}) %collective-permute-start.16) | collective-permute-done | bytes 131104 | tf_op jit(solution)/shard_map/ppermute | solution.py:369
  41.8 0.8 %finish.1 = bf16[8,2,8192]{2,1,0:T(2,128)(2,1)} custom-call(f32[16,4096]{1,0:T(8,128)S(1)} %slice.43.far_ref, bf16[16,4096]{1,0:T(8,128)(2,1)S(1)} %collective-permute-done.16.far_got_ref, f32[16,4096]{1,0:T(8,128)S(1)} %get-tuple-element.86.near_ref, bf16[16,4096]{1,0:T(8,128)(2,1)S(1)} %slice.50.near_got_ref), custom_call_target="tpu_custom_call" | custom-call | tf_op jit(solution)/shard_map/finish/pallas_call | solution.py:39
  (22 shorter events, 0.2 us)
Async XLA Ops:
  2.4 7.2 %collective-permute-start.1 = (bf16[2,320,128]{2,1,0:T(8,128)(2,1)S(1)}, bf16[2,320,128]{2,1,0:T(8,128)(2,1)S(1)}, u32[]{:S(2)}, u32[]{:S(2)}) collective-permute-start(bf16[2,320,128]{2,1,0:T(8,128)(2,1)S(1)} %get-tuple-element.50), channel_id=1, source_target_pairs={{0,2},{1,3},{2,0},{3,1},{4,6},{5,7},{6,4},{7,5},{8,10},{9,11},{10,... | collective-permute-start | bytes 491528 | tf_op jit(solution)/shard_map/ppermute | solution.py:369
  5.5 2.6 %collective-permute-start = (bf16[320,128]{1,0:T(8,128)(2,1)S(1)}, bf16[320,128]{1,0:T(8,128)(2,1)S(1)}, u32[]{:S(2)}, u32[]{:S(2)}) collective-permute-start(bf16[320,128]{1,0:T(8,128)(2,1)S(1)} %get-tuple-element.48), channel_id=1, source_target_pairs={{0,1},{1,0},{2,3},{3,2},{4,5},{5,4},{6,7},{7,6},{8,9},{9,8},{10,11... | collective-permute-start | bytes 245768 | tf_op jit(solution)/shard_map/ppermute | solution.py:369
  5.5 10.3 %collective-permute-start.4 = (bf16[32,2048]{1,0:T(8,128)(2,1)S(1)}, bf16[32,2048]{1,0:T(8,128)(2,1)S(1)}, u32[]{:S(2)}, u32[]{:S(2)}) collective-permute-start(bf16[32,2048]{1,0:T(8,128)(2,1)S(1)} %get-tuple-element.64.refs_1_), channel_id=1, source_target_pairs={{0,8},{4,12},{8,0},{12,4},{1,9},{5,13},{9,1},{13,5},{2,10},{6,14},... | collective-permute-start | bytes 393224 | tf_op jit(solution)/shard_map/ppermute | solution.py:369
  8.1 7.8 %collective-permute-start.3 = (bf16[32,2048]{1,0:T(8,128)(2,1)S(1)}, bf16[32,2048]{1,0:T(8,128)(2,1)S(1)}, u32[]{:S(2)}, u32[]{:S(2)}) collective-permute-start(bf16[32,2048]{1,0:T(8,128)(2,1)S(1)} %get-tuple-element.64.refs_1_), channel_id=1, source_target_pairs={{0,4},{4,0},{8,12},{12,8},{1,5},{5,1},{9,13},{13,9},{2,6},{6,2},{1... | collective-permute-start | bytes 393224 | tf_op jit(solution)/shard_map/ppermute | solution.py:369
  9.7 1.3 %collective-permute-start.2 = (bf16[320,128]{1,0:T(8,128)(2,1)S(1)}, bf16[320,128]{1,0:T(8,128)(2,1)S(1)}, u32[]{:S(2)}, u32[]{:S(2)}) collective-permute-start(bf16[320,128]{1,0:T(8,128)(2,1)S(1)} %get-tuple-element.90), channel_id=1, source_target_pairs={{0,1},{1,0},{2,3},{3,2},{4,5},{5,4},{6,7},{7,6},{8,9},{9,8},{10,11... | collective-permute-start | bytes 245768 | tf_op jit(solution)/shard_map/ppermute | solution.py:369
  15.8 6.2 %collective-permute-start.5 = (bf16[16,2048]{1,0:T(8,128)(2,1)S(1)}, bf16[16,2048]{1,0:T(8,128)(2,1)S(1)}, u32[]{:S(2)}, u32[]{:S(2)}) collective-permute-start(bf16[16,2048]{1,0:T(8,128)(2,1)S(1)} %get-tuple-element.58), channel_id=1, source_target_pairs={{0,2},{1,3},{2,0},{3,1},{4,6},{5,7},{6,4},{7,5},{8,10},{9,11},{10,... | collective-permute-start | bytes 196616 | tf_op jit(solution)/shard_map/ppermute | solution.py:369
  17.6 4.4 %collective-permute-start.6 = (bf16[16,2048]{1,0:T(8,128)(2,1)S(1)}, bf16[16,2048]{1,0:T(8,128)(2,1)S(1)}, u32[]{:S(2)}, u32[]{:S(2)}) collective-permute-start(bf16[16,2048]{1,0:T(8,128)(2,1)S(1)} %get-tuple-element.59), channel_id=1, source_target_pairs={{0,1},{1,0},{2,3},{3,2},{4,5},{5,4},{6,7},{7,6},{8,9},{9,8},{10,11... | collective-permute-start | bytes 196616 | tf_op jit(solution)/shard_map/ppermute | solution.py:369
  17.6 4.4 %collective-permute-start.7 = (bf16[16,2048]{1,0:T(8,128)(2,1)S(1)}, bf16[16,2048]{1,0:T(8,128)(2,1)S(1)}, u32[]{:S(2)}, u32[]{:S(2)}) collective-permute-start(bf16[16,2048]{1,0:T(8,128)(2,1)S(1)} %get-tuple-element.60), channel_id=1, source_target_pairs={{0,3},{1,2},{2,1},{3,0},{4,7},{5,6},{6,5},{7,4},{8,11},{9,10},{10,... | collective-permute-start | bytes 196616 | tf_op jit(solution)/shard_map/ppermute | solution.py:369
  18.0 7.7 %collective-permute-start.9 = (bf16[32,2048]{1,0:T(8,128)(2,1)S(1)}, bf16[32,2048]{1,0:T(8,128)(2,1)S(1)}, u32[]{:S(2)}, u32[]{:S(2)}) collective-permute-start(bf16[32,2048]{1,0:T(8,128)(2,1)S(1)} %collective-permute-done.4.refs_3_), channel_id=1, source_target_pairs={{0,4},{4,0},{8,12},{12,8},{1,5},{5,1},{9,13},{13,9},{2,6},{6,2},{1... | collective-permute-start | bytes 393224 | tf_op jit(solution)/shard_map/ppermute | solution.py:369
  25.6 3.5 %collective-permute-start.8 = (bf16[32,4096]{1,0:T(8,128)(2,1)S(1)}, bf16[32,4096]{1,0:T(8,128)(2,1)S(1)}, u32[]{:S(2)}, u32[]{:S(2)}) collective-permute-start(bf16[32,4096]{1,0:T(8,128)(2,1)S(1)} %get-tuple-element.63), channel_id=1, source_target_pairs={{0,1},{1,0},{2,3},{3,2},{4,5},{5,4},{6,7},{7,6},{8,9},{9,8},{10,11... | collective-permute-start | bytes 786440 | tf_op jit(solution)/shard_map/ppermute | solution.py:369
  26.1 2.8 %collective-permute-start.10 = (bf16[32,128]{1,0:T(8,128)(2,1)S(1)}, bf16[32,128]{1,0:T(8,128)(2,1)S(1)}, u32[]{:S(2)}, u32[]{:S(2)}) collective-permute-start(bf16[32,128]{1,0:T(8,128)(2,1)S(1)} %get-tuple-element.69), channel_id=1, source_target_pairs={{0,1},{1,0},{2,3},{3,2},{4,5},{5,4},{6,7},{7,6},{8,9},{9,8},{10,11... | collective-permute-start | bytes 24584 | tf_op jit(solution)/shard_map/ppermute | solution.py:369
  28.8 6.9 %collective-permute-start.15 = (bf16[4,64,512]{2,1,0:T(8,128)(2,1)S(1)}, bf16[4,64,512]{2,1,0:T(8,128)(2,1)S(1)}, u32[]{:S(2)}, u32[]{:S(2)}) collective-permute-start(bf16[4,64,512]{2,1,0:T(8,128)(2,1)S(1)} %get-tuple-element.84.refs_8_), channel_id=1, source_target_pairs={{0,1},{1,0},{2,3},{3,2},{4,5},{5,4},{6,7},{7,6},{8,9},{9,8},{10,11... | collective-permute-start | bytes 786440 | tf_op jit(solution)/shard_map/ppermute | solution.py:369
  29.2 6.0 %collective-permute-start.11 = (bf16[16,4352]{1,0:T(8,128)(2,1)S(1)}, bf16[16,4352]{1,0:T(8,128)(2,1)S(1)}, u32[]{:S(2)}, u32[]{:S(2)}) collective-permute-start(bf16[16,4352]{1,0:T(8,128)(2,1)S(1)} %fusion), channel_id=1, source_target_pairs={{0,2},{1,3},{2,0},{3,1},{4,6},{5,7},{6,4},{7,5},{8,10},{9,11},{10,... | collective-permute-start | bytes 417800 | tf_op jit(solution)/shard_map/ppermute | solution.py:369
  32.9 2.8 %collective-permute-start.13 = (bf16[32,2048]{1,0:T(8,128)(2,1)S(1)}, bf16[32,2048]{1,0:T(8,128)(2,1)S(1)}, u32[]{:S(2)}, u32[]{:S(2)}) collective-permute-start(bf16[32,2048]{1,0:T(8,128)(2,1)S(1)} %get-tuple-element.82), channel_id=1, source_target_pairs={{0,1},{1,0},{2,3},{3,2},{4,5},{5,4},{6,7},{7,6},{8,9},{9,8},{10,11... | collective-permute-start | bytes 393224 | tf_op jit(solution)/shard_map/ppermute | solution.py:369
  33.2 2.1 %collective-permute-start.12 = (bf16[32,1024]{1,0:T(8,128)(2,1)S(1)}, bf16[32,1024]{1,0:T(8,128)(2,1)S(1)}, u32[]{:S(2)}, u32[]{:S(2)}) collective-permute-start(bf16[32,1024]{1,0:T(8,128)(2,1)S(1)} %get-tuple-element.81), channel_id=1, source_target_pairs={{0,1},{1,0},{2,3},{3,2},{4,5},{5,4},{6,7},{7,6},{8,9},{9,8},{10,11... | collective-permute-start | bytes 196616 | tf_op jit(solution)/shard_map/ppermute | solution.py:369
  34.4 1.3 %collective-permute-start.14 = (bf16[32,1024]{1,0:T(8,128)(2,1)S(1)}, bf16[32,1024]{1,0:T(8,128)(2,1)S(1)}, u32[]{:S(2)}, u32[]{:S(2)}) collective-permute-start(bf16[32,1024]{1,0:T(8,128)(2,1)S(1)} %get-tuple-element.83), channel_id=1, source_target_pairs={{0,1},{1,0},{2,3},{3,2},{4,5},{5,4},{6,7},{7,6},{8,9},{9,8},{10,11... | collective-permute-start | bytes 196616 | tf_op jit(solution)/shard_map/ppermute | solution.py:369
  36.1 5.7 %collective-permute-start.16 = (bf16[16,4096]{1,0:T(8,128)(2,1)S(1)}, bf16[16,4096]{1,0:T(8,128)(2,1)S(1)}, u32[]{:S(2)}, u32[]{:S(2)}) collective-permute-start(bf16[16,4096]{1,0:T(8,128)(2,1)S(1)} %get-tuple-element.85), channel_id=1, source_target_pairs={{0,2},{1,3},{2,0},{3,1},{4,6},{5,7},{6,4},{7,5},{8,10},{9,11},{10,... | collective-permute-start | bytes 393224 | tf_op jit(solution)/shard_map/ppermute | solution.py:369

commit v5 on v4

--- a/solution.py
+++ b/solution.py
@@ -74,20 +74,29 @@
     return copies
 
 
-def pack_kernel(query_hbm, new_hbm, cache_hbm, down_hbm, up_hbm, *refs, parts, own, steps):
-    *block_refs, cache_ref, factor_ref, query_ref, new_ref, up_ref, sem = refs
+def stage_kernel(after_ref, cache_hbm, cache_ref, sem, *, own):
+    slots = pl.ds(0, cache_hbm.shape[3])
+    copies = [
+        pltpu.make_async_copy(
+            cache_hbm.at[r, part], cache_ref.at[r, part, :, slots], sem.at[r, part]
+        )
+        for r in range(own)
+        for part in range(2)
+    ]
+    for copy in copies:
+        copy.start()
+    for copy in copies:
+        copy.wait()
+
+
+def pack_kernel(query_hbm, new_hbm, down_hbm, up_hbm, *refs, parts, own, steps):
+    *block_refs, factor_ref, query_ref, new_ref, up_ref, sem = refs
     slot, depth = down_hbm.shape
     pairs = [
         (query_hbm, query_ref),
         (new_hbm, new_ref),
         (up_hbm, up_ref),
         (down_hbm, factor_ref.at[pl.ds(0, slot)]),
-    ]
-    slots = pl.ds(0, cache_hbm.shape[3])
-    pairs += [
-        (cache_hbm.at[r, part], cache_ref.at[r, part, :, slots])
-        for r in range(own)
-        for part in range(2)
     ]
     copies = [pltpu.make_async_copy(*pair, sem.at[i]) for i, pair in enumerate(pairs)]
     for copy in copies:
@@ -308,6 +317,25 @@
             keep_ref[...] = low
 
 
+def handoff_kernel(send_ref, *refs, parts, slot):
+    attended_refs, refs = refs[:parts], refs[parts:]
+    *factor_refs, keep_ref, up_ref, handoff_ref, down_ref = refs
+    collect_kernel(None, *factor_refs, down_ref, up_ref, slot=slot)
+    half, width = send_ref.shape
+    handoff_ref[:, :width] = send_ref[...]
+    cut = up_ref.shape[2]
+    for k in range(up_ref.shape[0]):
+        for j in range(RANK // half):
+            handoff_ref[:, width : width + cut] = up_ref[k, j * half : (j + 1) * half, :]
+            width += cut
+    rows = [
+        jnp.concatenate([a[...] for a in attended_refs[i : i + parts // 2]], axis=0)
+        for i in (0, parts // 2)
+    ]
+    keep_ref[...] = dot_rows(rows[0], down_ref[...])
+    handoff_ref[:, width:] = jnp.concatenate(split(dot_rows(rows[1], down_ref[...])), axis=1)
+
+
 def fold_low(keep, got):
     return keep + got[:, :RANK].astype(F32) + got[:, RANK:].astype(F32)
 
@@ -316,7 +344,7 @@
     low_ref, low_got_ref, refs = refs[0], refs[1], refs[2:]
     keep_refs, refs = refs[:pieces], refs[pieces:]
     got_refs, refs = refs[:pieces], refs[pieces:]
-    up_refs, (own_ref, send_ref, extra_ref) = refs[:sets], refs[sets:]
+    *up_refs, own_ref, send_ref, extra_ref = refs
     me, place = lax.axis_index("tensor"), lax.axis_index("fsdp")
     half = low_ref.shape[0] // 2
     got = low_got_ref[...]
@@ -327,10 +355,22 @@
         both = dot(low, up_refs[0][...])
         extra_ref[...] = both[: 2 * half] + both[2 * half :]
     else:
-        cut = up_refs[0].shape[2]
-        for kt, up_ref in enumerate(up_refs):
-            for kf in range(up_ref.shape[0]):
-                both = dot(low, up_ref[kf])
+        spread, _, cut = up_refs[0].shape
+        for kt in range(sets):
+            for kf in range(spread):
+                if kt < len(up_refs) and len(up_refs[kt].shape) == 3:
+                    factor = up_refs[kt][kf]
+                else:
+                    tall = up_refs[kt].shape[0]
+                    first = extra_ref.shape[1] + kf * (RANK // tall) * cut
+                    factor = jnp.concatenate(
+                        [
+                            up_refs[kt][:, first + j * cut : first + (j + 1) * cut]
+                            for j in range(RANK // tall)
+                        ],
+                        axis=0,
+                    )
+                both = dot(low, factor)
                 column = (place ^ kf) * sets + ((me ^ kt) & (sets - 1))
                 start = pl.multiple_of(column * cut, cut)
                 extra_ref[:, pl.ds(start, cut)] = both[: 2 * half] + both[2 * half :]
@@ -372,22 +412,26 @@
 
     block = shape_of((own * heads * steps + pieces * tall, HEAD_DIM), BF16)
     per = depth // cut
-    *blocks, cross, cache, factors = call(
+    *blocks, cross, factors = call(
         functools.partial(pack_kernel, parts=parts, own=own, steps=steps),
         "pack",
-        [(HBM, a) for a in (queries, new, cache, down.T, up)],
+        [(HBM, a) for a in (queries, new, down.T, up)],
         [block] * sets
-        + [
-            shape_of((sets,) + block.shape, BF16),
-            pltpu.VMEM(cache.shape[:3] + (cache.shape[3] + tall, HEAD_DIM), BF16),
-            shape_of((slot + RANK // per, depth), BF16),
-        ],
+        + [shape_of((sets,) + block.shape, BF16), shape_of((slot + RANK // per, depth), BF16)],
         [
             pltpu.VMEM(queries.shape, BF16),
             pltpu.VMEM(new.shape, BF16),
             pltpu.VMEM(up.shape, BF16),
-            pltpu.SemaphoreType.DMA((4 + 2 * own,)),
+            pltpu.SemaphoreType.DMA((4,)),
         ],
+    )
+    (cache,) = call(
+        functools.partial(stage_kernel, own=own),
+        "stage",
+        [(ANY, blocks[0]), (HBM, cache)],
+        [pltpu.VMEM(cache.shape[:3] + (cache.shape[3] + tall, HEAD_DIM), BF16)],
+        [pltpu.SemaphoreType.DMA((own, 2))],
+        cost=pl.CostEstimate(flops=0, bytes_accessed=2 * cache.size, transcendentals=0),
     )
     cross = swap(cross, "tensor", sets)
     blocks = blocks[:1] + [swap(blocks[k], "tensor", k) for k in range(1, sets)]
@@ -467,34 +511,52 @@
             keep, send = both[:half], jnp.concatenate(split(both[half:]), axis=1)
 
     keep, send, buffers = project(attended, weight, buffers, 0, spread, half)
-    far_keep, far_got = reduce(keep, send)
-
-    down_rows, ups = call(
-        functools.partial(collect_kernel, slot=slot),
-        "collect",
-        [(ANY, keep)] + [(VMEM, factors[k]) for k in range(spread)],
-        [shape_of((RANK, depth), BF16), shape_of((spread, RANK, cut), BF16)],
-    )
-    low_keep, low_send = call(
-        lower_kernel,
-        "lower",
-        [(VMEM, a) for a in (*attended, down_rows)],
-        [shape_of((sets * tall, RANK), F32), shape_of((sets * tall, 2 * RANK), BF16)],
-    )
-    low = reduce_low(low_keep, low_send)
     ordered = cut % HEAD_DIM != 0
-    if ordered:
-        ups = lax.all_gather(up, ("fsdp", "tensor"), axis=1, tiled=True)
-        ups = ups.reshape(RANK, spread, 2, wide)
-        top = lax.axis_index("tensor") // sets
-        ups = lax.dynamic_index_in_dim(ups, top, 2, keepdims=False)
-        up_sets = {0: ups.reshape(RANK, half_width)}
+    if sets == 2 and not ordered:
+        inner = (spread * RANK * cut) // (2 * tall)
+        low_keep, ups, handoff = call(
+            functools.partial(handoff_kernel, parts=parts, slot=slot),
+            "handoff",
+            [(VMEM, a) for a in (send, *attended, *[factors[k] for k in range(spread)])],
+            [
+                shape_of((2 * tall, RANK), F32),
+                shape_of((spread, RANK, cut), BF16),
+                shape_of((2 * tall, half_width + inner + 2 * RANK), BF16),
+            ],
+            [pltpu.VMEM((RANK, depth), BF16)],
+        )
+        handoff = swap(handoff, "tensor", 1)
+        far_keep, far_got = keep, handoff[:, :half_width]
+        low = fold_low(low_keep, handoff[:, half_width + inner :])
+        up_sets = {0: ups, 1: handoff}
     else:
-        up_sets = {0: ups}
-        bit = sets // 2
-        while bit:
-            up_sets |= {k ^ bit: swap(u, "tensor", bit) for k, u in list(up_sets.items())}
-            bit //= 2
+        far_keep, far_got = reduce(keep, send)
+
+        down_rows, ups = call(
+            functools.partial(collect_kernel, slot=slot),
+            "collect",
+            [(ANY, keep)] + [(VMEM, factors[k]) for k in range(spread)],
+            [shape_of((RANK, depth), BF16), shape_of((spread, RANK, cut), BF16)],
+        )
+        low_keep, low_send = call(
+            lower_kernel,
+            "lower",
+            [(VMEM, a) for a in (*attended, down_rows)],
+            [shape_of((sets * tall, RANK), F32), shape_of((sets * tall, 2 * RANK), BF16)],
+        )
+        low = reduce_low(low_keep, low_send)
+        if ordered:
+            ups = lax.all_gather(up, ("fsdp", "tensor"), axis=1, tiled=True)
+            ups = ups.reshape(RANK, spread, 2, wide)
+            top = lax.axis_index("tensor") // sets
+            ups = lax.dynamic_index_in_dim(ups, top, 2, keepdims=False)
+            up_sets = {0: ups.reshape(RANK, half_width)}
+        else:
+            up_sets = {0: ups}
+            bit = sets // 2
+            while bit:
+                up_sets |= {k ^ bit: swap(u, "tensor", bit) for k, u in list(up_sets.items())}
+                bit //= 2
 
     far = far_keep + far_got.astype(F32)
     low_parts = jnp.concatenate(split(low), axis=1)
@@ -516,7 +578,7 @@
 
     ups = [up_sets[k] for k in range(len(up_sets))]
     near_keep, near_send = call(
-        functools.partial(adapt_kernel, pieces=len(near), sets=len(ups), ordered=ordered),
+        functools.partial(adapt_kernel, pieces=len(near), sets=sets, ordered=ordered),
         "adapt",
         [(VMEM, a) for a in (low, low_got, *[k for k, _ in near], *[g for _, g in near], *ups)],
         [shape_of((tall, half_width), F32), shape_of((tall, half_width), BF16)],

time: 42.8 us -> 42 us (0.981)
  waiting for transfers between devices: 6.82 us -> 5.59 us
  Pallas kernels: 19.8 us -> 20.8 us
  starting transfers between devices: 15.5 us -> 14.9 us
    ppermute x17 -> x15, waiting for transfers between devices: 6.82 us -> 5.59 us  [shards(): lax.ppermute(x, axis, [(i, i ^ k) for i in range(lax.axis_size(axis))])]
    pallas_call x11, Pallas kernels: 19.8 us -> 20.8 us  [call(): pl.pallas_call(kernel, in_specs=list(specs), out_specs=[VMEM] * len(outs)...]
    ppermute x17 -> x15, starting transfers between devices: 15.5 us -> 14.9 us  [shards(): lax.ppermute(x, axis, [(i, i ^ k) for i in range(lax.axis_size(axis))])]
  transfers between devices with their start and end apart: 17 -> 15, of which waited for: 4 -> 3; matrix products, arithmetic and copies ran while one was open for 1% -> 0% of each run, Pallas kernels for 38% -> 43%
where the time goes in v5:
time: 42 us; the launch traced here: 41.8 us
  Pallas kernels  20.8 us (50%)
  starting transfers between devices  14.9 us (35%)
  waiting for transfers between devices  5.59 us (13%)
    pallas_call x11, Pallas kernels, call(): pl.pallas_call(kernel, in_specs=list(specs), out_specs=[VMEM] * len(outs)...  20.8 us
    ppermute x15, starting transfers between devices, shards(): lax.ppermute(x, axis, [(i, i ^ k) for i in range(lax.axis_size(axis))])  14.9 us
    ppermute x15, waiting for transfers between devices, shards(): lax.ppermute(x, axis, [(i, i ^ k) for i in range(lax.axis_size(axis))])  5.59 us
  transfers between devices with their start and end apart: 15, of which 3 were waited for; matrix products, arithmetic and copies ran while one was open for 0% of the time, Pallas kernels for 43%

profile of v5, /device:TPU:0, one launch (start us, length us, event | category | flops | bytes accessed | tf_op | source)
XLA Modules:
  0.0 41.8 jit_solution(10685215579735021515)
XLA Ops:
  0.0 1.2 %pack.1 = (bf16[320,128]{1,0:T(8,128)(2,1)S(1)}, bf16[320,128]{1,0:T(8,128)(2,1)S(1)}, bf16[2,320,128]{2,1,0:T(8,128)(2,1)S(1)}, bf16[32,2048]{1,0:T(8,128)(2,1)S(1)}) custom-call(bf16[8,8,2048]{2,1,0:T(8,128)(2,1)} %query_hbm.1, bf16[8,8,512]{2,1,0:T(8,128)(2,1)} %new_hbm.1, bf16[16,2048]{1,0:T(8,128)(2,1)} %bitcast.5, bf16[64,512]{1,0:T(8,128)(2,1)} %up_hbm.1), custom_call_target="tpu_custom_call" | custom-call | tf_op jit(solution)/shard_map/pack/pallas_call | solution.py:39
  1.2 3.0 %collective-permute-start.1 = (bf16[2,320,128]{2,1,0:T(8,128)(2,1)S(1)}, bf16[2,320,128]{2,1,0:T(8,128)(2,1)S(1)}, u32[]{:S(2)}, u32[]{:S(2)}) collective-permute-start(bf16[2,320,128]{2,1,0:T(8,128)(2,1)S(1)} %get-tuple-element.48), channel_id=1, source_target_pairs={{0,2},{1,3},{2,0},{3,1},{4,6},{5,7},{6,4},{7,5},{8,10},{9,11},{10,... | collective-permute-start | bytes 491528 | tf_op jit(solution)/shard_map/ppermute | solution.py:409
  4.3 2.6 %collective-permute-start.4 = (bf16[32,2048]{1,0:T(8,128)(2,1)S(1)}, bf16[32,2048]{1,0:T(8,128)(2,1)S(1)}, u32[]{:S(2)}, u32[]{:S(2)}) collective-permute-start(bf16[32,2048]{1,0:T(8,128)(2,1)S(1)} %get-tuple-element.61.refs_4_), channel_id=1, source_target_pairs={{0,8},{4,12},{8,0},{12,4},{1,9},{5,13},{9,1},{13,5},{2,10},{6,14},... | collective-permute-start | bytes 393224 | tf_op jit(solution)/shard_map/ppermute | solution.py:409
  6.9 1.6 %collective-permute-start.3 = (bf16[32,2048]{1,0:T(8,128)(2,1)S(1)}, bf16[32,2048]{1,0:T(8,128)(2,1)S(1)}, u32[]{:S(2)}, u32[]{:S(2)}) collective-permute-start(bf16[32,2048]{1,0:T(8,128)(2,1)S(1)} %get-tuple-element.61.refs_4_), channel_id=1, source_target_pairs={{0,4},{4,0},{8,12},{12,8},{1,5},{5,1},{9,13},{13,9},{2,6},{6,2},{1... | collective-permute-start | bytes 393224 | tf_op jit(solution)/shard_map/ppermute | solution.py:409
  8.5 0.1 collective-permute-start.2
  8.6 2.2 %stage.1.refs_5_ = bf16[2,2,8,528,128]{4,3,2,1,0:T(8,128)(2,1)S(1)} custom-call(bf16[320,128]{1,0:T(8,128)(2,1)S(1)} %get-tuple-element.44.after_ref.refs_0_, bf16[2,2,8,512,128]{4,3,2,1,0:T(8,128)(2,1)} %cache_hbm.1), custom_call_target="tpu_custom_call" | custom-call | bytes 4194304 | tf_op jit(solution)/shard_map/stage/pallas_call | solution.py:39
  10.8 4.8 %attend.1 = (bf16[16,2048]{1,0:T(8,128)(2,1)S(1)}, bf16[16,2048]{1,0:T(8,128)(2,1)S(1)}, bf16[16,2048]{1,0:T(8,128)(2,1)S(1)}, bf16[16,2048]{1,0:T(8,128)(2,1)S(...) custom-call(s32[2]{0:T(128)} %length_hbm.1, ...), custom_call_target="tpu_custom_call", output_to_operand_aliasing={{5}: (6, {})} | custom-call | tf_op jit(solution)/shard_map/attend/pallas_call | solution.py:39
  15.6 1.8 %collective-permute-start.5 = (bf16[16,2048]{1,0:T(8,128)(2,1)S(1)}, bf16[16,2048]{1,0:T(8,128)(2,1)S(1)}, u32[]{:S(2)}, u32[]{:S(2)}) collective-permute-start(bf16[16,2048]{1,0:T(8,128)(2,1)S(1)} %get-tuple-element.55), channel_id=1, source_target_pairs={{0,2},{1,3},{2,0},{3,1},{4,6},{5,7},{6,4},{7,5},{8,10},{9,11},{10,... | collective-permute-start | bytes 196616 | tf_op jit(solution)/shard_map/ppermute | solution.py:409
  17.4 0.2 collective-permute-start.6
  17.6 0.2 collective-permute-start.7
  17.8 1.8 %collective-permute-start.8 = (bf16[32,2048]{1,0:T(8,128)(2,1)S(1)}, bf16[32,2048]{1,0:T(8,128)(2,1)S(1)}, u32[]{:S(2)}, u32[]{:S(2)}) collective-permute-start(bf16[32,2048]{1,0:T(8,128)(2,1)S(1)} %collective-permute-done.4.refs_6_), channel_id=1, source_target_pairs={{0,4},{4,0},{8,12},{12,8},{1,5},{5,1},{9,13},{13,9},{2,6},{6,2},{1... | collective-permute-start | bytes 393224 | tf_op jit(solution)/shard_map/ppermute | solution.py:409
  19.6 2.2 %fetch.1.refs_5_ = bf16[1,2048,1024]{2,1,0:T(8,128)(2,1)S(1)} custom-call(bf16[16,2048]{1,0:T(8,128)(2,1)S(1)} %get-tuple-element.69.after_ref.refs_0_, bf16[2048,8192]{1,0:T(8,128)(2,1)} %refs_5_.3), custom_call_target="tpu_custom_call" | custom-call | bytes 4194304 | tf_op jit(solution)/shard_map/fetch/pallas_call | solution.py:39
  21.8 3.5 %project.4 = (f32[32,4096]{1,0:T(8,128)S(1)}, bf16[32,4096]{1,0:T(8,128)(2,1)S(1)}, bf16[2,2048,1024]{2,1,0:T(8,128)(2,1)S(1)}) custom-call(bf16[16,2048]{1,0:T(8,128)(2,1)S(1)} %get-tuple-element.69.after_ref.refs_0_, bf16[16,2048]{1,0:T(8,128)(2,1)S(1)} %collective-permute-done.5.refs_1_, bf16[16,2048]{1,0:T(8,128)(2,1)S(1)} %collective-permute-done.6.refs_2_, ...), custom_call_target="tpu_custom_call" | custom-call | flops 1073741824 | bytes 16777216 | tf_op jit(solution)/shard_map/project/pallas_call | solution.py:39
  25.4 0.4 handoff.1
  25.7 0.3 collective-permute-start.9
  26.1 2.2 %project.5 = (f32[32,1024]{1,0:T(8,128)S(1)}, bf16[32,1024]{1,0:T(8,128)(2,1)S(1)}, bf16[1,2048,1024]{2,1,0:T(8,128)(2,1)S(1)}) custom-call(bf16[16,2048]{1,0:T(8,128)(2,1)S(1)} %get-tuple-element.69.after_ref.refs_0_, bf16[16,2048]{1,0:T(8,128)(2,1)S(1)} %collective-permute-done.5.refs_1_, bf16[16,2048]{1,0:T(8,128)(2,1)S(1)} %collective-permute-done.6.refs_2_, ...), custom_call_target="tpu_custom_call" | custom-call | flops 268435456 | bytes 4194304 | tf_op jit(solution)/shard_map/project/pallas_call | solution.py:39
  28.3 0.1 convert_add_fusion
  28.4 0.1 subtract_convert_fusion
  28.4 0.1 fusion.1
  28.5 0.1 fusion
  28.6 1.3 %collective-permute-start.10 = (bf16[16,4352]{1,0:T(8,128)(2,1)S(1)}, bf16[16,4352]{1,0:T(8,128)(2,1)S(1)}, u32[]{:S(2)}, u32[]{:S(2)}) collective-permute-start(bf16[16,4352]{1,0:T(8,128)(2,1)S(1)} %fusion), channel_id=1, source_target_pairs={{0,2},{1,3},{2,0},{3,1},{4,6},{5,7},{6,4},{7,5},{8,10},{9,11},{10,... | collective-permute-start | bytes 417800 | tf_op jit(solution)/shard_map/ppermute | solution.py:409
  29.9 2.2 %project.6 = (f32[32,2048]{1,0:T(8,128)S(1)}, bf16[32,2048]{1,0:T(8,128)(2,1)S(1)}, bf16[1,2048,1024]{2,1,0:T(8,128)(2,1)S(1)}) custom-call(bf16[16,2048]{1,0:T(8,128)(2,1)S(1)} %get-tuple-element.69.after_ref.refs_0_, bf16[16,2048]{1,0:T(8,128)(2,1)S(1)} %collective-permute-done.5.refs_1_, bf16[16,2048]{1,0:T(8,128)(2,1)S(1)} %collective-permute-done.6.refs_2_, ...), custom_call_target="tpu_custom_call" | custom-call | flops 536870912 | bytes 8388608 | tf_op jit(solution)/shard_map/project/pallas_call | solution.py:39
  32.1 0.2 collective-permute-start.12
  32.4 0.3 collective-permute-start.11
  32.7 0.9 %project.7 = (f32[32,1024]{1,0:T(8,128)S(1)}, bf16[32,1024]{1,0:T(8,128)(2,1)S(1)}) custom-call(bf16[16,2048]{1,0:T(8,128)(2,1)S(1)} %get-tuple-element.69.after_ref.refs_0_, bf16[16,2048]{1,0:T(8,128)(2,1)S(1)} %collective-permute-done.5.refs_1_, bf16[16,2048]{1,0:T(8,128)(2,1)S(1)} %collective-permute-done.6.refs_2_, ...), custom_call_target="tpu_custom_call" | custom-call | flops 268435456 | bytes 4194304 | tf_op jit(solution)/shard_map/project/pallas_call | solution.py:39
  33.6 0.2 collective-permute-start.13
  33.8 0.6 %collective-permute-done.10 = bf16[16,4352]{1,0:T(8,128)(2,1)S(1)} collective-permute-done((bf16[16,4352]{1,0:T(8,128)(2,1)S(1)}, bf16[16,4352]{1,0:T(8,128)(2,1)S(1)}, u32[]{:S(2)}, u32[]{:S(2)}) %collective-permute-start.10) | collective-permute-done | bytes 139296 | tf_op jit(solution)/shard_map/ppermute | solution.py:409
  34.4 0.5 %collective-permute-done.13.refs_7_ = bf16[32,1024]{1,0:T(8,128)(2,1)S(1)} collective-permute-done((bf16[32,1024]{1,0:T(8,128)(2,1)S(1)}, bf16[32,1024]{1,0:T(8,128)(2,1)S(1)}, u32[]{:S(2)}, u32[]{:S(2)}) %collective-permute-start.13) | collective-permute-done | bytes 65568 | tf_op jit(solution)/shard_map/ppermute | solution.py:409
  34.9 0.4 adapt.1
  35.3 1.1 %collective-permute-start.14 = (bf16[16,4096]{1,0:T(8,128)(2,1)S(1)}, bf16[16,4096]{1,0:T(8,128)(2,1)S(1)}, u32[]{:S(2)}, u32[]{:S(2)}) collective-permute-start(bf16[16,4096]{1,0:T(8,128)(2,1)S(1)} %get-tuple-element.81), channel_id=1, source_target_pairs={{0,2},{1,3},{2,0},{3,1},{4,6},{5,7},{6,4},{7,5},{8,10},{9,11},{10,... | collective-permute-start | bytes 393224 | tf_op jit(solution)/shard_map/ppermute | solution.py:409
  36.5 4.5 %collective-permute-done.14.far_got_ref = bf16[16,4096]{1,0:T(8,128)(2,1)S(1)} collective-permute-done((bf16[16,4096]{1,0:T(8,128)(2,1)S(1)}, bf16[16,4096]{1,0:T(8,128)(2,1)S(1)}, u32[]{:S(2)}, u32[]{:S(2)}) %collective-permute-start.14) | collective-permute-done | bytes 131104 | tf_op jit(solution)/shard_map/ppermute | solution.py:409
  40.9 0.8 %finish.1 = bf16[8,2,8192]{2,1,0:T(2,128)(2,1)} custom-call(f32[16,4096]{1,0:T(8,128)S(1)} %slice.51.far_ref, bf16[16,4096]{1,0:T(8,128)(2,1)S(1)} %collective-permute-done.14.far_got_ref, f32[16,4096]{1,0:T(8,128)S(1)} %get-tuple-element.82.near_ref, bf16[16,4096]{1,0:T(8,128)(2,1)S(1)} %slice.58.near_got_ref), custom_call_target="tpu_custom_call" | custom-call | tf_op jit(solution)/shard_map/finish/pallas_call | solution.py:39
  (18 shorter events, 0.1 us)
Async XLA Ops:
  1.2 7.2 %collective-permute-start.1 = (bf16[2,320,128]{2,1,0:T(8,128)(2,1)S(1)}, bf16[2,320,128]{2,1,0:T(8,128)(2,1)S(1)}, u32[]{:S(2)}, u32[]{:S(2)}) collective-permute-start(bf16[2,320,128]{2,1,0:T(8,128)(2,1)S(1)} %get-tuple-element.48), channel_id=1, source_target_pairs={{0,2},{1,3},{2,0},{3,1},{4,6},{5,7},{6,4},{7,5},{8,10},{9,11},{10,... | collective-permute-start | bytes 491528 | tf_op jit(solution)/shard_map/ppermute | solution.py:409
  4.3 2.6 %collective-permute-start = (bf16[320,128]{1,0:T(8,128)(2,1)S(1)}, bf16[320,128]{1,0:T(8,128)(2,1)S(1)}, u32[]{:S(2)}, u32[]{:S(2)}) collective-permute-start(bf16[320,128]{1,0:T(8,128)(2,1)S(1)} %get-tuple-element.46), channel_id=1, source_target_pairs={{0,1},{1,0},{2,3},{3,2},{4,5},{5,4},{6,7},{7,6},{8,9},{9,8},{10,11... | collective-permute-start | bytes 245768 | tf_op jit(solution)/shard_map/ppermute | solution.py:409
  4.3 11.3 %collective-permute-start.4 = (bf16[32,2048]{1,0:T(8,128)(2,1)S(1)}, bf16[32,2048]{1,0:T(8,128)(2,1)S(1)}, u32[]{:S(2)}, u32[]{:S(2)}) collective-permute-start(bf16[32,2048]{1,0:T(8,128)(2,1)S(1)} %get-tuple-element.61.refs_4_), channel_id=1, source_target_pairs={{0,8},{4,12},{8,0},{12,4},{1,9},{5,13},{9,1},{13,5},{2,10},{6,14},... | collective-permute-start | bytes 393224 | tf_op jit(solution)/shard_map/ppermute | solution.py:409
  6.9 8.7 %collective-permute-start.3 = (bf16[32,2048]{1,0:T(8,128)(2,1)S(1)}, bf16[32,2048]{1,0:T(8,128)(2,1)S(1)}, u32[]{:S(2)}, u32[]{:S(2)}) collective-permute-start(bf16[32,2048]{1,0:T(8,128)(2,1)S(1)} %get-tuple-element.61.refs_4_), channel_id=1, source_target_pairs={{0,4},{4,0},{8,12},{12,8},{1,5},{5,1},{9,13},{13,9},{2,6},{6,2},{1... | collective-permute-start | bytes 393224 | tf_op jit(solution)/shard_map/ppermute | solution.py:409
  8.5 2.3 %collective-permute-start.2 = (bf16[320,128]{1,0:T(8,128)(2,1)S(1)}, bf16[320,128]{1,0:T(8,128)(2,1)S(1)}, u32[]{:S(2)}, u32[]{:S(2)}) collective-permute-start(bf16[320,128]{1,0:T(8,128)(2,1)S(1)} %get-tuple-element.86), channel_id=1, source_target_pairs={{0,1},{1,0},{2,3},{3,2},{4,5},{5,4},{6,7},{7,6},{8,9},{9,8},{10,11... | collective-permute-start | bytes 245768 | tf_op jit(solution)/shard_map/ppermute | solution.py:409
  15.6 6.2 %collective-permute-start.5 = (bf16[16,2048]{1,0:T(8,128)(2,1)S(1)}, bf16[16,2048]{1,0:T(8,128)(2,1)S(1)}, u32[]{:S(2)}, u32[]{:S(2)}) collective-permute-start(bf16[16,2048]{1,0:T(8,128)(2,1)S(1)} %get-tuple-element.55), channel_id=1, source_target_pairs={{0,2},{1,3},{2,0},{3,1},{4,6},{5,7},{6,4},{7,5},{8,10},{9,11},{10,... | collective-permute-start | bytes 196616 | tf_op jit(solution)/shard_map/ppermute | solution.py:409
  17.4 4.4 %collective-permute-start.6 = (bf16[16,2048]{1,0:T(8,128)(2,1)S(1)}, bf16[16,2048]{1,0:T(8,128)(2,1)S(1)}, u32[]{:S(2)}, u32[]{:S(2)}) collective-permute-start(bf16[16,2048]{1,0:T(8,128)(2,1)S(1)} %get-tuple-element.56), channel_id=1, source_target_pairs={{0,1},{1,0},{2,3},{3,2},{4,5},{5,4},{6,7},{7,6},{8,9},{9,8},{10,11... | collective-permute-start | bytes 196616 | tf_op jit(solution)/shard_map/ppermute | solution.py:409
  17.6 4.2 %collective-permute-start.7 = (bf16[16,2048]{1,0:T(8,128)(2,1)S(1)}, bf16[16,2048]{1,0:T(8,128)(2,1)S(1)}, u32[]{:S(2)}, u32[]{:S(2)}) collective-permute-start(bf16[16,2048]{1,0:T(8,128)(2,1)S(1)} %get-tuple-element.57), channel_id=1, source_target_pairs={{0,3},{1,2},{2,1},{3,0},{4,7},{5,6},{6,5},{7,4},{8,11},{9,10},{10,... | collective-permute-start | bytes 196616 | tf_op jit(solution)/shard_map/ppermute | solution.py:409
  17.8 7.6 %collective-permute-start.8 = (bf16[32,2048]{1,0:T(8,128)(2,1)S(1)}, bf16[32,2048]{1,0:T(8,128)(2,1)S(1)}, u32[]{:S(2)}, u32[]{:S(2)}) collective-permute-start(bf16[32,2048]{1,0:T(8,128)(2,1)S(1)} %collective-permute-done.4.refs_6_), channel_id=1, source_target_pairs={{0,4},{4,0},{8,12},{12,8},{1,5},{5,1},{9,13},{13,9},{2,6},{6,2},{1... | collective-permute-start | bytes 393224 | tf_op jit(solution)/shard_map/ppermute | solution.py:409
  25.7 2.5 %collective-permute-start.9 = (bf16[32,8320]{1,0:T(8,128)(2,1)S(1)}, bf16[32,8320]{1,0:T(8,128)(2,1)S(1)}, u32[]{:S(2)}, u32[]{:S(2)}) collective-permute-start(bf16[32,8320]{1,0:T(8,128)(2,1)S(1)} %get-tuple-element.64), channel_id=1, source_target_pairs={{0,1},{1,0},{2,3},{3,2},{4,5},{5,4},{6,7},{7,6},{8,9},{9,8},{10,11... | collective-permute-start | bytes 1597448 | tf_op jit(solution)/shard_map/ppermute | solution.py:409
  28.6 5.8 %collective-permute-start.10 = (bf16[16,4352]{1,0:T(8,128)(2,1)S(1)}, bf16[16,4352]{1,0:T(8,128)(2,1)S(1)}, u32[]{:S(2)}, u32[]{:S(2)}) collective-permute-start(bf16[16,4352]{1,0:T(8,128)(2,1)S(1)} %fusion), channel_id=1, source_target_pairs={{0,2},{1,3},{2,0},{3,1},{4,6},{5,7},{6,4},{7,5},{8,10},{9,11},{10,... | collective-permute-start | bytes 417800 | tf_op jit(solution)/shard_map/ppermute | solution.py:409
  32.1 2.8 %collective-permute-start.12 = (bf16[32,2048]{1,0:T(8,128)(2,1)S(1)}, bf16[32,2048]{1,0:T(8,128)(2,1)S(1)}, u32[]{:S(2)}, u32[]{:S(2)}) collective-permute-start(bf16[32,2048]{1,0:T(8,128)(2,1)S(1)} %get-tuple-element.78), channel_id=1, source_target_pairs={{0,1},{1,0},{2,3},{3,2},{4,5},{5,4},{6,7},{7,6},{8,9},{9,8},{10,11... | collective-permute-start | bytes 393224 | tf_op jit(solution)/shard_map/ppermute | solution.py:409
  32.4 2.1 %collective-permute-start.11 = (bf16[32,1024]{1,0:T(8,128)(2,1)S(1)}, bf16[32,1024]{1,0:T(8,128)(2,1)S(1)}, u32[]{:S(2)}, u32[]{:S(2)}) collective-permute-start(bf16[32,1024]{1,0:T(8,128)(2,1)S(1)} %get-tuple-element.77), channel_id=1, source_target_pairs={{0,1},{1,0},{2,3},{3,2},{4,5},{5,4},{6,7},{7,6},{8,9},{9,8},{10,11... | collective-permute-start | bytes 196616 | tf_op jit(solution)/shard_map/ppermute | solution.py:409
  33.6 1.3 %collective-permute-start.13 = (bf16[32,1024]{1,0:T(8,128)(2,1)S(1)}, bf16[32,1024]{1,0:T(8,128)(2,1)S(1)}, u32[]{:S(2)}, u32[]{:S(2)}) collective-permute-start(bf16[32,1024]{1,0:T(8,128)(2,1)S(1)} %get-tuple-element.79), channel_id=1, source_target_pairs={{0,1},{1,0},{2,3},{3,2},{4,5},{5,4},{6,7},{7,6},{8,9},{9,8},{10,11... | collective-permute-start | bytes 196616 | tf_op jit(solution)/shard_map/ppermute | solution.py:409
  35.3 5.7 %collective-permute-start.14 = (bf16[16,4096]{1,0:T(8,128)(2,1)S(1)}, bf16[16,4096]{1,0:T(8,128)(2,1)S(1)}, u32[]{:S(2)}, u32[]{:S(2)}) collective-permute-start(bf16[16,4096]{1,0:T(8,128)(2,1)S(1)} %get-tuple-element.81), channel_id=1, source_target_pairs={{0,2},{1,3},{2,0},{3,1},{4,6},{5,7},{6,4},{7,5},{8,10},{9,11},{10,... | collective-permute-start | bytes 393224 | tf_op jit(solution)/shard_map/ppermute | solution.py:409

commit v6 on v5

--- a/solution.py
+++ b/solution.py
@@ -210,7 +210,7 @@
             for h in range(GROUP):
                 head = summed * GROUP + h
                 attended_ref[
-                    head >> log2(heads), head & (heads - 1), r * steps : (r + 1) * steps, :
+                    head >> log2(heads), head & (heads - 1), pl.ds(r, steps, stride=own), :
                 ] = total[h * steps : (h + 1) * steps]
         return 0
 
@@ -383,6 +383,17 @@
         send_ref[:, lanes] = total[half:].astype(BF16)
 
 
+def join_kernel(keep_ref, low_keep_ref, handoff_ref, own_ref, message_ref, low_ref):
+    half, width = own_ref.shape
+    own_ref[...] = keep_ref[:half, :] + handoff_ref[:half, :width].astype(F32)
+    total = keep_ref[half:, :] + handoff_ref[half:, :width].astype(F32)
+    message_ref[:, :width] = total.astype(BF16)
+    low = fold_low(low_keep_ref[...], handoff_ref[:, handoff_ref.shape[1] - 2 * RANK :])
+    low_ref[...] = low
+    parts = jnp.concatenate(split(low), axis=1)
+    message_ref[:, width:] = jnp.concatenate([parts[half:], parts[:half]], axis=1)
+
+
 def finish_kernel(far_ref, far_got_ref, near_ref, near_got_ref, out_ref, *, own, steps, strips):
     top = lax.axis_index("tensor") >> (log2(lax.axis_size("tensor")) - 1)
     wide = near_ref.shape[1] // strips
@@ -391,8 +402,7 @@
             lanes = slice(i * wide, (i + 1) * wide)
             total = (keep_ref[:, lanes] + got_ref[:, lanes].astype(F32)).astype(BF16)
             start = pl.multiple_of((2 * i + half) * wide, wide)
-            for r in range(own):
-                out_ref[:, r, pl.ds(start, wide)] = total[r * steps : (r + 1) * steps]
+            out_ref[:, :, pl.ds(start, wide)] = total.reshape(steps, own, wide)
 
 
 def shards(queries, cache, new, lengths, weight, down, up):
@@ -434,6 +444,7 @@
         cost=pl.CostEstimate(flops=0, bytes_accessed=2 * cache.size, transcendentals=0),
     )
     cross = swap(cross, "tensor", sets)
+    cross, cache = lax.optimization_barrier((cross, cache))
     blocks = blocks[:1] + [swap(blocks[k], "tensor", k) for k in range(1, sets)]
     blocks += [cross[0]] + [swap(cross[k], "tensor", k) for k in range(1, sets)]
     factors = {0: factors}
@@ -441,7 +452,6 @@
     while bit > 1:
         factors |= {k ^ bit: swap(v, "fsdp", bit) for k, v in list(factors.items())}
         bit //= 2
-    near_factors, blocks[1] = lax.optimization_barrier((factors[0], blocks[1]))
 
     half, quarter = spread // 2, spread // 4
     early = half + quarter
@@ -480,9 +490,8 @@
             )[0],
         )
     ]
-    factors[1] = swap(near_factors, "fsdp", 1)
     attended, factors = lax.optimization_barrier((list(attended), factors))
-    factors |= {k ^ 1: swap(v, "fsdp", 1) for k, v in list(factors.items()) if k > 1}
+    factors |= {k ^ 1: swap(v, "fsdp", 1) for k, v in list(factors.items())}
     got = {k: swap(attended[k], "tensor", k) for k in range(parts - 1, 0, -1)}
     attended = [attended[0]] + [got[k] for k in range(1, parts)]
 
@@ -526,8 +535,16 @@
             [pltpu.VMEM((RANK, depth), BF16)],
         )
         handoff = swap(handoff, "tensor", 1)
-        far_keep, far_got = keep, handoff[:, :half_width]
-        low = fold_low(low_keep, handoff[:, half_width + inner :])
+        far, message, low = call(
+            join_kernel,
+            "join",
+            [(VMEM, a) for a in (keep, low_keep, handoff)],
+            [
+                shape_of((tall, half_width), F32),
+                shape_of((tall, half_width + 4 * RANK), BF16),
+                shape_of((2 * tall, RANK), F32),
+            ],
+        )
         up_sets = {0: ups, 1: handoff}
     else:
         far_keep, far_got = reduce(keep, send)
@@ -557,10 +574,11 @@
             while bit:
                 up_sets |= {k ^ bit: swap(u, "tensor", bit) for k, u in list(up_sets.items())}
                 bit //= 2
-
-    far = far_keep + far_got.astype(F32)
-    low_parts = jnp.concatenate(split(low), axis=1)
-    message = jnp.concatenate([far[tall:].astype(BF16), low_parts[tall:], low_parts[:tall]], axis=1)
+        far = far_keep + far_got.astype(F32)
+        low_parts = jnp.concatenate(split(low), axis=1)
+        message = jnp.concatenate([far[tall:].astype(BF16), low_parts[tall:], low_parts[:tall]], axis=1)
+        far = far[:tall]
+
     near = []
 
     def add_near(low, high, ahead):
@@ -589,7 +607,7 @@
     return call(
         functools.partial(finish_kernel, own=own, steps=steps, strips=spread),
         "finish",
-        [(VMEM, a) for a in (far[:tall], far_got, near_keep, near_got)],
+        [(VMEM, a) for a in (far, far_got, near_keep, near_got)],
         [shape_of((steps, own, weight.shape[1]), BF16)],
     )[0]
 

time: 42 us -> 41.7 us (level)
  starting transfers between devices: 14.9 us -> 13.4 us
  waiting for transfers between devices: 5.59 us -> 7.02 us
    ppermute x15, starting transfers between devices: 14.9 us -> 13.4 us  [shards(): lax.ppermute(x, axis, [(i, i ^ k) for i in range(lax.axis_size(axis))])]
    ppermute x15, waiting for transfers between devices: 5.59 us -> 7.02 us  [shards(): lax.ppermute(x, axis, [(i, i ^ k) for i in range(lax.axis_size(axis))])]
    pallas_call x11 -> x12, Pallas kernels: 20.8 us -> 20.9 us  [call(): pl.pallas_call(kernel, in_specs=list(specs), out_specs=[VMEM] * len(outs)...]
  transfers between devices with their start and end apart: 15 -> 15, of which waited for: 3 -> 4; matrix products, arithmetic and copies ran while one was open for 0% -> 0% of each run, Pallas kernels for 43% -> 43%
where the time goes in v6:
time: 41.7 us; the launch traced here: 41.5 us
  Pallas kernels  20.9 us (50%)
  starting transfers between devices  13.4 us (32%)
  waiting for transfers between devices  7.02 us (17%)
    pallas_call x12, Pallas kernels, call(): pl.pallas_call(kernel, in_specs=list(specs), out_specs=[VMEM] * len(outs)...  20.9 us
    ppermute x15, starting transfers between devices, shards(): lax.ppermute(x, axis, [(i, i ^ k) for i in range(lax.axis_size(axis))])  13.4 us
    ppermute x15, waiting for transfers between devices, shards(): lax.ppermute(x, axis, [(i, i ^ k) for i in range(lax.axis_size(axis))])  7.02 us
  transfers between devices with their start and end apart: 15, of which 4 were waited for; matrix products, arithmetic and copies ran while one was open for 0% of the time, Pallas kernels for 43%

profile of v6, /device:TPU:0, one launch (start us, length us, event | category | flops | bytes accessed | tf_op | source)
XLA Modules:
  0.0 41.5 jit_solution(2981021465709950747)
XLA Ops:
  0.0 1.2 %pack.1 = (bf16[320,128]{1,0:T(8,128)(2,1)S(1)}, bf16[320,128]{1,0:T(8,128)(2,1)S(1)}, bf16[2,320,128]{2,1,0:T(8,128)(2,1)S(1)}, bf16[32,2048]{1,0:T(8,128)(2,1)S(1)}) custom-call(bf16[8,8,2048]{2,1,0:T(8,128)(2,1)} %query_hbm.1, bf16[8,8,512]{2,1,0:T(8,128)(2,1)} %new_hbm.1, bf16[16,2048]{1,0:T(8,128)(2,1)} %bitcast.5, bf16[64,512]{1,0:T(8,128)(2,1)} %up_hbm.1), custom_call_target="tpu_custom_call" | custom-call | tf_op jit(solution)/shard_map/pack/pallas_call | solution.py:39
  1.2 3.0 %collective-permute-start.1 = (bf16[2,320,128]{2,1,0:T(8,128)(2,1)S(1)}, bf16[2,320,128]{2,1,0:T(8,128)(2,1)S(1)}, u32[]{:S(2)}, u32[]{:S(2)}) collective-permute-start(bf16[2,320,128]{2,1,0:T(8,128)(2,1)S(1)} %get-tuple-element.48), channel_id=1, source_target_pairs={{0,2},{1,3},{2,0},{3,1},{4,6},{5,7},{6,4},{7,5},{8,10},{9,11},{10,... | collective-permute-start | bytes 491528 | tf_op jit(solution)/shard_map/ppermute | solution.py:419
  4.3 2.6 %collective-permute-start.3 = (bf16[32,2048]{1,0:T(8,128)(2,1)S(1)}, bf16[32,2048]{1,0:T(8,128)(2,1)S(1)}, u32[]{:S(2)}, u32[]{:S(2)}) collective-permute-start(bf16[32,2048]{1,0:T(8,128)(2,1)S(1)} %get-tuple-element.63.refs_4_), channel_id=1, source_target_pairs={{0,8},{4,12},{8,0},{12,4},{1,9},{5,13},{9,1},{13,5},{2,10},{6,14},... | collective-permute-start | bytes 393224 | tf_op jit(solution)/shard_map/ppermute | solution.py:419
  6.9 2.2 %stage.1.refs_5_ = bf16[2,2,8,528,128]{4,3,2,1,0:T(8,128)(2,1)S(1)} custom-call(bf16[320,128]{1,0:T(8,128)(2,1)S(1)} %get-tuple-element.46.after_ref.refs_0_, bf16[2,2,8,512,128]{4,3,2,1,0:T(8,128)(2,1)} %cache_hbm.1), custom_call_target="tpu_custom_call" | custom-call | bytes 4194304 | tf_op jit(solution)/shard_map/stage/pallas_call | solution.py:39
  9.1 0.0 collective-permute-done.1
  9.1 0.3 collective-permute-start.2
  9.4 0.0 collective-permute-done.refs_1_
  9.4 1.0 %collective-permute-done.2.refs_3_ = bf16[320,128]{1,0:T(8,128)(2,1)S(1)} collective-permute-done((bf16[320,128]{1,0:T(8,128)(2,1)S(1)}, bf16[320,128]{1,0:T(8,128)(2,1)S(1)}, u32[]{:S(2)}, u32[]{:S(2)}) %collective-permute-start.2) | collective-permute-done | bytes 81952 | tf_op jit(solution)/shard_map/ppermute | solution.py:419
  10.4 4.8 %attend.1 = (bf16[16,2048]{1,0:T(8,128)(2,1)S(1)}, bf16[16,2048]{1,0:T(8,128)(2,1)S(1)}, bf16[16,2048]{1,0:T(8,128)(2,1)S(1)}, bf16[16,2048]{1,0:T(8,128)(2,1)S(...) custom-call(s32[2]{0:T(128)} %length_hbm.1, ...), custom_call_target="tpu_custom_call", output_to_operand_aliasing={{5}: (6, {})} | custom-call | tf_op jit(solution)/shard_map/attend/pallas_call | solution.py:39
  15.2 1.2 %collective-permute-start.4 = (bf16[16,2048]{1,0:T(8,128)(2,1)S(1)}, bf16[16,2048]{1,0:T(8,128)(2,1)S(1)}, u32[]{:S(2)}, u32[]{:S(2)}) collective-permute-start(bf16[16,2048]{1,0:T(8,128)(2,1)S(1)} %get-tuple-element.57), channel_id=1, source_target_pairs={{0,2},{1,3},{2,0},{3,1},{4,6},{5,7},{6,4},{7,5},{8,10},{9,11},{10,... | collective-permute-start | bytes 196616 | tf_op jit(solution)/shard_map/ppermute | solution.py:419
  16.4 1.0 %collective-permute-start.6 = (bf16[16,2048]{1,0:T(8,128)(2,1)S(1)}, bf16[16,2048]{1,0:T(8,128)(2,1)S(1)}, u32[]{:S(2)}, u32[]{:S(2)}) collective-permute-start(bf16[16,2048]{1,0:T(8,128)(2,1)S(1)} %get-tuple-element.59), channel_id=1, source_target_pairs={{0,3},{1,2},{2,1},{3,0},{4,7},{5,6},{6,5},{7,4},{8,11},{9,10},{10,... | collective-permute-start | bytes 196616 | tf_op jit(solution)/shard_map/ppermute | solution.py:419
  17.4 1.6 %collective-permute-start.7 = (bf16[32,2048]{1,0:T(8,128)(2,1)S(1)}, bf16[32,2048]{1,0:T(8,128)(2,1)S(1)}, u32[]{:S(2)}, u32[]{:S(2)}) collective-permute-start(bf16[32,2048]{1,0:T(8,128)(2,1)S(1)} %get-tuple-element.63.refs_4_), channel_id=1, source_target_pairs={{0,4},{4,0},{8,12},{12,8},{1,5},{5,1},{9,13},{13,9},{2,6},{6,2},{1... | collective-permute-start | bytes 393224 | tf_op jit(solution)/shard_map/ppermute | solution.py:419
  19.0 0.4 %collective-permute-start.8 = (bf16[32,2048]{1,0:T(8,128)(2,1)S(1)}, bf16[32,2048]{1,0:T(8,128)(2,1)S(1)}, u32[]{:S(2)}, u32[]{:S(2)}) collective-permute-start(bf16[32,2048]{1,0:T(8,128)(2,1)S(1)} %collective-permute-done.3.refs_6_), channel_id=1, source_target_pairs={{0,4},{4,0},{8,12},{12,8},{1,5},{5,1},{9,13},{13,9},{2,6},{6,2},{1... | collective-permute-start | bytes 393224 | tf_op jit(solution)/shard_map/ppermute | solution.py:419
  19.5 2.2 %fetch.1.refs_5_ = bf16[1,2048,1024]{2,1,0:T(8,128)(2,1)S(1)} custom-call(bf16[16,2048]{1,0:T(8,128)(2,1)S(1)} %get-tuple-element.73.after_ref.refs_0_, bf16[2048,8192]{1,0:T(8,128)(2,1)} %refs_5_.3), custom_call_target="tpu_custom_call" | custom-call | bytes 4194304 | tf_op jit(solution)/shard_map/fetch/pallas_call | solution.py:39
  21.7 3.5 %project.4 = (f32[32,4096]{1,0:T(8,128)S(1)}, bf16[32,4096]{1,0:T(8,128)(2,1)S(1)}, bf16[2,2048,1024]{2,1,0:T(8,128)(2,1)S(1)}) custom-call(bf16[16,2048]{1,0:T(8,128)(2,1)S(1)} %get-tuple-element.73.after_ref.refs_0_, bf16[16,2048]{1,0:T(8,128)(2,1)S(1)} %collective-permute-done.4.refs_1_, bf16[16,2048]{1,0:T(8,128)(2,1)S(1)} %collective-permute-done.5.refs_2_, ...), custom_call_target="tpu_custom_call" | custom-call | flops 1073741824 | bytes 16777216 | tf_op jit(solution)/shard_map/project/pallas_call | solution.py:39
  25.2 0.4 %collective-permute-done.8.refs_7_ = bf16[32,2048]{1,0:T(8,128)(2,1)S(1)} collective-permute-done((bf16[32,2048]{1,0:T(8,128)(2,1)S(1)}, bf16[32,2048]{1,0:T(8,128)(2,1)S(1)}, u32[]{:S(2)}, u32[]{:S(2)}) %collective-permute-start.8) | collective-permute-done | bytes 131104 | tf_op jit(solution)/shard_map/ppermute | solution.py:419
  25.7 0.4 handoff.1
  26.0 0.0 collective-permute-start.9
  26.1 2.2 %project.5 = (f32[32,1024]{1,0:T(8,128)S(1)}, bf16[32,1024]{1,0:T(8,128)(2,1)S(1)}, bf16[1,2048,1024]{2,1,0:T(8,128)(2,1)S(1)}) custom-call(bf16[16,2048]{1,0:T(8,128)(2,1)S(1)} %get-tuple-element.73.after_ref.refs_0_, bf16[16,2048]{1,0:T(8,128)(2,1)S(1)} %collective-permute-done.4.refs_1_, bf16[16,2048]{1,0:T(8,128)(2,1)S(1)} %collective-permute-done.5.refs_2_, ...), custom_call_target="tpu_custom_call" | custom-call | flops 268435456 | bytes 4194304 | tf_op jit(solution)/shard_map/project/pallas_call | solution.py:39
  28.3 0.1 join.1
  28.4 1.2 %collective-permute-start.10 = (bf16[16,4352]{1,0:T(8,128)(2,1)S(1)}, bf16[16,4352]{1,0:T(8,128)(2,1)S(1)}, u32[]{:S(2)}, u32[]{:S(2)}) collective-permute-start(bf16[16,4352]{1,0:T(8,128)(2,1)S(1)} %get-tuple-element.70), channel_id=1, source_target_pairs={{0,2},{1,3},{2,0},{3,1},{4,6},{5,7},{6,4},{7,5},{8,10},{9,11},{10,... | collective-permute-start | bytes 417800 | tf_op jit(solution)/shard_map/ppermute | solution.py:419
  29.6 2.2 %project.6 = (f32[32,2048]{1,0:T(8,128)S(1)}, bf16[32,2048]{1,0:T(8,128)(2,1)S(1)}, bf16[1,2048,1024]{2,1,0:T(8,128)(2,1)S(1)}) custom-call(bf16[16,2048]{1,0:T(8,128)(2,1)S(1)} %get-tuple-element.73.after_ref.refs_0_, bf16[16,2048]{1,0:T(8,128)(2,1)S(1)} %collective-permute-done.4.refs_1_, bf16[16,2048]{1,0:T(8,128)(2,1)S(1)} %collective-permute-done.5.refs_2_, ...), custom_call_target="tpu_custom_call" | custom-call | flops 536870912 | bytes 8388608 | tf_op jit(solution)/shard_map/project/pallas_call | solution.py:39
  31.8 0.3 collective-permute-start.12
  32.1 0.3 collective-permute-start.11
  32.4 0.9 %project.7 = (f32[32,1024]{1,0:T(8,128)S(1)}, bf16[32,1024]{1,0:T(8,128)(2,1)S(1)}) custom-call(bf16[16,2048]{1,0:T(8,128)(2,1)S(1)} %get-tuple-element.73.after_ref.refs_0_, bf16[16,2048]{1,0:T(8,128)(2,1)S(1)} %collective-permute-done.4.refs_1_, bf16[16,2048]{1,0:T(8,128)(2,1)S(1)} %collective-permute-done.5.refs_2_, ...), custom_call_target="tpu_custom_call" | custom-call | flops 268435456 | bytes 4194304 | tf_op jit(solution)/shard_map/project/pallas_call | solution.py:39
  33.3 0.3 collective-permute-start.13
  33.6 1.0 %collective-permute-done.10 = bf16[16,4352]{1,0:T(8,128)(2,1)S(1)} collective-permute-done((bf16[16,4352]{1,0:T(8,128)(2,1)S(1)}, bf16[16,4352]{1,0:T(8,128)(2,1)S(1)}, u32[]{:S(2)}, u32[]{:S(2)}) %collective-permute-start.10) | collective-permute-done | bytes 139296 | tf_op jit(solution)/shard_map/ppermute | solution.py:419
  34.6 0.0 collective-permute-done.13.refs_7_
  34.6 0.4 adapt.1
  35.0 1.2 %collective-permute-start.14 = (bf16[16,4096]{1,0:T(8,128)(2,1)S(1)}, bf16[16,4096]{1,0:T(8,128)(2,1)S(1)}, u32[]{:S(2)}, u32[]{:S(2)}) collective-permute-start(bf16[16,4096]{1,0:T(8,128)(2,1)S(1)} %get-tuple-element.85), channel_id=1, source_target_pairs={{0,2},{1,3},{2,0},{3,1},{4,6},{5,7},{6,4},{7,5},{8,10},{9,11},{10,... | collective-permute-start | bytes 393224 | tf_op jit(solution)/shard_map/ppermute | solution.py:419
  36.2 4.5 %collective-permute-done.14.far_got_ref = bf16[16,4096]{1,0:T(8,128)(2,1)S(1)} collective-permute-done((bf16[16,4096]{1,0:T(8,128)(2,1)S(1)}, bf16[16,4096]{1,0:T(8,128)(2,1)S(1)}, u32[]{:S(2)}, u32[]{:S(2)}) %collective-permute-start.14) | collective-permute-done | bytes 131104 | tf_op jit(solution)/shard_map/ppermute | solution.py:419
  40.7 0.8 %finish.1 = bf16[8,2,8192]{2,1,0:T(2,128)(2,1)} custom-call(f32[16,4096]{1,0:T(8,128)S(1)} %get-tuple-element.67.far_ref, bf16[16,4096]{1,0:T(8,128)(2,1)S(1)} %collective-permute-done.14.far_got_ref, f32[16,4096]{1,0:T(8,128)S(1)} %get-tuple-element.86.near_ref, bf16[16,4096]{1,0:T(8,128)(2,1)S(1)} %slice.17.near_got_ref), custom_call_target="tpu_custom_call" | custom-call | tf_op jit(solution)/shard_map/finish/pallas_call | solution.py:39
  (13 shorter events, 0.1 us)
Async XLA Ops:
  1.2 7.8 %collective-permute-start.1 = (bf16[2,320,128]{2,1,0:T(8,128)(2,1)S(1)}, bf16[2,320,128]{2,1,0:T(8,128)(2,1)S(1)}, u32[]{:S(2)}, u32[]{:S(2)}) collective-permute-start(bf16[2,320,128]{2,1,0:T(8,128)(2,1)S(1)} %get-tuple-element.48), channel_id=1, source_target_pairs={{0,2},{1,3},{2,0},{3,1},{4,6},{5,7},{6,4},{7,5},{8,10},{9,11},{10,... | collective-permute-start | bytes 491528 | tf_op jit(solution)/shard_map/ppermute | solution.py:419
  4.3 5.1 %collective-permute-start = (bf16[320,128]{1,0:T(8,128)(2,1)S(1)}, bf16[320,128]{1,0:T(8,128)(2,1)S(1)}, u32[]{:S(2)}, u32[]{:S(2)}) collective-permute-start(bf16[320,128]{1,0:T(8,128)(2,1)S(1)} %get-tuple-element.47), channel_id=1, source_target_pairs={{0,1},{1,0},{2,3},{3,2},{4,5},{5,4},{6,7},{7,6},{8,9},{9,8},{10,11... | collective-permute-start | bytes 245768 | tf_op jit(solution)/shard_map/ppermute | solution.py:419
  4.3 11.0 %collective-permute-start.3 = (bf16[32,2048]{1,0:T(8,128)(2,1)S(1)}, bf16[32,2048]{1,0:T(8,128)(2,1)S(1)}, u32[]{:S(2)}, u32[]{:S(2)}) collective-permute-start(bf16[32,2048]{1,0:T(8,128)(2,1)S(1)} %get-tuple-element.63.refs_4_), channel_id=1, source_target_pairs={{0,8},{4,12},{8,0},{12,4},{1,9},{5,13},{9,1},{13,5},{2,10},{6,14},... | collective-permute-start | bytes 393224 | tf_op jit(solution)/shard_map/ppermute | solution.py:419
  9.1 1.3 %collective-permute-start.2 = (bf16[320,128]{1,0:T(8,128)(2,1)S(1)}, bf16[320,128]{1,0:T(8,128)(2,1)S(1)}, u32[]{:S(2)}, u32[]{:S(2)}) collective-permute-start(bf16[320,128]{1,0:T(8,128)(2,1)S(1)} %get-tuple-element.87), channel_id=1, source_target_pairs={{0,1},{1,0},{2,3},{3,2},{4,5},{5,4},{6,7},{7,6},{8,9},{9,8},{10,11... | collective-permute-start | bytes 245768 | tf_op jit(solution)/shard_map/ppermute | solution.py:419
  15.2 6.4 %collective-permute-start.4 = (bf16[16,2048]{1,0:T(8,128)(2,1)S(1)}, bf16[16,2048]{1,0:T(8,128)(2,1)S(1)}, u32[]{:S(2)}, u32[]{:S(2)}) collective-permute-start(bf16[16,2048]{1,0:T(8,128)(2,1)S(1)} %get-tuple-element.57), channel_id=1, source_target_pairs={{0,2},{1,3},{2,0},{3,1},{4,6},{5,7},{6,4},{7,5},{8,10},{9,11},{10,... | collective-permute-start | bytes 196616 | tf_op jit(solution)/shard_map/ppermute | solution.py:419
  16.4 5.3 %collective-permute-start.5 = (bf16[16,2048]{1,0:T(8,128)(2,1)S(1)}, bf16[16,2048]{1,0:T(8,128)(2,1)S(1)}, u32[]{:S(2)}, u32[]{:S(2)}) collective-permute-start(bf16[16,2048]{1,0:T(8,128)(2,1)S(1)} %get-tuple-element.58), channel_id=1, source_target_pairs={{0,1},{1,0},{2,3},{3,2},{4,5},{5,4},{6,7},{7,6},{8,9},{9,8},{10,11... | collective-permute-start | bytes 196616 | tf_op jit(solution)/shard_map/ppermute | solution.py:419
  16.4 5.3 %collective-permute-start.6 = (bf16[16,2048]{1,0:T(8,128)(2,1)S(1)}, bf16[16,2048]{1,0:T(8,128)(2,1)S(1)}, u32[]{:S(2)}, u32[]{:S(2)}) collective-permute-start(bf16[16,2048]{1,0:T(8,128)(2,1)S(1)} %get-tuple-element.59), channel_id=1, source_target_pairs={{0,3},{1,2},{2,1},{3,0},{4,7},{5,6},{6,5},{7,4},{8,11},{9,10},{10,... | collective-permute-start | bytes 196616 | tf_op jit(solution)/shard_map/ppermute | solution.py:419
  17.4 7.8 %collective-permute-start.7 = (bf16[32,2048]{1,0:T(8,128)(2,1)S(1)}, bf16[32,2048]{1,0:T(8,128)(2,1)S(1)}, u32[]{:S(2)}, u32[]{:S(2)}) collective-permute-start(bf16[32,2048]{1,0:T(8,128)(2,1)S(1)} %get-tuple-element.63.refs_4_), channel_id=1, source_target_pairs={{0,4},{4,0},{8,12},{12,8},{1,5},{5,1},{9,13},{13,9},{2,6},{6,2},{1... | collective-permute-start | bytes 393224 | tf_op jit(solution)/shard_map/ppermute | solution.py:419
  19.0 6.6 %collective-permute-start.8 = (bf16[32,2048]{1,0:T(8,128)(2,1)S(1)}, bf16[32,2048]{1,0:T(8,128)(2,1)S(1)}, u32[]{:S(2)}, u32[]{:S(2)}) collective-permute-start(bf16[32,2048]{1,0:T(8,128)(2,1)S(1)} %collective-permute-done.3.refs_6_), channel_id=1, source_target_pairs={{0,4},{4,0},{8,12},{12,8},{1,5},{5,1},{9,13},{13,9},{2,6},{6,2},{1... | collective-permute-start | bytes 393224 | tf_op jit(solution)/shard_map/ppermute | solution.py:419
  26.0 2.3 %collective-permute-start.9 = (bf16[32,8320]{1,0:T(8,128)(2,1)S(1)}, bf16[32,8320]{1,0:T(8,128)(2,1)S(1)}, u32[]{:S(2)}, u32[]{:S(2)}) collective-permute-start(bf16[32,8320]{1,0:T(8,128)(2,1)S(1)} %get-tuple-element.66), channel_id=1, source_target_pairs={{0,1},{1,0},{2,3},{3,2},{4,5},{5,4},{6,7},{7,6},{8,9},{9,8},{10,11... | collective-permute-start | bytes 1597448 | tf_op jit(solution)/shard_map/ppermute | solution.py:419
  28.4 6.1 %collective-permute-start.10 = (bf16[16,4352]{1,0:T(8,128)(2,1)S(1)}, bf16[16,4352]{1,0:T(8,128)(2,1)S(1)}, u32[]{:S(2)}, u32[]{:S(2)}) collective-permute-start(bf16[16,4352]{1,0:T(8,128)(2,1)S(1)} %get-tuple-element.70), channel_id=1, source_target_pairs={{0,2},{1,3},{2,0},{3,1},{4,6},{5,7},{6,4},{7,5},{8,10},{9,11},{10,... | collective-permute-start | bytes 417800 | tf_op jit(solution)/shard_map/ppermute | solution.py:419
  31.8 2.8 %collective-permute-start.12 = (bf16[32,2048]{1,0:T(8,128)(2,1)S(1)}, bf16[32,2048]{1,0:T(8,128)(2,1)S(1)}, u32[]{:S(2)}, u32[]{:S(2)}) collective-permute-start(bf16[32,2048]{1,0:T(8,128)(2,1)S(1)} %get-tuple-element.82), channel_id=1, source_target_pairs={{0,1},{1,0},{2,3},{3,2},{4,5},{5,4},{6,7},{7,6},{8,9},{9,8},{10,11... | collective-permute-start | bytes 393224 | tf_op jit(solution)/shard_map/ppermute | solution.py:419
  32.1 2.5 %collective-permute-start.11 = (bf16[32,1024]{1,0:T(8,128)(2,1)S(1)}, bf16[32,1024]{1,0:T(8,128)(2,1)S(1)}, u32[]{:S(2)}, u32[]{:S(2)}) collective-permute-start(bf16[32,1024]{1,0:T(8,128)(2,1)S(1)} %get-tuple-element.81), channel_id=1, source_target_pairs={{0,1},{1,0},{2,3},{3,2},{4,5},{5,4},{6,7},{7,6},{8,9},{9,8},{10,11... | collective-permute-start | bytes 196616 | tf_op jit(solution)/shard_map/ppermute | solution.py:419
  33.3 1.3 %collective-permute-start.13 = (bf16[32,1024]{1,0:T(8,128)(2,1)S(1)}, bf16[32,1024]{1,0:T(8,128)(2,1)S(1)}, u32[]{:S(2)}, u32[]{:S(2)}) collective-permute-start(bf16[32,1024]{1,0:T(8,128)(2,1)S(1)} %get-tuple-element.83), channel_id=1, source_target_pairs={{0,1},{1,0},{2,3},{3,2},{4,5},{5,4},{6,7},{7,6},{8,9},{9,8},{10,11... | collective-permute-start | bytes 196616 | tf_op jit(solution)/shard_map/ppermute | solution.py:419
  35.0 5.7 %collective-permute-start.14 = (bf16[16,4096]{1,0:T(8,128)(2,1)S(1)}, bf16[16,4096]{1,0:T(8,128)(2,1)S(1)}, u32[]{:S(2)}, u32[]{:S(2)}) collective-permute-start(bf16[16,4096]{1,0:T(8,128)(2,1)S(1)} %get-tuple-element.85), channel_id=1, source_target_pairs={{0,2},{1,3},{2,0},{3,1},{4,6},{5,7},{6,4},{7,5},{8,10},{9,11},{10,... | collective-permute-start | bytes 393224 | tf_op jit(solution)/shard_map/ppermute | solution.py:419

commit v7 on v6

--- a/solution.py
+++ b/solution.py
@@ -454,8 +454,8 @@
         bit //= 2
 
     half, quarter = spread // 2, spread // 4
-    early = half + quarter
-    fetched = quarter
+    early = half
+    fetched = half
     attended = call(
         functools.partial(attend_kernel, parts=parts, own=own, steps=steps),
         "attend",

time: 41.7 us -> 41.4 us (level)
  waiting for transfers between devices: 7.02 us -> 6.6 us
    ppermute x15, waiting for transfers between devices: 7.02 us -> 6.6 us  [shards(): lax.ppermute(x, axis, [(i, i ^ k) for i in range(lax.axis_size(axis))])]
  transfers between devices with their start and end apart: 15 -> 15, of which waited for: 4 -> 3; matrix products, arithmetic and copies ran while one was open for 0% -> 0% of each run, Pallas kernels for 43% -> 44%
where the time goes in v7:
time: 41.4 us; the launch traced here: 41.2 us
  Pallas kernels  21 us (51%)
  starting transfers between devices  13.4 us (32%)
  waiting for transfers between devices  6.6 us (16%)
    pallas_call x12, Pallas kernels, call(): pl.pallas_call(kernel, in_specs=list(specs), out_specs=[VMEM] * len(outs)...  21 us
    ppermute x15, starting transfers between devices, shards(): lax.ppermute(x, axis, [(i, i ^ k) for i in range(lax.axis_size(axis))])  13.4 us
    ppermute x15, waiting for transfers between devices, shards(): lax.ppermute(x, axis, [(i, i ^ k) for i in range(lax.axis_size(axis))])  6.6 us
  transfers between devices with their start and end apart: 15, of which 3 were waited for; matrix products, arithmetic and copies ran while one was open for 0% of the time, Pallas kernels for 44%

profile of v7, /device:TPU:0, one launch (start us, length us, event | category | flops | bytes accessed | tf_op | source)
XLA Modules:
  0.0 41.2 jit_solution(12958848176780586223)
XLA Ops:
  0.0 1.2 %pack.1 = (bf16[320,128]{1,0:T(8,128)(2,1)S(1)}, bf16[320,128]{1,0:T(8,128)(2,1)S(1)}, bf16[2,320,128]{2,1,0:T(8,128)(2,1)S(1)}, bf16[32,2048]{1,0:T(8,128)(2,1)S(1)}) custom-call(bf16[8,8,2048]{2,1,0:T(8,128)(2,1)} %query_hbm.1, bf16[8,8,512]{2,1,0:T(8,128)(2,1)} %new_hbm.1, bf16[16,2048]{1,0:T(8,128)(2,1)} %bitcast.5, bf16[64,512]{1,0:T(8,128)(2,1)} %up_hbm.1), custom_call_target="tpu_custom_call" | custom-call | tf_op jit(solution)/shard_map/pack/pallas_call | solution.py:39
  1.2 3.0 %collective-permute-start.1 = (bf16[2,320,128]{2,1,0:T(8,128)(2,1)S(1)}, bf16[2,320,128]{2,1,0:T(8,128)(2,1)S(1)}, u32[]{:S(2)}, u32[]{:S(2)}) collective-permute-start(bf16[2,320,128]{2,1,0:T(8,128)(2,1)S(1)} %get-tuple-element.48), channel_id=1, source_target_pairs={{0,2},{1,3},{2,0},{3,1},{4,6},{5,7},{6,4},{7,5},{8,10},{9,11},{10,... | collective-permute-start | bytes 491528 | tf_op jit(solution)/shard_map/ppermute | solution.py:419
  4.3 0.0 collective-permute-start
  4.3 2.6 %collective-permute-start.3 = (bf16[32,2048]{1,0:T(8,128)(2,1)S(1)}, bf16[32,2048]{1,0:T(8,128)(2,1)S(1)}, u32[]{:S(2)}, u32[]{:S(2)}) collective-permute-start(bf16[32,2048]{1,0:T(8,128)(2,1)S(1)} %get-tuple-element.63.refs_4_), channel_id=1, source_target_pairs={{0,8},{4,12},{8,0},{12,4},{1,9},{5,13},{9,1},{13,5},{2,10},{6,14},... | collective-permute-start | bytes 393224 | tf_op jit(solution)/shard_map/ppermute | solution.py:419
  6.9 2.2 %stage.1.refs_5_ = bf16[2,2,8,528,128]{4,3,2,1,0:T(8,128)(2,1)S(1)} custom-call(bf16[320,128]{1,0:T(8,128)(2,1)S(1)} %get-tuple-element.46.after_ref.refs_0_, bf16[2,2,8,512,128]{4,3,2,1,0:T(8,128)(2,1)} %cache_hbm.1), custom_call_target="tpu_custom_call" | custom-call | bytes 4194304 | tf_op jit(solution)/shard_map/stage/pallas_call | solution.py:39
  9.1 0.0 collective-permute-done.1
  9.1 0.3 collective-permute-start.2
  9.4 1.0 %collective-permute-done.2.refs_3_ = bf16[320,128]{1,0:T(8,128)(2,1)S(1)} collective-permute-done((bf16[320,128]{1,0:T(8,128)(2,1)S(1)}, bf16[320,128]{1,0:T(8,128)(2,1)S(1)}, u32[]{:S(2)}, u32[]{:S(2)}) %collective-permute-start.2) | collective-permute-done | bytes 81952 | tf_op jit(solution)/shard_map/ppermute | solution.py:419
  10.4 3.6 %attend.1 = (bf16[16,2048]{1,0:T(8,128)(2,1)S(1)}, bf16[16,2048]{1,0:T(8,128)(2,1)S(1)}, bf16[16,2048]{1,0:T(8,128)(2,1)S(1)}, bf16[16,2048]{1,0:T(8,128)(2,1)S(...) custom-call(s32[2]{0:T(128)} %length_hbm.1, ...), custom_call_target="tpu_custom_call", output_to_operand_aliasing={{5}: (6, {})} | custom-call | tf_op jit(solution)/shard_map/attend/pallas_call | solution.py:39
  14.1 1.2 %collective-permute-start.4 = (bf16[16,2048]{1,0:T(8,128)(2,1)S(1)}, bf16[16,2048]{1,0:T(8,128)(2,1)S(1)}, u32[]{:S(2)}, u32[]{:S(2)}) collective-permute-start(bf16[16,2048]{1,0:T(8,128)(2,1)S(1)} %get-tuple-element.57), channel_id=1, source_target_pairs={{0,2},{1,3},{2,0},{3,1},{4,6},{5,7},{6,4},{7,5},{8,10},{9,11},{10,... | collective-permute-start | bytes 196616 | tf_op jit(solution)/shard_map/ppermute | solution.py:419
  15.3 0.0 collective-permute-start.5
  15.3 1.0 %collective-permute-start.6 = (bf16[16,2048]{1,0:T(8,128)(2,1)S(1)}, bf16[16,2048]{1,0:T(8,128)(2,1)S(1)}, u32[]{:S(2)}, u32[]{:S(2)}) collective-permute-start(bf16[16,2048]{1,0:T(8,128)(2,1)S(1)} %get-tuple-element.59), channel_id=1, source_target_pairs={{0,3},{1,2},{2,1},{3,0},{4,7},{5,6},{6,5},{7,4},{8,11},{9,10},{10,... | collective-permute-start | bytes 196616 | tf_op jit(solution)/shard_map/ppermute | solution.py:419
  16.3 1.6 %collective-permute-start.7 = (bf16[32,2048]{1,0:T(8,128)(2,1)S(1)}, bf16[32,2048]{1,0:T(8,128)(2,1)S(1)}, u32[]{:S(2)}, u32[]{:S(2)}) collective-permute-start(bf16[32,2048]{1,0:T(8,128)(2,1)S(1)} %get-tuple-element.63.refs_4_), channel_id=1, source_target_pairs={{0,4},{4,0},{8,12},{12,8},{1,5},{5,1},{9,13},{13,9},{2,6},{6,2},{1... | collective-permute-start | bytes 393224 | tf_op jit(solution)/shard_map/ppermute | solution.py:419
  17.9 0.4 %collective-permute-start.8 = (bf16[32,2048]{1,0:T(8,128)(2,1)S(1)}, bf16[32,2048]{1,0:T(8,128)(2,1)S(1)}, u32[]{:S(2)}, u32[]{:S(2)}) collective-permute-start(bf16[32,2048]{1,0:T(8,128)(2,1)S(1)} %collective-permute-done.3.refs_6_), channel_id=1, source_target_pairs={{0,4},{4,0},{8,12},{12,8},{1,5},{5,1},{9,13},{13,9},{2,6},{6,2},{1... | collective-permute-start | bytes 393224 | tf_op jit(solution)/shard_map/ppermute | solution.py:419
  18.3 3.5 %fetch.1.refs_5_ = bf16[2,2048,1024]{2,1,0:T(8,128)(2,1)S(1)} custom-call(bf16[16,2048]{1,0:T(8,128)(2,1)S(1)} %get-tuple-element.73.after_ref.refs_0_, bf16[2048,8192]{1,0:T(8,128)(2,1)} %refs_5_.3), custom_call_target="tpu_custom_call" | custom-call | bytes 8388608 | tf_op jit(solution)/shard_map/fetch/pallas_call | solution.py:39
  21.9 3.5 %project.4 = (f32[32,4096]{1,0:T(8,128)S(1)}, bf16[32,4096]{1,0:T(8,128)(2,1)S(1)}, bf16[2,2048,1024]{2,1,0:T(8,128)(2,1)S(1)}) custom-call(bf16[16,2048]{1,0:T(8,128)(2,1)S(1)} %get-tuple-element.73.after_ref.refs_0_, bf16[16,2048]{1,0:T(8,128)(2,1)S(1)} %collective-permute-done.4.refs_1_, bf16[16,2048]{1,0:T(8,128)(2,1)S(1)} %collective-permute-done.5.refs_2_, ...), custom_call_target="tpu_custom_call" | custom-call | flops 1073741824 | bytes 16777216 | tf_op jit(solution)/shard_map/project/pallas_call | solution.py:39
  25.4 0.4 handoff.1
  25.8 0.0 collective-permute-start.9
  25.8 2.2 %project.5 = (f32[32,1024]{1,0:T(8,128)S(1)}, bf16[32,1024]{1,0:T(8,128)(2,1)S(1)}, bf16[1,2048,1024]{2,1,0:T(8,128)(2,1)S(1)}) custom-call(bf16[16,2048]{1,0:T(8,128)(2,1)S(1)} %get-tuple-element.73.after_ref.refs_0_, bf16[16,2048]{1,0:T(8,128)(2,1)S(1)} %collective-permute-done.4.refs_1_, bf16[16,2048]{1,0:T(8,128)(2,1)S(1)} %collective-permute-done.5.refs_2_, ...), custom_call_target="tpu_custom_call" | custom-call | flops 268435456 | bytes 4194304 | tf_op jit(solution)/shard_map/project/pallas_call | solution.py:39
  28.1 0.1 join.1
  28.2 1.2 %collective-permute-start.10 = (bf16[16,4352]{1,0:T(8,128)(2,1)S(1)}, bf16[16,4352]{1,0:T(8,128)(2,1)S(1)}, u32[]{:S(2)}, u32[]{:S(2)}) collective-permute-start(bf16[16,4352]{1,0:T(8,128)(2,1)S(1)} %get-tuple-element.70), channel_id=1, source_target_pairs={{0,2},{1,3},{2,0},{3,1},{4,6},{5,7},{6,4},{7,5},{8,10},{9,11},{10,... | collective-permute-start | bytes 417800 | tf_op jit(solution)/shard_map/ppermute | solution.py:419
  29.4 2.2 %project.6 = (f32[32,2048]{1,0:T(8,128)S(1)}, bf16[32,2048]{1,0:T(8,128)(2,1)S(1)}, bf16[1,2048,1024]{2,1,0:T(8,128)(2,1)S(1)}) custom-call(bf16[16,2048]{1,0:T(8,128)(2,1)S(1)} %get-tuple-element.73.after_ref.refs_0_, bf16[16,2048]{1,0:T(8,128)(2,1)S(1)} %collective-permute-done.4.refs_1_, bf16[16,2048]{1,0:T(8,128)(2,1)S(1)} %collective-permute-done.5.refs_2_, ...), custom_call_target="tpu_custom_call" | custom-call | flops 536870912 | bytes 8388608 | tf_op jit(solution)/shard_map/project/pallas_call | solution.py:39
  31.6 0.3 collective-permute-start.12
  31.9 0.3 collective-permute-start.11
  32.2 0.9 %project.7 = (f32[32,1024]{1,0:T(8,128)S(1)}, bf16[32,1024]{1,0:T(8,128)(2,1)S(1)}) custom-call(bf16[16,2048]{1,0:T(8,128)(2,1)S(1)} %get-tuple-element.73.after_ref.refs_0_, bf16[16,2048]{1,0:T(8,128)(2,1)S(1)} %collective-permute-done.4.refs_1_, bf16[16,2048]{1,0:T(8,128)(2,1)S(1)} %collective-permute-done.5.refs_2_, ...), custom_call_target="tpu_custom_call" | custom-call | flops 268435456 | bytes 4194304 | tf_op jit(solution)/shard_map/project/pallas_call | solution.py:39
  33.0 0.3 collective-permute-start.13
  33.3 1.0 %collective-permute-done.10 = bf16[16,4352]{1,0:T(8,128)(2,1)S(1)} collective-permute-done((bf16[16,4352]{1,0:T(8,128)(2,1)S(1)}, bf16[16,4352]{1,0:T(8,128)(2,1)S(1)}, u32[]{:S(2)}, u32[]{:S(2)}) %collective-permute-start.10) | collective-permute-done | bytes 139296 | tf_op jit(solution)/shard_map/ppermute | solution.py:419
  34.3 0.0 collective-permute-done.13.refs_7_
  34.4 0.4 adapt.1
  34.8 1.2 %collective-permute-start.14 = (bf16[16,4096]{1,0:T(8,128)(2,1)S(1)}, bf16[16,4096]{1,0:T(8,128)(2,1)S(1)}, u32[]{:S(2)}, u32[]{:S(2)}) collective-permute-start(bf16[16,4096]{1,0:T(8,128)(2,1)S(1)} %get-tuple-element.85), channel_id=1, source_target_pairs={{0,2},{1,3},{2,0},{3,1},{4,6},{5,7},{6,4},{7,5},{8,10},{9,11},{10,... | collective-permute-start | bytes 393224 | tf_op jit(solution)/shard_map/ppermute | solution.py:419
  35.9 4.5 %collective-permute-done.14.far_got_ref = bf16[16,4096]{1,0:T(8,128)(2,1)S(1)} collective-permute-done((bf16[16,4096]{1,0:T(8,128)(2,1)S(1)}, bf16[16,4096]{1,0:T(8,128)(2,1)S(1)}, u32[]{:S(2)}, u32[]{:S(2)}) %collective-permute-start.14) | collective-permute-done | bytes 131104 | tf_op jit(solution)/shard_map/ppermute | solution.py:419
  40.4 0.8 %finish.1 = bf16[8,2,8192]{2,1,0:T(2,128)(2,1)} custom-call(f32[16,4096]{1,0:T(8,128)S(1)} %get-tuple-element.67.far_ref, bf16[16,4096]{1,0:T(8,128)(2,1)S(1)} %collective-permute-done.14.far_got_ref, f32[16,4096]{1,0:T(8,128)S(1)} %get-tuple-element.86.near_ref, bf16[16,4096]{1,0:T(8,128)(2,1)S(1)} %slice.17.near_got_ref), custom_call_target="tpu_custom_call" | custom-call | tf_op jit(solution)/shard_map/finish/pallas_call | solution.py:39
  (13 shorter events, 0.1 us)
Async XLA Ops:
  1.2 7.8 %collective-permute-start.1 = (bf16[2,320,128]{2,1,0:T(8,128)(2,1)S(1)}, bf16[2,320,128]{2,1,0:T(8,128)(2,1)S(1)}, u32[]{:S(2)}, u32[]{:S(2)}) collective-permute-start(bf16[2,320,128]{2,1,0:T(8,128)(2,1)S(1)} %get-tuple-element.48), channel_id=1, source_target_pairs={{0,2},{1,3},{2,0},{3,1},{4,6},{5,7},{6,4},{7,5},{8,10},{9,11},{10,... | collective-permute-start | bytes 491528 | tf_op jit(solution)/shard_map/ppermute | solution.py:419
  4.3 5.1 %collective-permute-start = (bf16[320,128]{1,0:T(8,128)(2,1)S(1)}, bf16[320,128]{1,0:T(8,128)(2,1)S(1)}, u32[]{:S(2)}, u32[]{:S(2)}) collective-permute-start(bf16[320,128]{1,0:T(8,128)(2,1)S(1)} %get-tuple-element.47), channel_id=1, source_target_pairs={{0,1},{1,0},{2,3},{3,2},{4,5},{5,4},{6,7},{7,6},{8,9},{9,8},{10,11... | collective-permute-start | bytes 245768 | tf_op jit(solution)/shard_map/ppermute | solution.py:419
  4.3 9.8 %collective-permute-start.3 = (bf16[32,2048]{1,0:T(8,128)(2,1)S(1)}, bf16[32,2048]{1,0:T(8,128)(2,1)S(1)}, u32[]{:S(2)}, u32[]{:S(2)}) collective-permute-start(bf16[32,2048]{1,0:T(8,128)(2,1)S(1)} %get-tuple-element.63.refs_4_), channel_id=1, source_target_pairs={{0,8},{4,12},{8,0},{12,4},{1,9},{5,13},{9,1},{13,5},{2,10},{6,14},... | collective-permute-start | bytes 393224 | tf_op jit(solution)/shard_map/ppermute | solution.py:419
  9.1 1.3 %collective-permute-start.2 = (bf16[320,128]{1,0:T(8,128)(2,1)S(1)}, bf16[320,128]{1,0:T(8,128)(2,1)S(1)}, u32[]{:S(2)}, u32[]{:S(2)}) collective-permute-start(bf16[320,128]{1,0:T(8,128)(2,1)S(1)} %get-tuple-element.87), channel_id=1, source_target_pairs={{0,1},{1,0},{2,3},{3,2},{4,5},{5,4},{6,7},{7,6},{8,9},{9,8},{10,11... | collective-permute-start | bytes 245768 | tf_op jit(solution)/shard_map/ppermute | solution.py:419
  14.1 7.7 %collective-permute-start.4 = (bf16[16,2048]{1,0:T(8,128)(2,1)S(1)}, bf16[16,2048]{1,0:T(8,128)(2,1)S(1)}, u32[]{:S(2)}, u32[]{:S(2)}) collective-permute-start(bf16[16,2048]{1,0:T(8,128)(2,1)S(1)} %get-tuple-element.57), channel_id=1, source_target_pairs={{0,2},{1,3},{2,0},{3,1},{4,6},{5,7},{6,4},{7,5},{8,10},{9,11},{10,... | collective-permute-start | bytes 196616 | tf_op jit(solution)/shard_map/ppermute | solution.py:419
  15.3 6.6 %collective-permute-start.5 = (bf16[16,2048]{1,0:T(8,128)(2,1)S(1)}, bf16[16,2048]{1,0:T(8,128)(2,1)S(1)}, u32[]{:S(2)}, u32[]{:S(2)}) collective-permute-start(bf16[16,2048]{1,0:T(8,128)(2,1)S(1)} %get-tuple-element.58), channel_id=1, source_target_pairs={{0,1},{1,0},{2,3},{3,2},{4,5},{5,4},{6,7},{7,6},{8,9},{9,8},{10,11... | collective-permute-start | bytes 196616 | tf_op jit(solution)/shard_map/ppermute | solution.py:419
  15.3 6.6 %collective-permute-start.6 = (bf16[16,2048]{1,0:T(8,128)(2,1)S(1)}, bf16[16,2048]{1,0:T(8,128)(2,1)S(1)}, u32[]{:S(2)}, u32[]{:S(2)}) collective-permute-start(bf16[16,2048]{1,0:T(8,128)(2,1)S(1)} %get-tuple-element.59), channel_id=1, source_target_pairs={{0,3},{1,2},{2,1},{3,0},{4,7},{5,6},{6,5},{7,4},{8,11},{9,10},{10,... | collective-permute-start | bytes 196616 | tf_op jit(solution)/shard_map/ppermute | solution.py:419
  16.3 9.1 %collective-permute-start.7 = (bf16[32,2048]{1,0:T(8,128)(2,1)S(1)}, bf16[32,2048]{1,0:T(8,128)(2,1)S(1)}, u32[]{:S(2)}, u32[]{:S(2)}) collective-permute-start(bf16[32,2048]{1,0:T(8,128)(2,1)S(1)} %get-tuple-element.63.refs_4_), channel_id=1, source_target_pairs={{0,4},{4,0},{8,12},{12,8},{1,5},{5,1},{9,13},{13,9},{2,6},{6,2},{1... | collective-permute-start | bytes 393224 | tf_op jit(solution)/shard_map/ppermute | solution.py:419
  17.9 7.5 %collective-permute-start.8 = (bf16[32,2048]{1,0:T(8,128)(2,1)S(1)}, bf16[32,2048]{1,0:T(8,128)(2,1)S(1)}, u32[]{:S(2)}, u32[]{:S(2)}) collective-permute-start(bf16[32,2048]{1,0:T(8,128)(2,1)S(1)} %collective-permute-done.3.refs_6_), channel_id=1, source_target_pairs={{0,4},{4,0},{8,12},{12,8},{1,5},{5,1},{9,13},{13,9},{2,6},{6,2},{1... | collective-permute-start | bytes 393224 | tf_op jit(solution)/shard_map/ppermute | solution.py:419
  25.8 2.3 %collective-permute-start.9 = (bf16[32,8320]{1,0:T(8,128)(2,1)S(1)}, bf16[32,8320]{1,0:T(8,128)(2,1)S(1)}, u32[]{:S(2)}, u32[]{:S(2)}) collective-permute-start(bf16[32,8320]{1,0:T(8,128)(2,1)S(1)} %get-tuple-element.66), channel_id=1, source_target_pairs={{0,1},{1,0},{2,3},{3,2},{4,5},{5,4},{6,7},{7,6},{8,9},{9,8},{10,11... | collective-permute-start | bytes 1597448 | tf_op jit(solution)/shard_map/ppermute | solution.py:419
  28.2 6.1 %collective-permute-start.10 = (bf16[16,4352]{1,0:T(8,128)(2,1)S(1)}, bf16[16,4352]{1,0:T(8,128)(2,1)S(1)}, u32[]{:S(2)}, u32[]{:S(2)}) collective-permute-start(bf16[16,4352]{1,0:T(8,128)(2,1)S(1)} %get-tuple-element.70), channel_id=1, source_target_pairs={{0,2},{1,3},{2,0},{3,1},{4,6},{5,7},{6,4},{7,5},{8,10},{9,11},{10,... | collective-permute-start | bytes 417800 | tf_op jit(solution)/shard_map/ppermute | solution.py:419
  31.6 2.8 %collective-permute-start.12 = (bf16[32,2048]{1,0:T(8,128)(2,1)S(1)}, bf16[32,2048]{1,0:T(8,128)(2,1)S(1)}, u32[]{:S(2)}, u32[]{:S(2)}) collective-permute-start(bf16[32,2048]{1,0:T(8,128)(2,1)S(1)} %get-tuple-element.82), channel_id=1, source_target_pairs={{0,1},{1,0},{2,3},{3,2},{4,5},{5,4},{6,7},{7,6},{8,9},{9,8},{10,11... | collective-permute-start | bytes 393224 | tf_op jit(solution)/shard_map/ppermute | solution.py:419
  31.9 2.5 %collective-permute-start.11 = (bf16[32,1024]{1,0:T(8,128)(2,1)S(1)}, bf16[32,1024]{1,0:T(8,128)(2,1)S(1)}, u32[]{:S(2)}, u32[]{:S(2)}) collective-permute-start(bf16[32,1024]{1,0:T(8,128)(2,1)S(1)} %get-tuple-element.81), channel_id=1, source_target_pairs={{0,1},{1,0},{2,3},{3,2},{4,5},{5,4},{6,7},{7,6},{8,9},{9,8},{10,11... | collective-permute-start | bytes 196616 | tf_op jit(solution)/shard_map/ppermute | solution.py:419
  33.0 1.3 %collective-permute-start.13 = (bf16[32,1024]{1,0:T(8,128)(2,1)S(1)}, bf16[32,1024]{1,0:T(8,128)(2,1)S(1)}, u32[]{:S(2)}, u32[]{:S(2)}) collective-permute-start(bf16[32,1024]{1,0:T(8,128)(2,1)S(1)} %get-tuple-element.83), channel_id=1, source_target_pairs={{0,1},{1,0},{2,3},{3,2},{4,5},{5,4},{6,7},{7,6},{8,9},{9,8},{10,11... | collective-permute-start | bytes 196616 | tf_op jit(solution)/shard_map/ppermute | solution.py:419
  34.8 5.7 %collective-permute-start.14 = (bf16[16,4096]{1,0:T(8,128)(2,1)S(1)}, bf16[16,4096]{1,0:T(8,128)(2,1)S(1)}, u32[]{:S(2)}, u32[]{:S(2)}) collective-permute-start(bf16[16,4096]{1,0:T(8,128)(2,1)S(1)} %get-tuple-element.85), channel_id=1, source_target_pairs={{0,2},{1,3},{2,0},{3,1},{4,6},{5,7},{6,4},{7,5},{8,10},{9,11},{10,... | collective-permute-start | bytes 393224 | tf_op jit(solution)/shard_map/ppermute | solution.py:419

commit v8 on v7

--- a/solution.py
+++ b/solution.py
@@ -89,12 +89,13 @@
         copy.wait()
 
 
-def pack_kernel(query_hbm, new_hbm, down_hbm, up_hbm, *refs, parts, own, steps):
-    *block_refs, factor_ref, query_ref, new_ref, up_ref, sem = refs
+def pack_kernel(query_hbm, new_hbm, down_hbm, up_hbm, length_hbm, *refs, parts, own, steps):
+    *block_refs, factor_ref, limit_ref, query_ref, new_ref, up_ref, length_ref, sem = refs
     slot, depth = down_hbm.shape
     pairs = [
         (query_hbm, query_ref),
         (new_hbm, new_ref),
+        (length_hbm, length_ref),
         (up_hbm, up_ref),
         (down_hbm, factor_ref.at[pl.ds(0, slot)]),
     ]
@@ -110,8 +111,10 @@
     part_out = (i >> log2(steps * own)) ^ me
     source = step_out * (parts * own) + part_out * own + row_out
     select = jnp.where(source == j, 1.0, 0.0).astype(BF16)
-    for copy in copies[:3]:
+    for copy in copies[:4]:
         copy.wait()
+    for r in range(own):
+        limit_ref[r] = jnp.full(limit_ref.shape[1:], length_ref[r], jnp.int32)
     queries = dot(select, query_ref[...].reshape(count, query_ref.shape[2]))
     new = dot(select, new_ref[...].reshape(count, new_ref.shape[2]))
     heads = queries.shape[1] // HEAD_DIM
@@ -136,18 +139,16 @@
     tall = RANK // per
     for c in range(per):
         factor_ref[slot : slot + tall, c * cut : (c + 1) * cut] = up_ref[c * tall : (c + 1) * tall, :]
-    for copy in copies[3:]:
+    for copy in copies[4:]:
         copy.wait()
 
 
-def attend_kernel(length_hbm, *refs, parts, own, steps):
+def attend_kernel(limit_ref, *refs, parts, own, steps):
     block_refs, refs = refs[:parts], refs[parts:]
     weight_hbm, refs = refs[0], refs[2:]
     out_refs, refs = refs[:parts], refs[parts:]
-    strips_ref, cache_ref, length_ref, held_ref, attended_ref = refs[:5]
-    scores_ref, weights_ref, mask_ref, length_sem, sem = refs[5:]
-    length_copy = pltpu.make_async_copy(length_hbm, length_ref, length_sem)
-    length_copy.start()
+    strips_ref, cache_ref, held_ref, attended_ref = refs[:4]
+    scores_ref, weights_ref, mask_ref, sem = refs[4:]
     heads = HEADS // parts
     pieces = 2 * KV_HEADS // parts
     query_rows = own * heads * steps
@@ -181,10 +182,12 @@
 
     slot = lax.broadcasted_iota(jnp.int32, (count, slots + tall), 1)
     step = lax.broadcasted_iota(jnp.int32, (count, slots + tall), 0) & (steps - 1)
-    length_copy.wait()
     for r in range(own):
+        limit = jnp.concatenate([limit_ref[r]] * GROUP, axis=0)
+        limit = jnp.concatenate([limit] * (-(-(slots + tall) // HEAD_DIM)), axis=1)
+        limit = limit[:, : slots + tall]
         fresh = slot - slots - r * steps
-        valid = (slot < length_ref[r]) | ((fresh >= 0) & (fresh <= step))
+        valid = (slot < limit) | ((fresh >= 0) & (fresh <= step))
         mask_ref[r] = jnp.where(valid, 0.0, -1e30)
     ones = jnp.ones((slots + tall, HEAD_DIM), BF16)
 
@@ -422,17 +425,22 @@
 
     block = shape_of((own * heads * steps + pieces * tall, HEAD_DIM), BF16)
     per = depth // cut
-    *blocks, cross, factors = call(
+    *blocks, cross, factors, limits = call(
         functools.partial(pack_kernel, parts=parts, own=own, steps=steps),
         "pack",
-        [(HBM, a) for a in (queries, new, down.T, up)],
+        [(HBM, a) for a in (queries, new, down.T, up, lengths)],
         [block] * sets
-        + [shape_of((sets,) + block.shape, BF16), shape_of((slot + RANK // per, depth), BF16)],
+        + [
+            shape_of((sets,) + block.shape, BF16),
+            shape_of((slot + RANK // per, depth), BF16),
+            shape_of((own, steps, HEAD_DIM), jnp.int32),
+        ],
         [
             pltpu.VMEM(queries.shape, BF16),
             pltpu.VMEM(new.shape, BF16),
             pltpu.VMEM(up.shape, BF16),
-            pltpu.SemaphoreType.DMA((4,)),
+            pltpu.SMEM(lengths.shape, jnp.int32),
+            pltpu.SemaphoreType.DMA((5,)),
         ],
     )
     (cache,) = call(
@@ -459,17 +467,15 @@
     attended = call(
         functools.partial(attend_kernel, parts=parts, own=own, steps=steps),
         "attend",
-        [(HBM, lengths)] + [(VMEM, b) for b in blocks] + [(HBM, weight), (VMEM, cache)],
+        [(VMEM, limits)] + [(VMEM, b) for b in blocks] + [(HBM, weight), (VMEM, cache)],
         [shape_of((tall, width), BF16)] * parts
         + [pltpu.VMEM((early, depth, wide), BF16), pltpu.VMEM(cache.shape, BF16)],
         [
-            pltpu.SMEM(lengths.shape, jnp.int32),
             pltpu.VMEM((parts, own * heads * steps, HEAD_DIM), BF16),
             pltpu.VMEM((parts, heads, tall, HEAD_DIM), F32),
             pltpu.VMEM((own, GROUP * steps, cache.shape[3]), F32),
             pltpu.VMEM((own, 2 * GROUP * steps, cache.shape[3]), BF16),
             pltpu.VMEM((own, GROUP * steps, cache.shape[3]), F32),
-            pltpu.SemaphoreType.DMA(()),
             pltpu.SemaphoreType.DMA((early,)),
         ],
         alias={parts + 2: parts + 1},

time: 41.4 us -> 41.4 us (level)
  no operation moved by 1% of the time
where the time goes in v8:
time: 41.4 us; the launch traced here: 41.2 us
  Pallas kernels  21 us (51%)
  starting transfers between devices  13.4 us (32%)
  waiting for transfers between devices  6.6 us (16%)
    pallas_call x12, Pallas kernels, call(): pl.pallas_call(kernel, in_specs=list(specs), out_specs=[VMEM] * len(outs)...  21 us
    ppermute x15, starting transfers between devices, shards(): lax.ppermute(x, axis, [(i, i ^ k) for i in range(lax.axis_size(axis))])  13.4 us
    ppermute x15, waiting for transfers between devices, shards(): lax.ppermute(x, axis, [(i, i ^ k) for i in range(lax.axis_size(axis))])  6.6 us
  transfers between devices with their start and end apart: 15, of which 3 were waited for; matrix products, arithmetic and copies ran while one was open for 0% of the time, Pallas kernels for 44%

profile of v8, /device:TPU:0, one launch (start us, length us, event | category | flops | bytes accessed | tf_op | source)
XLA Modules:
  0.0 41.2 jit_solution(6707725739449257817)
XLA Ops:
  0.0 1.2 %pack.1 = (bf16[320,128]{1,0:T(8,128)(2,1)S(1)}, bf16[320,128]{1,0:T(8,128)(2,1)S(1)}, bf16[2,320,128]{2,1,0:T(8,128)(2,1)S(1)}, bf16[32,2048]{1,0:T(8,128)(2,1)S(1)}, s32[2,8,128]{2,1,0:T(8,128)S(1)}) custom-call(bf16[8,8,2048]{2,1,0:T(8,128)(2,1)} %query_hbm.1, bf16[8,8,512]{2,1,0:T(8,128)(2,1)} %new_hbm.1, bf16[16,2048]{1,0:T(8,128)(2,1)} %bitcast.5, ...), custom_call_target="tpu_custom_call" | custom-call | tf_op jit(solution)/shard_map/pack/pallas_call | solution.py:39
  1.2 3.0 %collective-permute-start.1 = (bf16[2,320,128]{2,1,0:T(8,128)(2,1)S(1)}, bf16[2,320,128]{2,1,0:T(8,128)(2,1)S(1)}, u32[]{:S(2)}, u32[]{:S(2)}) collective-permute-start(bf16[2,320,128]{2,1,0:T(8,128)(2,1)S(1)} %get-tuple-element.50), channel_id=1, source_target_pairs={{0,2},{1,3},{2,0},{3,1},{4,6},{5,7},{6,4},{7,5},{8,10},{9,11},{10,... | collective-permute-start | bytes 491528 | tf_op jit(solution)/shard_map/ppermute | solution.py:422
  4.3 0.0 collective-permute-start
  4.3 2.6 %collective-permute-start.3 = (bf16[32,2048]{1,0:T(8,128)(2,1)S(1)}, bf16[32,2048]{1,0:T(8,128)(2,1)S(1)}, u32[]{:S(2)}, u32[]{:S(2)}) collective-permute-start(bf16[32,2048]{1,0:T(8,128)(2,1)S(1)} %get-tuple-element.65.refs_4_), channel_id=1, source_target_pairs={{0,8},{4,12},{8,0},{12,4},{1,9},{5,13},{9,1},{13,5},{2,10},{6,14},... | collective-permute-start | bytes 393224 | tf_op jit(solution)/shard_map/ppermute | solution.py:422
  6.9 2.2 %stage.1.refs_5_ = bf16[2,2,8,528,128]{4,3,2,1,0:T(8,128)(2,1)S(1)} custom-call(bf16[320,128]{1,0:T(8,128)(2,1)S(1)} %get-tuple-element.48.after_ref.refs_0_, bf16[2,2,8,512,128]{4,3,2,1,0:T(8,128)(2,1)} %cache_hbm.1), custom_call_target="tpu_custom_call" | custom-call | bytes 4194304 | tf_op jit(solution)/shard_map/stage/pallas_call | solution.py:39
  9.1 0.3 collective-permute-start.2
  9.4 0.0 collective-permute-done.refs_1_
  9.4 1.0 %collective-permute-done.2.refs_3_ = bf16[320,128]{1,0:T(8,128)(2,1)S(1)} collective-permute-done((bf16[320,128]{1,0:T(8,128)(2,1)S(1)}, bf16[320,128]{1,0:T(8,128)(2,1)S(1)}, u32[]{:S(2)}, u32[]{:S(2)}) %collective-permute-start.2) | collective-permute-done | bytes 81952 | tf_op jit(solution)/shard_map/ppermute | solution.py:422
  10.5 3.6 %attend.1 = (bf16[16,2048]{1,0:T(8,128)(2,1)S(1)}, bf16[16,2048]{1,0:T(8,128)(2,1)S(1)}, bf16[16,2048]{1,0:T(8,128)(2,1)S(1)}, bf16[16,2048]{1,0:T(8,128)(2,1)S(...) custom-call(s32[2,8,128]{2,1,0:T(8,128)S(1)} %get-tuple-element.47.l, ...), custom_call_target="tpu_custom_call", output_to_operand_aliasing={{5}: (6, {})} | custom-call | tf_op jit(solution)/shard_map/attend/pallas_call | solution.py:39
  14.0 0.0 collective-permute-done.3.refs_6_
  14.0 1.2 %collective-permute-start.4 = (bf16[16,2048]{1,0:T(8,128)(2,1)S(1)}, bf16[16,2048]{1,0:T(8,128)(2,1)S(1)}, u32[]{:S(2)}, u32[]{:S(2)}) collective-permute-start(bf16[16,2048]{1,0:T(8,128)(2,1)S(1)} %get-tuple-element.59), channel_id=1, source_target_pairs={{0,2},{1,3},{2,0},{3,1},{4,6},{5,7},{6,4},{7,5},{8,10},{9,11},{10,... | collective-permute-start | bytes 196616 | tf_op jit(solution)/shard_map/ppermute | solution.py:422
  15.2 1.0 %collective-permute-start.6 = (bf16[16,2048]{1,0:T(8,128)(2,1)S(1)}, bf16[16,2048]{1,0:T(8,128)(2,1)S(1)}, u32[]{:S(2)}, u32[]{:S(2)}) collective-permute-start(bf16[16,2048]{1,0:T(8,128)(2,1)S(1)} %get-tuple-element.61), channel_id=1, source_target_pairs={{0,3},{1,2},{2,1},{3,0},{4,7},{5,6},{6,5},{7,4},{8,11},{9,10},{10,... | collective-permute-start | bytes 196616 | tf_op jit(solution)/shard_map/ppermute | solution.py:422
  16.2 1.6 %collective-permute-start.7 = (bf16[32,2048]{1,0:T(8,128)(2,1)S(1)}, bf16[32,2048]{1,0:T(8,128)(2,1)S(1)}, u32[]{:S(2)}, u32[]{:S(2)}) collective-permute-start(bf16[32,2048]{1,0:T(8,128)(2,1)S(1)} %get-tuple-element.65.refs_4_), channel_id=1, source_target_pairs={{0,4},{4,0},{8,12},{12,8},{1,5},{5,1},{9,13},{13,9},{2,6},{6,2},{1... | collective-permute-start | bytes 393224 | tf_op jit(solution)/shard_map/ppermute | solution.py:422
  17.8 0.4 %collective-permute-start.8 = (bf16[32,2048]{1,0:T(8,128)(2,1)S(1)}, bf16[32,2048]{1,0:T(8,128)(2,1)S(1)}, u32[]{:S(2)}, u32[]{:S(2)}) collective-permute-start(bf16[32,2048]{1,0:T(8,128)(2,1)S(1)} %collective-permute-done.3.refs_6_), channel_id=1, source_target_pairs={{0,4},{4,0},{8,12},{12,8},{1,5},{5,1},{9,13},{13,9},{2,6},{6,2},{1... | collective-permute-start | bytes 393224 | tf_op jit(solution)/shard_map/ppermute | solution.py:422
  18.3 3.5 %fetch.1.refs_5_ = bf16[2,2048,1024]{2,1,0:T(8,128)(2,1)S(1)} custom-call(bf16[16,2048]{1,0:T(8,128)(2,1)S(1)} %get-tuple-element.75.after_ref.refs_0_, bf16[2048,8192]{1,0:T(8,128)(2,1)} %refs_5_.3), custom_call_target="tpu_custom_call" | custom-call | bytes 8388608 | tf_op jit(solution)/shard_map/fetch/pallas_call | solution.py:39
  21.8 3.5 %project.4 = (f32[32,4096]{1,0:T(8,128)S(1)}, bf16[32,4096]{1,0:T(8,128)(2,1)S(1)}, bf16[2,2048,1024]{2,1,0:T(8,128)(2,1)S(1)}) custom-call(bf16[16,2048]{1,0:T(8,128)(2,1)S(1)} %get-tuple-element.75.after_ref.refs_0_, bf16[16,2048]{1,0:T(8,128)(2,1)S(1)} %collective-permute-done.4.refs_1_, bf16[16,2048]{1,0:T(8,128)(2,1)S(1)} %collective-permute-done.5.refs_2_, ...), custom_call_target="tpu_custom_call" | custom-call | flops 1073741824 | bytes 16777216 | tf_op jit(solution)/shard_map/project/pallas_call | solution.py:39
  25.3 0.4 handoff.1
  25.7 0.0 collective-permute-start.9
  25.8 2.2 %project.5 = (f32[32,1024]{1,0:T(8,128)S(1)}, bf16[32,1024]{1,0:T(8,128)(2,1)S(1)}, bf16[1,2048,1024]{2,1,0:T(8,128)(2,1)S(1)}) custom-call(bf16[16,2048]{1,0:T(8,128)(2,1)S(1)} %get-tuple-element.75.after_ref.refs_0_, bf16[16,2048]{1,0:T(8,128)(2,1)S(1)} %collective-permute-done.4.refs_1_, bf16[16,2048]{1,0:T(8,128)(2,1)S(1)} %collective-permute-done.5.refs_2_, ...), custom_call_target="tpu_custom_call" | custom-call | flops 268435456 | bytes 4194304 | tf_op jit(solution)/shard_map/project/pallas_call | solution.py:39
  28.0 0.1 join.1
  28.1 1.2 %collective-permute-start.10 = (bf16[16,4352]{1,0:T(8,128)(2,1)S(1)}, bf16[16,4352]{1,0:T(8,128)(2,1)S(1)}, u32[]{:S(2)}, u32[]{:S(2)}) collective-permute-start(bf16[16,4352]{1,0:T(8,128)(2,1)S(1)} %get-tuple-element.72), channel_id=1, source_target_pairs={{0,2},{1,3},{2,0},{3,1},{4,6},{5,7},{6,4},{7,5},{8,10},{9,11},{10,... | collective-permute-start | bytes 417800 | tf_op jit(solution)/shard_map/ppermute | solution.py:422
  29.3 2.2 %project.6 = (f32[32,2048]{1,0:T(8,128)S(1)}, bf16[32,2048]{1,0:T(8,128)(2,1)S(1)}, bf16[1,2048,1024]{2,1,0:T(8,128)(2,1)S(1)}) custom-call(bf16[16,2048]{1,0:T(8,128)(2,1)S(1)} %get-tuple-element.75.after_ref.refs_0_, bf16[16,2048]{1,0:T(8,128)(2,1)S(1)} %collective-permute-done.4.refs_1_, bf16[16,2048]{1,0:T(8,128)(2,1)S(1)} %collective-permute-done.5.refs_2_, ...), custom_call_target="tpu_custom_call" | custom-call | flops 536870912 | bytes 8388608 | tf_op jit(solution)/shard_map/project/pallas_call | solution.py:39
  31.5 0.3 collective-permute-start.12
  31.8 0.3 collective-permute-start.11
  32.1 0.9 %project.7 = (f32[32,1024]{1,0:T(8,128)S(1)}, bf16[32,1024]{1,0:T(8,128)(2,1)S(1)}) custom-call(bf16[16,2048]{1,0:T(8,128)(2,1)S(1)} %get-tuple-element.75.after_ref.refs_0_, bf16[16,2048]{1,0:T(8,128)(2,1)S(1)} %collective-permute-done.4.refs_1_, bf16[16,2048]{1,0:T(8,128)(2,1)S(1)} %collective-permute-done.5.refs_2_, ...), custom_call_target="tpu_custom_call" | custom-call | flops 268435456 | bytes 4194304 | tf_op jit(solution)/shard_map/project/pallas_call | solution.py:39
  33.0 0.3 collective-permute-start.13
  33.2 1.0 %collective-permute-done.10 = bf16[16,4352]{1,0:T(8,128)(2,1)S(1)} collective-permute-done((bf16[16,4352]{1,0:T(8,128)(2,1)S(1)}, bf16[16,4352]{1,0:T(8,128)(2,1)S(1)}, u32[]{:S(2)}, u32[]{:S(2)}) %collective-permute-start.10) | collective-permute-done | bytes 139296 | tf_op jit(solution)/shard_map/ppermute | solution.py:422
  34.3 0.0 collective-permute-done.13.refs_7_
  34.3 0.4 adapt.1
  34.7 1.2 %collective-permute-start.14 = (bf16[16,4096]{1,0:T(8,128)(2,1)S(1)}, bf16[16,4096]{1,0:T(8,128)(2,1)S(1)}, u32[]{:S(2)}, u32[]{:S(2)}) collective-permute-start(bf16[16,4096]{1,0:T(8,128)(2,1)S(1)} %get-tuple-element.87), channel_id=1, source_target_pairs={{0,2},{1,3},{2,0},{3,1},{4,6},{5,7},{6,4},{7,5},{8,10},{9,11},{10,... | collective-permute-start | bytes 393224 | tf_op jit(solution)/shard_map/ppermute | solution.py:422
  35.9 4.5 %collective-permute-done.14.far_got_ref = bf16[16,4096]{1,0:T(8,128)(2,1)S(1)} collective-permute-done((bf16[16,4096]{1,0:T(8,128)(2,1)S(1)}, bf16[16,4096]{1,0:T(8,128)(2,1)S(1)}, u32[]{:S(2)}, u32[]{:S(2)}) %collective-permute-start.14) | collective-permute-done | bytes 131104 | tf_op jit(solution)/shard_map/ppermute | solution.py:422
  40.4 0.8 %finish.1 = bf16[8,2,8192]{2,1,0:T(2,128)(2,1)} custom-call(f32[16,4096]{1,0:T(8,128)S(1)} %get-tuple-element.69.far_ref, bf16[16,4096]{1,0:T(8,128)(2,1)S(1)} %collective-permute-done.14.far_got_ref, f32[16,4096]{1,0:T(8,128)S(1)} %get-tuple-element.88.near_ref, bf16[16,4096]{1,0:T(8,128)(2,1)S(1)} %slice.17.near_got_ref), custom_call_target="tpu_custom_call" | custom-call | tf_op jit(solution)/shard_map/finish/pallas_call | solution.py:39
  (13 shorter events, 0.1 us)
Async XLA Ops:
  1.2 7.8 %collective-permute-start.1 = (bf16[2,320,128]{2,1,0:T(8,128)(2,1)S(1)}, bf16[2,320,128]{2,1,0:T(8,128)(2,1)S(1)}, u32[]{:S(2)}, u32[]{:S(2)}) collective-permute-start(bf16[2,320,128]{2,1,0:T(8,128)(2,1)S(1)} %get-tuple-element.50), channel_id=1, source_target_pairs={{0,2},{1,3},{2,0},{3,1},{4,6},{5,7},{6,4},{7,5},{8,10},{9,11},{10,... | collective-permute-start | bytes 491528 | tf_op jit(solution)/shard_map/ppermute | solution.py:422
  4.3 5.1 %collective-permute-start = (bf16[320,128]{1,0:T(8,128)(2,1)S(1)}, bf16[320,128]{1,0:T(8,128)(2,1)S(1)}, u32[]{:S(2)}, u32[]{:S(2)}) collective-permute-start(bf16[320,128]{1,0:T(8,128)(2,1)S(1)} %get-tuple-element.49), channel_id=1, source_target_pairs={{0,1},{1,0},{2,3},{3,2},{4,5},{5,4},{6,7},{7,6},{8,9},{9,8},{10,11... | collective-permute-start | bytes 245768 | tf_op jit(solution)/shard_map/ppermute | solution.py:422
  4.3 9.8 %collective-permute-start.3 = (bf16[32,2048]{1,0:T(8,128)(2,1)S(1)}, bf16[32,2048]{1,0:T(8,128)(2,1)S(1)}, u32[]{:S(2)}, u32[]{:S(2)}) collective-permute-start(bf16[32,2048]{1,0:T(8,128)(2,1)S(1)} %get-tuple-element.65.refs_4_), channel_id=1, source_target_pairs={{0,8},{4,12},{8,0},{12,4},{1,9},{5,13},{9,1},{13,5},{2,10},{6,14},... | collective-permute-start | bytes 393224 | tf_op jit(solution)/shard_map/ppermute | solution.py:422
  9.1 1.3 %collective-permute-start.2 = (bf16[320,128]{1,0:T(8,128)(2,1)S(1)}, bf16[320,128]{1,0:T(8,128)(2,1)S(1)}, u32[]{:S(2)}, u32[]{:S(2)}) collective-permute-start(bf16[320,128]{1,0:T(8,128)(2,1)S(1)} %get-tuple-element.89), channel_id=1, source_target_pairs={{0,1},{1,0},{2,3},{3,2},{4,5},{5,4},{6,7},{7,6},{8,9},{9,8},{10,11... | collective-permute-start | bytes 245768 | tf_op jit(solution)/shard_map/ppermute | solution.py:422
  14.0 7.7 %collective-permute-start.4 = (bf16[16,2048]{1,0:T(8,128)(2,1)S(1)}, bf16[16,2048]{1,0:T(8,128)(2,1)S(1)}, u32[]{:S(2)}, u32[]{:S(2)}) collective-permute-start(bf16[16,2048]{1,0:T(8,128)(2,1)S(1)} %get-tuple-element.59), channel_id=1, source_target_pairs={{0,2},{1,3},{2,0},{3,1},{4,6},{5,7},{6,4},{7,5},{8,10},{9,11},{10,... | collective-permute-start | bytes 196616 | tf_op jit(solution)/shard_map/ppermute | solution.py:422
  15.2 6.6 %collective-permute-start.5 = (bf16[16,2048]{1,0:T(8,128)(2,1)S(1)}, bf16[16,2048]{1,0:T(8,128)(2,1)S(1)}, u32[]{:S(2)}, u32[]{:S(2)}) collective-permute-start(bf16[16,2048]{1,0:T(8,128)(2,1)S(1)} %get-tuple-element.60), channel_id=1, source_target_pairs={{0,1},{1,0},{2,3},{3,2},{4,5},{5,4},{6,7},{7,6},{8,9},{9,8},{10,11... | collective-permute-start | bytes 196616 | tf_op jit(solution)/shard_map/ppermute | solution.py:422
  15.2 6.6 %collective-permute-start.6 = (bf16[16,2048]{1,0:T(8,128)(2,1)S(1)}, bf16[16,2048]{1,0:T(8,128)(2,1)S(1)}, u32[]{:S(2)}, u32[]{:S(2)}) collective-permute-start(bf16[16,2048]{1,0:T(8,128)(2,1)S(1)} %get-tuple-element.61), channel_id=1, source_target_pairs={{0,3},{1,2},{2,1},{3,0},{4,7},{5,6},{6,5},{7,4},{8,11},{9,10},{10,... | collective-permute-start | bytes 196616 | tf_op jit(solution)/shard_map/ppermute | solution.py:422
  16.2 9.1 %collective-permute-start.7 = (bf16[32,2048]{1,0:T(8,128)(2,1)S(1)}, bf16[32,2048]{1,0:T(8,128)(2,1)S(1)}, u32[]{:S(2)}, u32[]{:S(2)}) collective-permute-start(bf16[32,2048]{1,0:T(8,128)(2,1)S(1)} %get-tuple-element.65.refs_4_), channel_id=1, source_target_pairs={{0,4},{4,0},{8,12},{12,8},{1,5},{5,1},{9,13},{13,9},{2,6},{6,2},{1... | collective-permute-start | bytes 393224 | tf_op jit(solution)/shard_map/ppermute | solution.py:422
  17.8 7.5 %collective-permute-start.8 = (bf16[32,2048]{1,0:T(8,128)(2,1)S(1)}, bf16[32,2048]{1,0:T(8,128)(2,1)S(1)}, u32[]{:S(2)}, u32[]{:S(2)}) collective-permute-start(bf16[32,2048]{1,0:T(8,128)(2,1)S(1)} %collective-permute-done.3.refs_6_), channel_id=1, source_target_pairs={{0,4},{4,0},{8,12},{12,8},{1,5},{5,1},{9,13},{13,9},{2,6},{6,2},{1... | collective-permute-start | bytes 393224 | tf_op jit(solution)/shard_map/ppermute | solution.py:422
  25.7 2.3 %collective-permute-start.9 = (bf16[32,8320]{1,0:T(8,128)(2,1)S(1)}, bf16[32,8320]{1,0:T(8,128)(2,1)S(1)}, u32[]{:S(2)}, u32[]{:S(2)}) collective-permute-start(bf16[32,8320]{1,0:T(8,128)(2,1)S(1)} %get-tuple-element.68), channel_id=1, source_target_pairs={{0,1},{1,0},{2,3},{3,2},{4,5},{5,4},{6,7},{7,6},{8,9},{9,8},{10,11... | collective-permute-start | bytes 1597448 | tf_op jit(solution)/shard_map/ppermute | solution.py:422
  28.1 6.1 %collective-permute-start.10 = (bf16[16,4352]{1,0:T(8,128)(2,1)S(1)}, bf16[16,4352]{1,0:T(8,128)(2,1)S(1)}, u32[]{:S(2)}, u32[]{:S(2)}) collective-permute-start(bf16[16,4352]{1,0:T(8,128)(2,1)S(1)} %get-tuple-element.72), channel_id=1, source_target_pairs={{0,2},{1,3},{2,0},{3,1},{4,6},{5,7},{6,4},{7,5},{8,10},{9,11},{10,... | collective-permute-start | bytes 417800 | tf_op jit(solution)/shard_map/ppermute | solution.py:422
  31.5 2.8 %collective-permute-start.12 = (bf16[32,2048]{1,0:T(8,128)(2,1)S(1)}, bf16[32,2048]{1,0:T(8,128)(2,1)S(1)}, u32[]{:S(2)}, u32[]{:S(2)}) collective-permute-start(bf16[32,2048]{1,0:T(8,128)(2,1)S(1)} %get-tuple-element.84), channel_id=1, source_target_pairs={{0,1},{1,0},{2,3},{3,2},{4,5},{5,4},{6,7},{7,6},{8,9},{9,8},{10,11... | collective-permute-start | bytes 393224 | tf_op jit(solution)/shard_map/ppermute | solution.py:422
  31.8 2.5 %collective-permute-start.11 = (bf16[32,1024]{1,0:T(8,128)(2,1)S(1)}, bf16[32,1024]{1,0:T(8,128)(2,1)S(1)}, u32[]{:S(2)}, u32[]{:S(2)}) collective-permute-start(bf16[32,1024]{1,0:T(8,128)(2,1)S(1)} %get-tuple-element.83), channel_id=1, source_target_pairs={{0,1},{1,0},{2,3},{3,2},{4,5},{5,4},{6,7},{7,6},{8,9},{9,8},{10,11... | collective-permute-start | bytes 196616 | tf_op jit(solution)/shard_map/ppermute | solution.py:422
  33.0 1.3 %collective-permute-start.13 = (bf16[32,1024]{1,0:T(8,128)(2,1)S(1)}, bf16[32,1024]{1,0:T(8,128)(2,1)S(1)}, u32[]{:S(2)}, u32[]{:S(2)}) collective-permute-start(bf16[32,1024]{1,0:T(8,128)(2,1)S(1)} %get-tuple-element.85), channel_id=1, source_target_pairs={{0,1},{1,0},{2,3},{3,2},{4,5},{5,4},{6,7},{7,6},{8,9},{9,8},{10,11... | collective-permute-start | bytes 196616 | tf_op jit(solution)/shard_map/ppermute | solution.py:422
  34.7 5.7 %collective-permute-start.14 = (bf16[16,4096]{1,0:T(8,128)(2,1)S(1)}, bf16[16,4096]{1,0:T(8,128)(2,1)S(1)}, u32[]{:S(2)}, u32[]{:S(2)}) collective-permute-start(bf16[16,4096]{1,0:T(8,128)(2,1)S(1)} %get-tuple-element.87), channel_id=1, source_target_pairs={{0,2},{1,3},{2,0},{3,1},{4,6},{5,7},{6,4},{7,5},{8,10},{9,11},{10,... | collective-permute-start | bytes 393224 | tf_op jit(solution)/shard_map/ppermute | solution.py:422
